TPU v7x, 128 devices: a whole 4x4x4 slice. The times are simulated.
128 devices in a mesh: blk: 32 (over z, x, core), rep: 4 (over y).
Axes of the slice: x: 4, y: 4, z: 4, core: 2. Of those that a mesh axis runs over, the one named last changes fastest.
Arguments:
- density: bfloat16 [512, 9, 128, 128], P(('blk', 'rep')), may hold values from -0.48 to 0.48, as said below
- pattern: int32 [512, 9], P(('blk', 'rep')), may hold values from 0 to 1, as said below
- orbitals: int32 [512], replicated, may hold values from 96 to 128
Outputs:
- purified: bfloat16 [512, 9, 128, 128], P(('blk', 'rep'))
Inputs may be any that keep to these rules, and one draw needn't show every extreme that they name: `density`: the stored matrix is symmetric: the block at [c, s] is the transpose of the block at [(c + s - 4) mod 512, 8 - s]. The pattern is symmetric: pattern[c, s] = pattern[(c + s - 4) mod 512, 8 - s]; every diagonal block (s = 4) is 1.
All inputs are finite; a program needn't handle non-finite values.
Results may differ from a plain program's by a relative error of at most 0.0037.
Values may be sent and summed in bfloat16 or wider, within the bound.
No kernel may reach another device: no remote copies, remote signals or barrier semaphores. Data moves between devices by JAX's collectives and lax.ppermute only.
A program may use at most 64 MiB of HBM per device.

v0:
```python
import jax
import jax.numpy as jnp
from jax import lax
from jax.sharding import PartitionSpec as P


def passed_along(array, axis, by):
    count = lax.axis_size(axis)
    return lax.ppermute(array, axis, [(i, (i + by) % count) for i in range(count)])


def outer_terms(left, right, reach_len):
    own_cols, band_len, tile_size = (left.shape[0], left.shape[1], left.shape[2])
    columns = []
    for slot in range(band_len):
        slot_gap = slot - reach_len
        first_pair = max(0, -slot_gap)
        last_pair = min(band_len - 1, band_len - 1 - slot_gap)
        products = jnp.einsum(
            "kvab,kvcb->kvac",
            left[:, first_pair + slot_gap : last_pair + slot_gap + 1],
            right[:, first_pair : last_pair + 1],
            preferred_element_type=jnp.float32,
        )
        column = jnp.zeros((own_cols + 2 * reach_len, tile_size, tile_size), jnp.float32)
        for pair_slot in range(first_pair, last_pair + 1):
            column = column.at[pair_slot : pair_slot + own_cols].add(
                products[:, pair_slot - first_pair]
            )
        columns.append(column)
    return jnp.stack(columns, axis=1)


def per_device(density, pattern, orbitals):
    own_cols, band_len, tile_size = (density.shape[0], density.shape[1], density.shape[2])
    reach_len = (band_len - 1) // 2
    all_blocks = orbitals.shape[0]
    first_col = lax.axis_index(("blk", "rep")) * own_cols
    doubled = jnp.concatenate([orbitals, orbitals])
    start_at = (first_col - reach_len + all_blocks) % all_blocks
    near_counts = lax.dynamic_slice_in_dim(doubled, start_at, own_cols + 2 * reach_len)
    row_counts = jnp.stack(
        [near_counts[slot : slot + own_cols] for slot in range(band_len)], axis=1
    )
    col_counts = near_counts[reach_len : reach_len + own_cols]
    lane_ids = jnp.arange(tile_size, dtype=jnp.int32)
    visible = (
        (lane_ids[None, None, :, None] < row_counts[:, :, None, None])
        & (lane_ids[None, None, None, :] < col_counts[:, None, None, None])
        & (pattern[:, :, None, None] == 1)
    )
    masked = jnp.where(visible, density, jnp.zeros_like(density))
    in_pattern = (pattern == 1)[:, :, None, None]
    hop_count = -(-reach_len // own_cols)
    reaches = []
    for distance in range(-hop_count, hop_count + 1):
        low_end = max(0, -distance * own_cols - reach_len)
        high_end = min(own_cols, own_cols + reach_len - distance * own_cols)
        if distance != 0 and low_end < high_end:
            reaches.append((distance, low_end, high_end))

    def gathered_sum(left, right):
        term = outer_terms(left, right, reach_len)
        total = term[reach_len : reach_len + own_cols]
        for distance, low_end, high_end in reaches:
            begin = distance * own_cols + reach_len
            arrived = passed_along(
                term[begin + low_end : begin + high_end], ("blk", "rep"), distance
            )
            total = total.at[low_end:high_end].add(arrived)
        return total

    square = gathered_sum(masked, masked)
    squared = jnp.where(in_pattern, square, jnp.zeros_like(square)).astype(jnp.bfloat16)
    cube = gathered_sum(squared, masked)
    mixed = 3.0 * square - 2.0 * cube
    return jnp.where(in_pattern, mixed, jnp.zeros_like(mixed)).astype(jnp.bfloat16)


def solution(mesh):
    placed = (P(("blk", "rep"), None, None, None), P(("blk", "rep"), None), P())
    return jax.shard_map(
        per_device,
        mesh=mesh,
        in_specs=placed,
        out_specs=P(("blk", "rep"), None, None, None),
        check_vma=False,
    )
```

profile of v0, /device:TPU:1, one launch (start us, length us, event | category | flops | bytes accessed | tf_op | source)
XLA Modules:
  0.0 150.4 jit_solution(7495683640043400698)
XLA Ops:
  0.0 0.7 broadcast_compare_fusion
  0.7 0.8 pad_add_fusion
  2.7 2.6 %and_select_fusion = bf16[4,9,128,128]{3,2,1,0:T(8,128)(2,1)S(1)} fusion(bf16[4,9,128,128]{3,2,1,0:T(8,128)(2,1)} %param.263, pred[4,128]{1,0:T(4,128)(4,1)S(1)} %iota_compare_fusion.1, pred[4,9,128]{2,1,0:T(8,128)(4,1)S(1)} %iota_compare_fusion, pred[4,9]{1,0:T(4,128)(4,1)S(1)} %broadcast_compare_fusion), kind=kLoop, calls=%fused_computation.9 | loop fusion | flops 1769472 | bytes 2364452 | tf_op jit(solution)/shard_map/jit(_where)/select_n | solution.py:52
  5.5 0.6 fusion.52
  6.1 0.6 fusion.54
  7.0 0.7 fusion.44
  7.6 0.7 fusion.46
  8.7 0.8 fusion.32
  9.5 0.7 fusion.34
  10.2 0.6 fusion.291
  10.8 0.8 fusion.20
  11.7 0.8 fusion.22
  12.5 0.9 fusion.13
  18.7 0.6 fusion.286
  19.2 4.2 %collective-permute-start = (f32[4,9,128,128]{3,2,1,0:T(8,128)S(1)}, f32[4,9,128,128]{3,2,1,0:T(8,128)S(1)}, u32[]{:S(2)}, u32[]{:S(2)}) collective-permute-start(f32[4,9,128,128]{3,2,1,0:T(8,128)S(1)} %get-tuple-element.1551), channel_id=1, source_target_pairs={{0,127},{1,0},{2,1},{3,2},{4,3},{5,4},{6,5},{7,6},{8,7},{9,8},{10,... | collective-permute-start | bytes 7077896 | tf_op jit(solution)/shard_map/ppermute | solution.py:9
  23.4 51.1 %collective-permute-done = f32[4,9,128,128]{3,2,1,0:T(8,128)S(1)} collective-permute-done((f32[4,9,128,128]{3,2,1,0:T(8,128)S(1)}, f32[4,9,128,128]{3,2,1,0:T(8,128)S(1)}, u32[]{:S(2)}, u32[]{:S(2)}) %collective-permute-start) | collective-permute-done | bytes 2359328 | tf_op jit(solution)/shard_map/ppermute | solution.py:9
  74.5 3.7 %collective-permute-done.1 = f32[4,9,128,128]{3,2,1,0:T(8,128)S(1)} collective-permute-done((f32[4,9,128,128]{3,2,1,0:T(8,128)S(1)}, f32[4,9,128,128]{3,2,1,0:T(8,128)S(1)}, u32[]{:S(2)}, u32[]{:S(2)}) %collective-permute-start.1) | collective-permute-done | bytes 2359328 | tf_op jit(solution)/shard_map/ppermute | solution.py:9
  78.2 0.8 select_convert_fusion
  79.0 0.9 fusion.6
  81.8 0.6 fusion.39
  82.7 0.6 fusion.41
  83.7 0.7 fusion.27
  84.8 0.7 fusion.29
  86.0 0.8 fusion.15
  87.3 0.8 fusion.17
  88.6 0.9 fusion.8
  90.0 0.8 fusion.10
  92.1 0.6 fusion.285
  92.8 1.5 collective-permute-start.3
  94.2 49.1 %collective-permute-done.2 = f32[4,9,128,128]{3,2,1,0:T(8,128)S(1)} collective-permute-done((f32[4,9,128,128]{3,2,1,0:T(8,128)S(1)}, f32[4,9,128,128]{3,2,1,0:T(8,128)S(1)}, u32[]{:S(2)}, u32[]{:S(2)}) %collective-permute-start.2) | collective-permute-done | bytes 2359328 | tf_op jit(solution)/shard_map/ppermute | solution.py:9
  143.4 4.2 %collective-permute-done.3 = f32[4,9,128,128]{3,2,1,0:T(8,128)S(1)} collective-permute-done((f32[4,9,128,128]{3,2,1,0:T(8,128)S(1)}, f32[4,9,128,128]{3,2,1,0:T(8,128)S(1)}, u32[]{:S(2)}, u32[]{:S(2)}) %collective-permute-start.3) | collective-permute-done | bytes 2359328 | tf_op jit(solution)/shard_map/ppermute | solution.py:9
  147.6 2.8 %fusion.4 = bf16[4,9,128,128]{3,2,1,0:T(8,128)(2,1)} fusion(f32[4,9,128,128]{3,2,1,0:T(8,128)S(1)} %collective-permute-done.3, f32[4,9,128,128]{3,2,1,0:T(8,128)S(1)} %collective-permute-done.2, f32[12,9,128,128]{3,2,1,0:T(8,128)S(1)} %constant_dynamic-update-slice_fusion.9, pred[4,9]{1,0:T(4,128)(4,1)S(1)} %broadcast_compare_fusion, ...), kind=kLoop, calls=%fused_computation.5 | loop fusion | flops 5308416 | bytes 15335460 | tf_op jit(solution)/shard_map/convert_element_type | solution.py:77
  (199 shorter events, 12.7 us)
Async XLA Ops:
  19.2 55.3 %collective-permute-start = (f32[4,9,128,128]{3,2,1,0:T(8,128)S(1)}, f32[4,9,128,128]{3,2,1,0:T(8,128)S(1)}, u32[]{:S(2)}, u32[]{:S(2)}) collective-permute-start(f32[4,9,128,128]{3,2,1,0:T(8,128)S(1)} %get-tuple-element.1551), channel_id=1, source_target_pairs={{0,127},{1,0},{2,1},{3,2},{4,3},{5,4},{6,5},{7,6},{8,7},{9,8},{10,... | collective-permute-start | bytes 7077896 | tf_op jit(solution)/shard_map/ppermute | solution.py:9
  23.4 54.8 %collective-permute-start.1 = (f32[4,9,128,128]{3,2,1,0:T(8,128)S(1)}, f32[4,9,128,128]{3,2,1,0:T(8,128)S(1)}, u32[]{:S(2)}, u32[]{:S(2)}) collective-permute-start(f32[4,9,128,128]{3,2,1,0:T(8,128)S(1)} %get-tuple-element.1552), channel_id=1, source_target_pairs={{0,1},{1,2},{2,3},{3,4},{4,5},{5,6},{6,7},{7,8},{8,9},{9,10},{10,1... | collective-permute-start | bytes 7077896 | tf_op jit(solution)/shard_map/ppermute | solution.py:9
  92.7 50.7 %collective-permute-start.2 = (f32[4,9,128,128]{3,2,1,0:T(8,128)S(1)}, f32[4,9,128,128]{3,2,1,0:T(8,128)S(1)}, u32[]{:S(2)}, u32[]{:S(2)}) collective-permute-start(f32[4,9,128,128]{3,2,1,0:T(8,128)S(1)} %get-tuple-element.1549), channel_id=1, source_target_pairs={{0,127},{1,0},{2,1},{3,2},{4,3},{5,4},{6,5},{7,6},{8,7},{9,8},{10,... | collective-permute-start | bytes 7077896 | tf_op jit(solution)/shard_map/ppermute | solution.py:9
  92.8 54.8 %collective-permute-start.3 = (f32[4,9,128,128]{3,2,1,0:T(8,128)S(1)}, f32[4,9,128,128]{3,2,1,0:T(8,128)S(1)}, u32[]{:S(2)}, u32[]{:S(2)}) collective-permute-start(f32[4,9,128,128]{3,2,1,0:T(8,128)S(1)} %get-tuple-element.1550), channel_id=1, source_target_pairs={{0,1},{1,2},{2,3},{3,4},{4,5},{5,6},{6,7},{7,8},{8,9},{9,10},{10,1... | collective-permute-start | bytes 7077896 | tf_op jit(solution)/shard_map/ppermute | solution.py:9
where the time goes:
time: 151 us; the launch traced here: 150 us
  waiting for transfers between devices  108 us (72%)
  other arithmetic  13.7 us (9%)
  matrix products  13.2 us (9%)
  local copies, waits for them, and re-layouts  8.24 us (5%)
  starting transfers between devices  5.74 us (4%)
    ppermute x4, waiting for transfers between devices, passed_along(): lax.ppermute(array, axis, [(i, (i + by) % count) for i in range(count)])  108 us
    dot_general x18, matrix products, outer_terms(): jnp.einsum('kvab,kvcb->kvac', left[:, first_pair + slot_gap:last_pair + s...  13.2 us
    scatter-add x104, other arithmetic, outer_terms(): column.at[pair_slot:pair_slot + own_cols]  5.9 us
    ppermute x4, starting transfers between devices, passed_along(): lax.ppermute(array, axis, [(i, (i + by) % count) for i in range(count)])  5.74 us
  transfers between devices with their start and end apart: 4, of which 4 were waited for; matrix products, arithmetic and copies ran while one was open for 0% of the time, Pallas kernels for 0%

commit v1 on v0

v1 whole, which is shorter than its diff:
```python
import jax
import jax.numpy as jnp
from jax import lax
from jax.experimental import pallas as pl
from jax.experimental.pallas import tpu as pltpu
from jax.sharding import PartitionSpec as P

AXES = ("blk", "rep")
T = 128
COLS = 4
REACH = 4
BAND = 9
SIDE = COLS * T
BELOW = [(a, b) for b in range(COLS) for a in range(b + 1, COLS)]
PACKED = (len(BELOW) + COLS // 2) * T + 16
F32 = jnp.float32
BF16 = jnp.bfloat16
LIMIT = 40 * 1024 * 1024

VMEM = pl.BlockSpec(memory_space=pltpu.VMEM)
SMEM = pl.BlockSpec(memory_space=pltpu.SMEM)
ANY = pl.BlockSpec(memory_space=pl.ANY)


def rows_cols():
    return (
        lax.broadcasted_iota(jnp.int32, (T, T), 0),
        lax.broadcasted_iota(jnp.int32, (T, T), 1),
    )


def at(index):
    return slice(index * T, (index + 1) * T)


def half(index):
    return slice(2 * index * T, 2 * (index + 1) * T)


def span(first, last):
    return slice(2 * first * T, 2 * (last + 1) * T)


def dot(a, b):
    return lax.dot_general(a, b, (((1,), (0,)), ((), ())), preferred_element_type=F32)


def dot_tn(a, b):
    return lax.dot_general(a, b, (((0,), (0,)), ((), ())), preferred_element_type=F32)


def pack(out_ref, block):
    row, col = rows_cols()
    for index, (a, b) in enumerate(BELOW):
        out_ref[at(index), :] = block(a, b).astype(BF16)
    strip_row = lax.broadcasted_iota(jnp.int32, (16, T), 0)
    strip = jnp.zeros((16, T), F32)
    for pair in range(COLS // 2):
        first = block(2 * pair, 2 * pair).astype(F32)
        second = block(2 * pair + 1, 2 * pair + 1).astype(F32)
        out_ref[at(len(BELOW) + pair), :] = jnp.where(row >= col, first, second).astype(BF16)
        diagonal = jnp.sum(jnp.where(row == col, second, 0.0), axis=0, keepdims=True)
        strip = jnp.where(strip_row == pair, diagonal, strip)
    out_ref[PACKED - 16 : PACKED, :] = strip.astype(BF16)


def unpack(packed_ref, full_ref):
    row, col = rows_cols()
    for index, (a, b) in enumerate(BELOW):
        block = packed_ref[at(index), :]
        full_ref[at(a), at(b)] = block
        full_ref[at(b), at(a)] = block.T
    strip = packed_ref[PACKED - 16 : PACKED, :].astype(F32)
    for pair in range(COLS // 2):
        both = packed_ref[at(len(BELOW) + pair), :].astype(F32)
        turned = both.T
        first = jnp.where(row >= col, both, turned)
        second = jnp.where(row < col, both, turned)
        second = jnp.where(row == col, strip[pair : pair + 1, :], second)
        full_ref[at(2 * pair), at(2 * pair)] = first.astype(BF16)
        full_ref[at(2 * pair + 1), at(2 * pair + 1)] = second.astype(BF16)


def pack_own(density, pattern, orbitals, out, held, sems):
    first = lax.axis_index(AXES) * COLS
    copies = [
        pltpu.make_async_copy(
            density.at[b, pl.ds(REACH, COLS - b)], held.at[b, pl.ds(0, COLS - b)], sems.at[b]
        )
        for b in range(COLS)
    ]
    for copy in copies:
        copy.start()
    row, col = rows_cols()
    used = [orbitals[first + a] for a in range(COLS)]
    for copy in copies:
        copy.wait()

    def block(a, b):
        visible = (row < used[a] * pattern[b, a - b + REACH]) & (col < used[b])
        return jnp.where(visible, held[b, a - b].astype(F32), 0.0)

    pack(out, block)


def own_square(density, pattern, orbitals, wide, square, squared, packed):
    count = orbitals.shape[0]
    first = lax.axis_index(AXES) * COLS
    used = [orbitals[lax.rem(first + r - REACH + count, count)] for r in range(COLS + 2 * REACH)]
    row, col = rows_cols()
    zero = jnp.zeros((T, T), BF16)
    for c in range(COLS):
        for r in range(COLS + 2 * REACH):
            if c <= r < c + BAND:
                visible = (row < used[r] * pattern[c, r - c]) & (col < used[c + REACH])
                wide[at(r), at(c)] = jnp.where(visible, density[c, r - c].astype(F32), 0.0).astype(BF16)
            else:
                wide[at(r), at(c)] = zero
    left, own, right = (wide.at[k * SIDE : (k + 1) * SIDE] for k in range(3))
    for i, j in ((0, 0), (0, 1), (1, 0), (1, 1)):
        low = max(i, j)
        high = min(i, j)
        square[half(i), half(j)] = (
            dot(own[half(i), :], own[:, half(j)])
            + dot_tn(left[span(low, 1), half(i)], left[span(low, 1), half(j)])
            + dot_tn(right[span(0, high), half(i)], right[span(0, high), half(j)])
        )
    for b in range(COLS):
        for a in range(COLS):
            squared[at(a), at(b)] = jnp.where(pattern[b, a - b + REACH] == 1, square[at(a), at(b)], 0.0).astype(BF16)
    pack(packed, lambda a, b: squared[at(a), at(b)])


def side_blocks(side, tile):
    for a in (2 * tile[0], 2 * tile[0] + 1):
        for c in (2 * tile[1], 2 * tile[1] + 1):
            if side == 0 and a >= c:
                yield a, c, a - c, a - c
            if side == 1 and a <= c:
                yield a, c, a - c + 2 * REACH, COLS - c + a


TILES = (((0, 0), (1, 0), (1, 1)), ((0, 0), (0, 1), (1, 1)))


def full_by_side(side, tile, full, thin):
    i, j = tile
    inner = span(j, 1) if side == 0 else span(0, j)
    return dot(full[half(i), inner], thin[inner, half(j)])


def side_by_full(side, tile, thin, full):
    i, j = tile
    inner = span(0, i) if side == 0 else span(i, 1)
    return dot(thin[half(i), inner], full[inner, half(j)])


def middle(packed_left, packed_right, wide, square, squared, pattern, acc, out, full, cross, tile_ref, held, sems):
    own = wide.at[SIDE : 2 * SIDE]
    for side, packed in ((0, packed_left), (1, packed_right)):
        thin = wide.at[side * 2 * SIDE : (side * 2 + 1) * SIDE]
        crossed = cross.at[side]
        unpack(packed, full)
        crossed[...] = jnp.zeros((SIDE, SIDE), BF16)
        for tile in TILES[side]:
            tile_ref[...] = full_by_side(side, tile, full, thin) + side_by_full(side, tile, thin, own)
            for a, c, slot, place in side_blocks(side, tile):
                block = tile_ref[at(a % 2), at(c % 2)]
                crossed[at(a), at(c)] = jnp.where(pattern[c, slot] == 1, block, 0.0).astype(BF16)
                acc[c, place] = 3.0 * block
        for tile in TILES[side]:
            tile_ref[...] = side_by_full(side, tile, crossed, own)
            for a, c, slot, place in side_blocks(side, tile):
                acc[c, place] = acc[c, place] - 2.0 * tile_ref[at(a % 2), at(c % 2)]
    left, right = wide.at[:SIDE], wide.at[2 * SIDE :]
    for j in range(2):
        for i in range(2):
            low, high = span(max(i, j), 1), span(0, min(i, j))
            tile_ref[...] = (
                dot(squared[half(i), :], own[:, half(j)])
                + dot_tn(cross[0, low, half(i)], left[low, half(j)])
                + dot_tn(cross[1, high, half(i)], right[high, half(j)])
            )
            for a in (2 * i, 2 * i + 1):
                for c in (2 * j, 2 * j + 1):
                    mixed = 3.0 * square[at(a), at(c)] - 2.0 * tile_ref[at(a % 2), at(c % 2)]
                    held[c, a] = jnp.where(pattern[c, a - c + REACH] == 1, mixed, 0.0).astype(BF16)
    copies = [
        pltpu.make_async_copy(held.at[c], out.at[c, pl.ds(REACH - c, COLS)], sems.at[c]) for c in range(COLS)
    ]
    for copy in copies:
        copy.start()
    for copy in copies:
        copy.wait()


def finish(packed_left, packed_right, wide, acc, pattern, begun, out, full, tile_ref, held, sems):
    del begun
    copies = []
    for side, packed in ((0, packed_left), (1, packed_right)):
        thin = wide.at[side * 2 * SIDE : (side * 2 + 1) * SIDE]
        unpack(packed, full)
        for tile in TILES[side]:
            tile_ref[...] = full_by_side(side, tile, full, thin)
            for a, c, slot, place in side_blocks(side, tile):
                mixed = acc[c, place] - 2.0 * tile_ref[at(a % 2), at(c % 2)]
                held[c, place] = jnp.where(pattern[c, slot] == 1, mixed, 0.0).astype(BF16)
        for c in range(COLS):
            place, slot, many = (0, 0, COLS - c) if side == 0 else (COLS - c, 2 * REACH - c, c + 1)
            copy = pltpu.make_async_copy(
                held.at[c, pl.ds(place, many)], out.at[c, pl.ds(slot, many)], sems.at[side, c]
            )
            copy.start()
            copies.append(copy)
    for copy in copies:
        copy.wait()


def call(kernel, outs, ins, out_specs, scratch, flops, moved, **more):
    return pl.pallas_call(
        kernel,
        out_shape=outs,
        in_specs=ins,
        out_specs=out_specs,
        scratch_shapes=scratch,
        compiler_params=pltpu.CompilerParams(vmem_limit_bytes=LIMIT),
        cost_estimate=pl.CostEstimate(flops=flops, bytes_accessed=moved, transcendentals=0),
        **more,
    )


def shape(*dims, dtype=BF16):
    return jax.ShapeDtypeStruct(dims, dtype)


def per_device(density, pattern, orbitals):
    count = lax.axis_size(AXES)

    def to_right(array):
        return lax.ppermute(array, AXES, [(i, (i + 1) % count) for i in range(count)])

    def to_left(array):
        return lax.ppermute(array, AXES, [(i, (i - 1) % count) for i in range(count)])

    packed = call(
        pack_own,
        shape(PACKED, T),
        [ANY, SMEM, SMEM],
        VMEM,
        [pltpu.VMEM((COLS, COLS, T, T), BF16), pltpu.SemaphoreType.DMA((COLS,))],
        0,
        2**20,
    )(density, pattern, orbitals)
    own_left, own_right = to_right(packed), to_left(packed)
    wide, square, squared, packed_square = call(
        own_square,
        (shape(3 * SIDE, SIDE), shape(SIDE, SIDE, dtype=F32), shape(SIDE, SIDE), shape(PACKED, T)),
        [VMEM, SMEM, SMEM],
        (VMEM,) * 4,
        [],
        2**30,
        2**22,
    )(density, pattern, orbitals)
    square_left, square_right = to_right(packed_square), to_left(packed_square)
    acc, begun = call(
        middle,
        (shape(COLS, COLS + 1, T, T, dtype=F32), shape(*density.shape)),
        [VMEM, VMEM, VMEM, VMEM, VMEM, SMEM],
        (VMEM, ANY),
        [
            pltpu.VMEM((SIDE, SIDE), BF16),
            pltpu.VMEM((2, SIDE, SIDE), BF16),
            pltpu.VMEM((2 * T, 2 * T), F32),
            pltpu.VMEM((COLS, COLS, T, T), BF16),
            pltpu.SemaphoreType.DMA((COLS,)),
        ],
        2**31,
        2**22,
    )(own_left, own_right, wide, square, squared, pattern)
    return call(
        finish,
        shape(*density.shape),
        [VMEM, VMEM, VMEM, VMEM, SMEM, ANY],
        ANY,
        [
            pltpu.VMEM((SIDE, SIDE), BF16),
            pltpu.VMEM((2 * T, 2 * T), F32),
            pltpu.VMEM((COLS, COLS + 1, T, T), BF16),
            pltpu.SemaphoreType.DMA((2, COLS)),
        ],
        2**29,
        2**22,
        input_output_aliases={5: 0},
    )(square_left, square_right, wide, acc, pattern, begun)


def solution(mesh):
    placed = (P(AXES, None, None, None), P(AXES, None), P())
    return jax.shard_map(
        per_device, mesh=mesh, in_specs=placed, out_specs=P(AXES, None, None, None), check_vma=False
    )
```

time: 151 us -> 27.5 us (0.18)
  the two profiles are of different devices: /device:TPU:1 before, /device:TPU:0 now
where the time goes in v1:
time: 27.5 us; the launch traced here: 27.3 us
  starting transfers between devices  15.6 us (57%)
  Pallas kernels  8.5 us (31%)
  local copies, waits for them, and re-layouts  2.63 us (10%)
  waiting for transfers between devices  0.54 us (2%)
    ppermute x2, starting transfers between devices, to_left(): lax.ppermute(array, AXES, [(i, (i - 1) % count) for i in range(count)])  13.8 us
    pallas_call x1, Pallas kernels, per_device(): call(middle, (shape(COLS, COLS + 1, T, T, dtype=F32), shape(*density.shap...  3.55 us
    unnamed x6, local copies, waits for them, and re-layouts  2.63 us
    pallas_call x1, Pallas kernels, per_device(): call(finish, shape(*density.shape), [VMEM, VMEM, VMEM, VMEM, SMEM, ANY],...  1.97 us
    ppermute x2, starting transfers between devices, to_right(): lax.ppermute(array, AXES, [(i, (i + 1) % count) for i in range(count)])  1.82 us
    pallas_call x1, Pallas kernels, per_device(): call(own_square, (shape(3 * SIDE, SIDE), shape(SIDE, SIDE, dtype=F32), sh...  1.77 us
    pallas_call x1, Pallas kernels, per_device(): call(pack_own, shape(PACKED, T), [ANY, SMEM, SMEM], VMEM, [pltpu.VMEM((CO...  1.2 us
  transfers between devices with their start and end apart: 4, of which 1 were waited for; matrix products, arithmetic and copies ran while one was open for 0% of the time, Pallas kernels for 19%

profile of v1, /device:TPU:0, one launch (start us, length us, event | category | flops | bytes accessed | tf_op | source)
XLA Modules:
  0.0 27.3 jit_solution(14197796809640258855)
XLA Ops:
  0.0 0.0 copy-start
  0.0 1.3 %copy-done = bf16[4,9,128,128]{3,2,1,0:T(8,128)(2,1)S(1)} copy-done((bf16[4,9,128,128]{3,2,1,0:T(8,128)(2,1)S(1)}, bf16[4,9,128,128]{3,2,1,0:T(8,128)(2,1)}, u32[]{:S(2)}) %copy-start) | copy-done | bytes 1179672
  1.3 0.0 copy-start.1
  1.3 0.7 %copy-done.1 = s32[4,9]{1,0:T(4,128)S(1)} copy-done((s32[4,9]{1,0:T(4,128)S(1)}, s32[4,9]{1,0:T(4,128)}, u32[]{:S(2)}) %copy-start.1) | copy-done | bytes 168
  2.0 0.0 copy-start.2
  2.0 0.7 %copy-done.2 = s32[512]{0:T(512)S(1)} copy-done((s32[512]{0:T(512)S(1)}, s32[512]{0:T(512)}, u32[]{:S(2)}) %copy-start.2) | copy-done | bytes 2072
  2.6 1.2 %shard_map.38 = bf16[1040,128]{1,0:T(8,128)(2,1)S(1)} custom-call(bf16[4,9,128,128]{3,2,1,0:T(8,128)(2,1)S(1)} %copy-done, s32[4,9]{1,0:T(4,128)S(1)} %copy-done.1, s32[512]{0:T(512)S(1)} %copy-done.2), custom_call_target="tpu_custom_call" | custom-call | bytes 1048576 | tf_op jit(solution)/shard_map/pallas_call | solution.py:245
  3.8 1.7 %collective-permute-start.2 = (bf16[1040,128]{1,0:T(8,128)(2,1)S(1)}, bf16[1040,128]{1,0:T(8,128)(2,1)S(1)}, u32[]{:S(2)}, u32[]{:S(2)}) collective-permute-start(bf16[1040,128]{1,0:T(8,128)(2,1)S(1)} %shard_map.38), channel_id=1, source_target_pairs={{0,1},{1,2},{2,3},{3,4},{4,5},{5,6},{6,7},{7,8},{8,9},{9,10},{10,1... | collective-permute-start | bytes 798728 | tf_op jit(solution)/shard_map/ppermute | solution.py:240
  5.6 6.6 %collective-permute-start.3 = (bf16[1040,128]{1,0:T(8,128)(2,1)S(1)}, bf16[1040,128]{1,0:T(8,128)(2,1)S(1)}, u32[]{:S(2)}, u32[]{:S(2)}) collective-permute-start(bf16[1040,128]{1,0:T(8,128)(2,1)S(1)} %shard_map.38), channel_id=1, source_target_pairs={{0,127},{1,0},{2,1},{3,2},{4,3},{5,4},{6,5},{7,6},{8,7},{9,8},{10,... | collective-permute-start | bytes 798728 | tf_op jit(solution)/shard_map/ppermute | solution.py:243
  12.2 1.8 %shard_map.37 = (bf16[1536,512]{1,0:T(8,128)(2,1)S(1)}, f32[512,512]{1,0:T(8,128)S(1)}, bf16[512,512]{1,0:T(8,128)(2,1)S(1)}, bf16[1040,128]{1,0:T(8,128)(2,1)S(1)}) custom-call(bf16[4,9,128,128]{3,2,1,0:T(8,128)(2,1)S(1)} %copy-done, s32[4,9]{1,0:T(4,128)S(1)} %copy-done.1, s32[512]{0:T(512)S(1)} %copy-done.2), custom_call_target="tpu_custom_call" | custom-call | flops 1073741824 | bytes 4194304 | tf_op jit(solution)/shard_map/pallas_call | solution.py:255
  14.0 0.1 collective-permute-start
  14.1 7.2 %collective-permute-start.1 = (bf16[1040,128]{1,0:T(8,128)(2,1)S(1)}, bf16[1040,128]{1,0:T(8,128)(2,1)S(1)}, u32[]{:S(2)}, u32[]{:S(2)}) collective-permute-start(bf16[1040,128]{1,0:T(8,128)(2,1)S(1)} %get-tuple-element.11), channel_id=1, source_target_pairs={{0,127},{1,0},{2,1},{3,2},{4,3},{5,4},{6,5},{7,6},{8,7},{9,8},{10,... | collective-permute-start | bytes 798728 | tf_op jit(solution)/shard_map/ppermute | solution.py:243
  21.2 0.0 collective-permute-done.2.packed_left
  21.2 0.0 collective-permute-done.3.packed_right
  21.2 3.5 %shard_map.39 = (f32[4,5,128,128]{3,2,1,0:T(8,128)S(1)}, bf16[4,9,128,128]{3,2,1,0:T(8,128)(2,1)}) custom-call(bf16[1040,128]{1,0:T(8,128)(2,1)S(1)} %collective-permute-done.2.packed_left, bf16[1040,128]{1,0:T(8,128)(2,1)S(1)} %collective-permute-done.3.packed_right, bf16[1536,512]{1,0:T(8,128)(2,1)S(1)} %get-tuple-element.12.wide, ...), custom_call_target="tpu_custom_call" | custom-call | flops 2147483648 | bytes 4194304 | tf_op jit(solution)/shard_map/pallas_call | solution.py:265
  24.8 0.5 %collective-permute-done.packed_left = bf16[1040,128]{1,0:T(8,128)(2,1)S(1)} collective-permute-done((bf16[1040,128]{1,0:T(8,128)(2,1)S(1)}, bf16[1040,128]{1,0:T(8,128)(2,1)S(1)}, u32[]{:S(2)}, u32[]{:S(2)}) %collective-permute-start) | collective-permute-done | bytes 266272 | tf_op jit(solution)/shard_map/ppermute | solution.py:240
  25.3 0.0 collective-permute-done.1.packed_right
  25.3 2.0 %shard_map.40 = bf16[4,9,128,128]{3,2,1,0:T(8,128)(2,1)} custom-call(bf16[1040,128]{1,0:T(8,128)(2,1)S(1)} %collective-permute-done.packed_left, bf16[1040,128]{1,0:T(8,128)(2,1)S(1)} %collective-permute-done.1.packed_right, bf16[1536,512]{1,0:T(8,128)(2,1)S(1)} %get-tuple-element.12.wide, ...), custom_call_target="tpu_custom_call", output_to_operand_aliasing={{}: (5, {})} | custom-call | flops 536870912 | bytes 4194304 | tf_op jit(solution)/shard_map/pallas_call | solution.py:280
Async XLA Ops:
  0.0 1.3 %copy-start = (bf16[4,9,128,128]{3,2,1,0:T(8,128)(2,1)S(1)}, bf16[4,9,128,128]{3,2,1,0:T(8,128)(2,1)}, u32[]{:S(2)}) copy-start(bf16[4,9,128,128]{3,2,1,0:T(8,128)(2,1)} %density.3) | copy-start | bytes 3538948
  1.3 0.7 %copy-start.1 = (s32[4,9]{1,0:T(4,128)S(1)}, s32[4,9]{1,0:T(4,128)}, u32[]{:S(2)}) copy-start(s32[4,9]{1,0:T(4,128)} %pattern.7) | copy-start | bytes 436
  2.0 0.7 %copy-start.2 = (s32[512]{0:T(512)S(1)}, s32[512]{0:T(512)}, u32[]{:S(2)}) copy-start(s32[512]{0:T(512)} %orbitals.3) | copy-start | bytes 6148
  3.8 17.4 %collective-permute-start.2 = (bf16[1040,128]{1,0:T(8,128)(2,1)S(1)}, bf16[1040,128]{1,0:T(8,128)(2,1)S(1)}, u32[]{:S(2)}, u32[]{:S(2)}) collective-permute-start(bf16[1040,128]{1,0:T(8,128)(2,1)S(1)} %shard_map.38), channel_id=1, source_target_pairs={{0,1},{1,2},{2,3},{3,4},{4,5},{5,6},{6,7},{7,8},{8,9},{9,10},{10,1... | collective-permute-start | bytes 798728 | tf_op jit(solution)/shard_map/ppermute | solution.py:240
  5.6 15.7 %collective-permute-start.3 = (bf16[1040,128]{1,0:T(8,128)(2,1)S(1)}, bf16[1040,128]{1,0:T(8,128)(2,1)S(1)}, u32[]{:S(2)}, u32[]{:S(2)}) collective-permute-start(bf16[1040,128]{1,0:T(8,128)(2,1)S(1)} %shard_map.38), channel_id=1, source_target_pairs={{0,127},{1,0},{2,1},{3,2},{4,3},{5,4},{6,5},{7,6},{8,7},{9,8},{10,... | collective-permute-start | bytes 798728 | tf_op jit(solution)/shard_map/ppermute | solution.py:243
  14.0 11.3 %collective-permute-start = (bf16[1040,128]{1,0:T(8,128)(2,1)S(1)}, bf16[1040,128]{1,0:T(8,128)(2,1)S(1)}, u32[]{:S(2)}, u32[]{:S(2)}) collective-permute-start(bf16[1040,128]{1,0:T(8,128)(2,1)S(1)} %get-tuple-element.11), channel_id=1, source_target_pairs={{0,1},{1,2},{2,3},{3,4},{4,5},{5,6},{6,7},{7,8},{8,9},{9,10},{10,1... | collective-permute-start | bytes 798728 | tf_op jit(solution)/shard_map/ppermute | solution.py:240
  14.1 11.3 %collective-permute-start.1 = (bf16[1040,128]{1,0:T(8,128)(2,1)S(1)}, bf16[1040,128]{1,0:T(8,128)(2,1)S(1)}, u32[]{:S(2)}, u32[]{:S(2)}) collective-permute-start(bf16[1040,128]{1,0:T(8,128)(2,1)S(1)} %get-tuple-element.11), channel_id=1, source_target_pairs={{0,127},{1,0},{2,1},{3,2},{4,3},{5,4},{6,5},{7,6},{8,7},{9,8},{10,... | collective-permute-start | bytes 798728 | tf_op jit(solution)/shard_map/ppermute | solution.py:243

commit v2 on v1

--- a/solution.py
+++ b/solution.py
@@ -1,3 +1,5 @@
+import functools
+
 import jax
 import jax.numpy as jnp
 from jax import lax
@@ -81,29 +83,35 @@
         full_ref[at(2 * pair + 1), at(2 * pair + 1)] = second.astype(BF16)
 
 
-def pack_own(density, pattern, orbitals, out, held, sems):
-    first = lax.axis_index(AXES) * COLS
-    copies = [
-        pltpu.make_async_copy(
-            density.at[b, pl.ds(REACH, COLS - b)], held.at[b, pl.ds(0, COLS - b)], sems.at[b]
-        )
-        for b in range(COLS)
-    ]
+def load(pairs, sems):
+    copies = [pltpu.make_async_copy(source, target, sems.at[i]) for i, (source, target) in enumerate(pairs)]
     for copy in copies:
         copy.start()
+    return copies
+
+
+def pack_own(density, pattern, orbitals, out, held, pattern_now, orbitals_now, sems):
+    first = lax.axis_index(AXES) * COLS
+    pairs = [(density.at[b, pl.ds(REACH, COLS - b)], held.at[b, pl.ds(0, COLS - b)]) for b in range(COLS)]
+    copies = load([(orbitals, orbitals_now), (pattern, pattern_now)] + pairs, sems)
     row, col = rows_cols()
-    used = [orbitals[first + a] for a in range(COLS)]
     for copy in copies:
         copy.wait()
+    used = [orbitals_now[first + a] for a in range(COLS)]
 
     def block(a, b):
-        visible = (row < used[a] * pattern[b, a - b + REACH]) & (col < used[b])
+        visible = (row < used[a] * pattern_now[b, a - b + REACH]) & (col < used[b])
         return jnp.where(visible, held[b, a - b].astype(F32), 0.0)
 
     pack(out, block)
 
 
-def own_square(density, pattern, orbitals, wide, square, squared, packed):
+def own_square(density, pattern_far, orbitals_far, wide, square, squared, packed, kept, pattern, orbitals, sems):
+    for copy in load([(orbitals_far, orbitals), (pattern_far, pattern)], sems):
+        copy.wait()
+    for c in range(COLS):
+        for slot in range(BAND):
+            kept[c * BAND + slot : c * BAND + slot + 1, :] = jnp.full((1, T), pattern[c, slot], jnp.int32)
     count = orbitals.shape[0]
     first = lax.axis_index(AXES) * COLS
     used = [orbitals[lax.rem(first + r - REACH + count, count)] for r in range(COLS + 2 * REACH)]
@@ -140,6 +148,10 @@
                 yield a, c, a - c + 2 * REACH, COLS - c + a
 
 
+def keep(kept, c, slot):
+    return kept[c * BAND + slot : c * BAND + slot + 1, :] == 1
+
+
 TILES = (((0, 0), (1, 0), (1, 1)), ((0, 0), (0, 1), (1, 1)))
 
 
@@ -155,18 +167,21 @@
     return dot(thin[half(i), inner], full[inner, half(j)])
 
 
-def middle(packed_left, packed_right, wide, square, squared, pattern, acc, out, full, cross, tile_ref, held, sems):
+def middle(packed_first, packed_second, wide, square, squared, kept, acc, out, both, cross, tile_ref, held, sems):
     own = wide.at[SIDE : 2 * SIDE]
-    for side, packed in ((0, packed_left), (1, packed_right)):
+    odd = lax.rem(lax.axis_index(AXES), 2)
+    unpack(packed_first, both.at[1 - odd])
+    unpack(packed_second, both.at[odd])
+    for side in range(2):
+        full = both.at[side]
         thin = wide.at[side * 2 * SIDE : (side * 2 + 1) * SIDE]
         crossed = cross.at[side]
-        unpack(packed, full)
         crossed[...] = jnp.zeros((SIDE, SIDE), BF16)
         for tile in TILES[side]:
             tile_ref[...] = full_by_side(side, tile, full, thin) + side_by_full(side, tile, thin, own)
             for a, c, slot, place in side_blocks(side, tile):
                 block = tile_ref[at(a % 2), at(c % 2)]
-                crossed[at(a), at(c)] = jnp.where(pattern[c, slot] == 1, block, 0.0).astype(BF16)
+                crossed[at(a), at(c)] = jnp.where(keep(kept, c, slot), block, 0.0).astype(BF16)
                 acc[c, place] = 3.0 * block
         for tile in TILES[side]:
             tile_ref[...] = side_by_full(side, tile, crossed, own)
@@ -184,7 +199,7 @@
             for a in (2 * i, 2 * i + 1):
                 for c in (2 * j, 2 * j + 1):
                     mixed = 3.0 * square[at(a), at(c)] - 2.0 * tile_ref[at(a % 2), at(c % 2)]
-                    held[c, a] = jnp.where(pattern[c, a - c + REACH] == 1, mixed, 0.0).astype(BF16)
+                    held[c, a] = jnp.where(keep(kept, c, a - c + REACH), mixed, 0.0).astype(BF16)
     copies = [
         pltpu.make_async_copy(held.at[c], out.at[c, pl.ds(REACH - c, COLS)], sems.at[c]) for c in range(COLS)
     ]
@@ -194,26 +209,35 @@
         copy.wait()
 
 
-def finish(packed_left, packed_right, wide, acc, pattern, begun, out, full, tile_ref, held, sems):
+def finish(turn, packed, wide, acc, kept, begun, out, full, tile_ref, held, sems):
     del begun
-    copies = []
-    for side, packed in ((0, packed_left), (1, packed_right)):
+    odd = lax.rem(lax.axis_index(AXES), 2)
+    unpack(packed, full)
+
+    def one(side):
         thin = wide.at[side * 2 * SIDE : (side * 2 + 1) * SIDE]
-        unpack(packed, full)
         for tile in TILES[side]:
             tile_ref[...] = full_by_side(side, tile, full, thin)
             for a, c, slot, place in side_blocks(side, tile):
                 mixed = acc[c, place] - 2.0 * tile_ref[at(a % 2), at(c % 2)]
-                held[c, place] = jnp.where(pattern[c, slot] == 1, mixed, 0.0).astype(BF16)
+                held[c, place] = jnp.where(keep(kept, c, slot), mixed, 0.0).astype(BF16)
+        copies = []
         for c in range(COLS):
             place, slot, many = (0, 0, COLS - c) if side == 0 else (COLS - c, 2 * REACH - c, c + 1)
-            copy = pltpu.make_async_copy(
-                held.at[c, pl.ds(place, many)], out.at[c, pl.ds(slot, many)], sems.at[side, c]
+            copies.append(
+                pltpu.make_async_copy(held.at[c, pl.ds(place, many)], out.at[c, pl.ds(slot, many)], sems.at[c])
             )
-            copy.start()
-            copies.append(copy)
-    for copy in copies:
-        copy.wait()
+            copies[-1].start()
+        for copy in copies:
+            copy.wait()
+
+    @pl.when(odd == turn)
+    def _():
+        one(1)
+
+    @pl.when(odd != turn)
+    def _():
+        one(0)
 
 
 def call(kernel, outs, ins, out_specs, scratch, flops, moved, **more):
@@ -236,39 +260,46 @@
 def per_device(density, pattern, orbitals):
     count = lax.axis_size(AXES)
 
-    def to_right(array):
-        return lax.ppermute(array, AXES, [(i, (i + 1) % count) for i in range(count)])
-
-    def to_left(array):
-        return lax.ppermute(array, AXES, [(i, (i - 1) % count) for i in range(count)])
-
+    def exchange(array):
+        first = [(i, i ^ 1) for i in range(count)]
+        second = [(i, (i + 1 if i % 2 else i - 1) % count) for i in range(count)]
+        return lax.ppermute(array, AXES, first), lax.ppermute(array, AXES, second)
+
+    far = [pltpu.with_memory_space_constraint(array, pltpu.HBM) for array in (density, pattern, orbitals)]
+    small = [pltpu.SMEM(pattern.shape, jnp.int32), pltpu.SMEM(orbitals.shape, jnp.int32)]
     packed = call(
         pack_own,
         shape(PACKED, T),
-        [ANY, SMEM, SMEM],
+        [ANY] * 3,
         VMEM,
-        [pltpu.VMEM((COLS, COLS, T, T), BF16), pltpu.SemaphoreType.DMA((COLS,))],
+        [pltpu.VMEM((COLS, COLS, T, T), BF16), *small, pltpu.SemaphoreType.DMA((COLS + 2,))],
         0,
         2**20,
-    )(density, pattern, orbitals)
-    own_left, own_right = to_right(packed), to_left(packed)
-    wide, square, squared, packed_square = call(
+    )(*far)
+    own_first, own_second = exchange(packed)
+    wide, square, squared, packed_square, kept = call(
         own_square,
-        (shape(3 * SIDE, SIDE), shape(SIDE, SIDE, dtype=F32), shape(SIDE, SIDE), shape(PACKED, T)),
-        [VMEM, SMEM, SMEM],
-        (VMEM,) * 4,
-        [],
+        (
+            shape(3 * SIDE, SIDE),
+            shape(SIDE, SIDE, dtype=F32),
+            shape(SIDE, SIDE),
+            shape(PACKED, T),
+            shape(40, T, dtype=jnp.int32),
+        ),
+        [VMEM, ANY, ANY],
+        (VMEM,) * 5,
+        [*small, pltpu.SemaphoreType.DMA((2,))],
         2**30,
         2**22,
-    )(density, pattern, orbitals)
-    square_left, square_right = to_right(packed_square), to_left(packed_square)
+    )(density, *far[1:])
+    square_first, square_second = exchange(packed_square)
     acc, begun = call(
         middle,
         (shape(COLS, COLS + 1, T, T, dtype=F32), shape(*density.shape)),
-        [VMEM, VMEM, VMEM, VMEM, VMEM, SMEM],
+        [VMEM] * 6,
         (VMEM, ANY),
         [
-            pltpu.VMEM((SIDE, SIDE), BF16),
+            pltpu.VMEM((2, SIDE, SIDE), BF16),
             pltpu.VMEM((2, SIDE, SIDE), BF16),
             pltpu.VMEM((2 * T, 2 * T), F32),
             pltpu.VMEM((COLS, COLS, T, T), BF16),
@@ -276,22 +307,25 @@
         ],
         2**31,
         2**22,
-    )(own_left, own_right, wide, square, squared, pattern)
-    return call(
-        finish,
-        shape(*density.shape),
-        [VMEM, VMEM, VMEM, VMEM, SMEM, ANY],
-        ANY,
-        [
-            pltpu.VMEM((SIDE, SIDE), BF16),
-            pltpu.VMEM((2 * T, 2 * T), F32),
-            pltpu.VMEM((COLS, COLS + 1, T, T), BF16),
-            pltpu.SemaphoreType.DMA((2, COLS)),
-        ],
-        2**29,
-        2**22,
-        input_output_aliases={5: 0},
-    )(square_left, square_right, wide, acc, pattern, begun)
+    )(own_first, own_second, wide, square, squared, kept)
+    out = begun
+    for turn, packed in enumerate((square_first, square_second)):
+        out = call(
+            functools.partial(finish, turn),
+            shape(*density.shape),
+            [VMEM] * 4 + [ANY],
+            ANY,
+            [
+                pltpu.VMEM((SIDE, SIDE), BF16),
+                pltpu.VMEM((2 * T, 2 * T), F32),
+                pltpu.VMEM((COLS, COLS + 1, T, T), BF16),
+                pltpu.SemaphoreType.DMA((COLS,)),
+            ],
+            2**28,
+            2**21,
+            input_output_aliases={4: 0},
+        )(packed, wide, acc, kept, out)
+    return out
 
 
 def solution(mesh):

time: 27.5 us -> 24.8 us (0.902)
  starting transfers between devices: 15.6 us -> 9.83 us
  waiting for transfers between devices: 0.54 us -> 5.93 us
  local copies, waits for them, and re-layouts: 2.63 us -> 0.01 us
  Pallas kernels: 8.5 us -> 8.84 us
    ppermute x4, starting transfers between devices: 15.6 us -> 9.83 us  [exchange(): return (lax.ppermute(array, AXES, first), lax.ppermute(array, AXES, second))]
    ppermute x4, waiting for transfers between devices: 0.54 us -> 5.93 us  [exchange(): return (lax.ppermute(array, AXES, first), lax.ppermute(array, AXES, second))]
    unnamed x6 -> x2, local copies, waits for them, and re-layouts: 2.63 us -> 0.01 us
    pallas_call x2 -> x3, Pallas kernels: 3.18 us -> 3.81 us  [the longest x2 2.56 us: per_device(): call(functools.partial(finish, turn), shape(*density.shape), [VMEM] * 4 +...]
    pallas_call x1, Pallas kernels: 3.55 us -> 3.12 us  [per_device(): call(middle, (shape(COLS, COLS + 1, T, T, dtype=F32), shape(*density.shap...]
  transfers between devices with their start and end apart: 4 -> 4, of which waited for: 1 -> 3; matrix products, arithmetic and copies ran while one was open for 0% -> 0% of each run, Pallas kernels for 19% -> 26%
where the time goes in v2:
time: 24.8 us; the launch traced here: 24.6 us
  starting transfers between devices  9.83 us (40%)
  Pallas kernels  8.84 us (36%)
  waiting for transfers between devices  5.93 us (24%)
    ppermute x4, starting transfers between devices, exchange(): return (lax.ppermute(array, AXES, first), lax.ppermute(array, AXES, second))  9.83 us
    ppermute x4, waiting for transfers between devices, exchange(): return (lax.ppermute(array, AXES, first), lax.ppermute(array, AXES, second))  5.93 us
    pallas_call x1, Pallas kernels, per_device(): call(middle, (shape(COLS, COLS + 1, T, T, dtype=F32), shape(*density.shap...  3.12 us
    pallas_call x2, Pallas kernels, per_device(): call(functools.partial(finish, turn), shape(*density.shape), [VMEM] * 4 +...  2.56 us
    pallas_call x1, Pallas kernels, per_device(): call(own_square, (shape(3 * SIDE, SIDE), shape(SIDE, SIDE, dtype=F32), sh...  1.92 us
    pallas_call x1, Pallas kernels, per_device(): call(pack_own, shape(PACKED, T), [ANY] * 3, VMEM, [pltpu.VMEM((COLS, COLS...  1.24 us
  transfers between devices with their start and end apart: 4, of which 3 were waited for; matrix products, arithmetic and copies ran while one was open for 0% of the time, Pallas kernels for 26%

profile of v2, /device:TPU:0, one launch (start us, length us, event | category | flops | bytes accessed | tf_op | source)
XLA Modules:
  0.0 24.6 jit_solution(12999977989686111311)
XLA Ops:
  0.0 0.0 copy-start
  0.0 1.2 %shard_map.38 = bf16[1040,128]{1,0:T(8,128)(2,1)S(1)} custom-call(bf16[4,9,128,128]{3,2,1,0:T(8,128)(2,1)} %density.3, s32[4,9]{1,0:T(4,128)} %pattern.1, s32[512]{0:T(512)} %orbitals.1), custom_call_target="tpu_custom_call" | custom-call | bytes 1048576 | tf_op jit(solution)/shard_map/pallas_call | solution.py:270
  1.3 1.7 %collective-permute-start.1 = (bf16[1040,128]{1,0:T(8,128)(2,1)S(1)}, bf16[1040,128]{1,0:T(8,128)(2,1)S(1)}, u32[]{:S(2)}, u32[]{:S(2)}) collective-permute-start(bf16[1040,128]{1,0:T(8,128)(2,1)S(1)} %shard_map.38), channel_id=1, source_target_pairs={{0,1},{1,0},{2,3},{3,2},{4,5},{5,4},{6,7},{7,6},{8,9},{9,8},{10,11... | collective-permute-start | bytes 798728 | tf_op jit(solution)/shard_map/ppermute | solution.py:266
  3.0 7.0 %collective-permute-start.2 = (bf16[1040,128]{1,0:T(8,128)(2,1)S(1)}, bf16[1040,128]{1,0:T(8,128)(2,1)S(1)}, u32[]{:S(2)}, u32[]{:S(2)}) collective-permute-start(bf16[1040,128]{1,0:T(8,128)(2,1)S(1)} %shard_map.38), channel_id=1, source_target_pairs={{0,127},{1,2},{2,1},{3,4},{4,3},{5,6},{6,5},{7,8},{8,7},{9,10},{10... | collective-permute-start | bytes 798728 | tf_op jit(solution)/shard_map/ppermute | solution.py:266
  10.0 0.0 copy-done
  10.0 1.9 %shard_map.37 = (bf16[1536,512]{1,0:T(8,128)(2,1)S(1)}, f32[512,512]{1,0:T(8,128)S(1)}, bf16[512,512]{1,0:T(8,128)(2,1)S(1)}, bf16[1040,128]{1,0:T(8,128)(2,1)S(1)}, s32[40,128]{1,0:T(8,128)S(1)}) custom-call(bf16[4,9,128,128]{3,2,1,0:T(8,128)(2,1)S(1)} %copy-done, s32[4,9]{1,0:T(4,128)} %pattern.1, s32[512]{0:T(512)} %orbitals.1), custom_call_target="tpu_custom_call" | custom-call | flops 1073741824 | bytes 4194304 | tf_op jit(solution)/shard_map/pallas_call | solution.py:280
  11.9 0.1 collective-permute-start.3
  12.0 1.0 %collective-permute-start = (bf16[1040,128]{1,0:T(8,128)(2,1)S(1)}, bf16[1040,128]{1,0:T(8,128)(2,1)S(1)}, u32[]{:S(2)}, u32[]{:S(2)}) collective-permute-start(bf16[1040,128]{1,0:T(8,128)(2,1)S(1)} %get-tuple-element.12), channel_id=1, source_target_pairs={{0,127},{1,2},{2,1},{3,4},{4,3},{5,6},{6,5},{7,8},{8,7},{9,10},{10... | collective-permute-start | bytes 798728 | tf_op jit(solution)/shard_map/ppermute | solution.py:266
  13.0 0.0 collective-permute-done.1.packed_first
  13.0 1.4 %collective-permute-done.2.packed_second = bf16[1040,128]{1,0:T(8,128)(2,1)S(1)} collective-permute-done((bf16[1040,128]{1,0:T(8,128)(2,1)S(1)}, bf16[1040,128]{1,0:T(8,128)(2,1)S(1)}, u32[]{:S(2)}, u32[]{:S(2)}) %collective-permute-start.2) | collective-permute-done | bytes 266272 | tf_op jit(solution)/shard_map/ppermute | solution.py:266
  14.4 3.1 %shard_map.39 = (f32[4,5,128,128]{3,2,1,0:T(8,128)S(1)}, bf16[4,9,128,128]{3,2,1,0:T(8,128)(2,1)}) custom-call(bf16[1040,128]{1,0:T(8,128)(2,1)S(1)} %collective-permute-done.1.packed_first, bf16[1040,128]{1,0:T(8,128)(2,1)S(1)} %collective-permute-done.2.packed_second, bf16[1536,512]{1,0:T(8,128)(2,1)S(1)} %get-tuple-element.13.wide, ...), custom_call_target="tpu_custom_call" | custom-call | flops 2147483648 | bytes 4194304 | tf_op jit(solution)/shard_map/pallas_call | solution.py:296
  17.5 0.9 %collective-permute-done.3.packed = bf16[1040,128]{1,0:T(8,128)(2,1)S(1)} collective-permute-done((bf16[1040,128]{1,0:T(8,128)(2,1)S(1)}, bf16[1040,128]{1,0:T(8,128)(2,1)S(1)}, u32[]{:S(2)}, u32[]{:S(2)}) %collective-permute-start.3) | collective-permute-done | bytes 266272 | tf_op jit(solution)/shard_map/ppermute | solution.py:266
  18.4 1.3 %shard_map.40.begun = bf16[4,9,128,128]{3,2,1,0:T(8,128)(2,1)} custom-call(bf16[1040,128]{1,0:T(8,128)(2,1)S(1)} %collective-permute-done.3.packed, bf16[1536,512]{1,0:T(8,128)(2,1)S(1)} %get-tuple-element.13.wide, f32[4,5,128,128]{3,2,1,0:T(8,128)S(1)} %get-tuple-element.17.acc, ...), custom_call_target="tpu_custom_call", output_to_operand_aliasing={{}: (4, {})} | custom-call | flops 268435456 | bytes 2097152 | tf_op jit(solution)/shard_map/pallas_call | solution.py:313
  19.7 3.7 %collective-permute-done.packed = bf16[1040,128]{1,0:T(8,128)(2,1)S(1)} collective-permute-done((bf16[1040,128]{1,0:T(8,128)(2,1)S(1)}, bf16[1040,128]{1,0:T(8,128)(2,1)S(1)}, u32[]{:S(2)}, u32[]{:S(2)}) %collective-permute-start) | collective-permute-done | bytes 266272 | tf_op jit(solution)/shard_map/ppermute | solution.py:266
  23.4 1.3 %shard_map.41 = bf16[4,9,128,128]{3,2,1,0:T(8,128)(2,1)} custom-call(bf16[1040,128]{1,0:T(8,128)(2,1)S(1)} %collective-permute-done.packed, bf16[1536,512]{1,0:T(8,128)(2,1)S(1)} %get-tuple-element.13.wide, f32[4,5,128,128]{3,2,1,0:T(8,128)S(1)} %get-tuple-element.17.acc, s32[40,128]{1,0:T(8,128)S(1)} %get-tuple-element.16.kept, ...), custom_call_target="tpu_custom_call", output_to_operand_aliasing={{}: (4, {})} | custom-call | flops 268435456 | bytes 2097152 | tf_op jit(solution)/shard_map/pallas_call | solution.py:313
Async XLA Ops:
  0.0 10.0 %copy-start = (bf16[4,9,128,128]{3,2,1,0:T(8,128)(2,1)S(1)}, bf16[4,9,128,128]{3,2,1,0:T(8,128)(2,1)}, u32[]{:S(2)}) copy-start(bf16[4,9,128,128]{3,2,1,0:T(8,128)(2,1)} %density.3) | copy-start | bytes 3538948
  1.3 11.8 %collective-permute-start.1 = (bf16[1040,128]{1,0:T(8,128)(2,1)S(1)}, bf16[1040,128]{1,0:T(8,128)(2,1)S(1)}, u32[]{:S(2)}, u32[]{:S(2)}) collective-permute-start(bf16[1040,128]{1,0:T(8,128)(2,1)S(1)} %shard_map.38), channel_id=1, source_target_pairs={{0,1},{1,0},{2,3},{3,2},{4,5},{5,4},{6,7},{7,6},{8,9},{9,8},{10,11... | collective-permute-start | bytes 798728 | tf_op jit(solution)/shard_map/ppermute | solution.py:266
  3.0 11.4 %collective-permute-start.2 = (bf16[1040,128]{1,0:T(8,128)(2,1)S(1)}, bf16[1040,128]{1,0:T(8,128)(2,1)S(1)}, u32[]{:S(2)}, u32[]{:S(2)}) collective-permute-start(bf16[1040,128]{1,0:T(8,128)(2,1)S(1)} %shard_map.38), channel_id=1, source_target_pairs={{0,127},{1,2},{2,1},{3,4},{4,3},{5,6},{6,5},{7,8},{8,7},{9,10},{10... | collective-permute-start | bytes 798728 | tf_op jit(solution)/shard_map/ppermute | solution.py:266
  11.9 6.5 %collective-permute-start.3 = (bf16[1040,128]{1,0:T(8,128)(2,1)S(1)}, bf16[1040,128]{1,0:T(8,128)(2,1)S(1)}, u32[]{:S(2)}, u32[]{:S(2)}) collective-permute-start(bf16[1040,128]{1,0:T(8,128)(2,1)S(1)} %get-tuple-element.12), channel_id=1, source_target_pairs={{0,1},{1,0},{2,3},{3,2},{4,5},{5,4},{6,7},{7,6},{8,9},{9,8},{10,11... | collective-permute-start | bytes 798728 | tf_op jit(solution)/shard_map/ppermute | solution.py:266
  12.0 11.4 %collective-permute-start = (bf16[1040,128]{1,0:T(8,128)(2,1)S(1)}, bf16[1040,128]{1,0:T(8,128)(2,1)S(1)}, u32[]{:S(2)}, u32[]{:S(2)}) collective-permute-start(bf16[1040,128]{1,0:T(8,128)(2,1)S(1)} %get-tuple-element.12), channel_id=1, source_target_pairs={{0,127},{1,2},{2,1},{3,4},{4,3},{5,6},{6,5},{7,8},{8,7},{9,10},{10... | collective-permute-start | bytes 798728 | tf_op jit(solution)/shard_map/ppermute | solution.py:266

commit v3 on v2

v3 whole, which is shorter than its diff:
```python
import jax
import jax.numpy as jnp
from jax import lax
from jax.experimental import pallas as pl
from jax.experimental.pallas import tpu as pltpu
from jax.sharding import PartitionSpec as P

AXES = ("blk", "rep")
T = 128
COLS = 4
REACH = 4
BAND = 9
SIDE = COLS * T
BELOW = [(a, b) for b in range(COLS) for a in range(b + 1, COLS)]
PACKED = (len(BELOW) + COLS // 2) * T + 16
F32 = jnp.float32
BF16 = jnp.bfloat16
LIMIT = 40 * 1024 * 1024

VMEM = pl.BlockSpec(memory_space=pltpu.VMEM)
SMEM = pl.BlockSpec(memory_space=pltpu.SMEM)
ANY = pl.BlockSpec(memory_space=pl.ANY)


def rows_cols():
    return (
        lax.broadcasted_iota(jnp.int32, (T, T), 0),
        lax.broadcasted_iota(jnp.int32, (T, T), 1),
    )


def at(index):
    return slice(index * T, (index + 1) * T)


def dot(a, b):
    return lax.dot_general(a, b, (((1,), (0,)), ((), ())), preferred_element_type=F32)


def dot_tn(a, b):
    return lax.dot_general(a, b, (((0,), (0,)), ((), ())), preferred_element_type=F32)


def pack(out_ref, block):
    row, col = rows_cols()
    for index, (a, b) in enumerate(BELOW):
        out_ref[at(index), :] = block(a, b).astype(BF16)
    strip_row = lax.broadcasted_iota(jnp.int32, (16, T), 0)
    strip = jnp.zeros((16, T), F32)
    for pair in range(COLS // 2):
        first = block(2 * pair, 2 * pair).astype(F32)
        second = block(2 * pair + 1, 2 * pair + 1).astype(F32)
        out_ref[at(len(BELOW) + pair), :] = jnp.where(row >= col, first, second).astype(BF16)
        diagonal = jnp.sum(jnp.where(row == col, second, 0.0), axis=0, keepdims=True)
        strip = jnp.where(strip_row == pair, diagonal, strip)
    out_ref[PACKED - 16 : PACKED, :] = strip.astype(BF16)


def unpack(read, full_ref):
    row, col = rows_cols()
    for index, (a, b) in enumerate(BELOW):
        block = read(at(index))
        full_ref[at(a), at(b)] = block
        full_ref[at(b), at(a)] = block.T
    strip = read(slice(PACKED - 16, PACKED)).astype(F32)
    for pair in range(COLS // 2):
        both = read(at(len(BELOW) + pair)).astype(F32)
        turned = both.T
        first = jnp.where(row >= col, both, turned)
        second = jnp.where(row < col, both, turned)
        second = jnp.where(row == col, strip[pair : pair + 1, :], second)
        full_ref[at(2 * pair), at(2 * pair)] = first.astype(BF16)
        full_ref[at(2 * pair + 1), at(2 * pair + 1)] = second.astype(BF16)


def load(pairs, sems):
    copies = [pltpu.make_async_copy(source, target, sems.at[i]) for i, (source, target) in enumerate(pairs)]
    for copy in copies:
        copy.start()
    return copies


def pack_own(density, pattern, orbitals, out, held, pattern_now, orbitals_now, sems):
    first = lax.axis_index(AXES) * COLS
    pairs = [(density.at[b, pl.ds(REACH, COLS - b)], held.at[b, pl.ds(0, COLS - b)]) for b in range(COLS)]
    copies = load([(orbitals, orbitals_now), (pattern, pattern_now)] + pairs, sems)
    row, col = rows_cols()
    for copy in copies:
        copy.wait()
    used = [orbitals_now[first + a] for a in range(COLS)]

    def block(a, b):
        visible = (row < used[a] * pattern_now[b, a - b + REACH]) & (col < used[b])
        return jnp.where(visible, held[b, a - b].astype(F32), 0.0)

    pack(out, block)


def span(first, last):
    return slice(2 * first * T, 2 * (last + 1) * T)


RANGE = ((span(0, 1), span(1, 1)), (span(0, 0), span(0, 1)))
HALVES = (span(0, 0), span(1, 1))


def side_blocks(side):
    place = 0
    for c in range(COLS):
        for a in range(c, COLS) if side == 0 else range(c + 1):
            yield a, c, a - c + 2 * REACH * side, place
            place += 1


def keep(kept, c, slot):
    return kept[c * BAND + slot : c * BAND + slot + 1, :] == 1


def side_of(wide, side):
    return wide.at[side * 2 * SIDE : (side * 2 + 1) * SIDE]


def side_by_own(side, thin, own, out):
    if side == 0:
        out[HALVES[0], HALVES[0]] = dot(thin[HALVES[0], HALVES[0]], own[HALVES[0], HALVES[0]])
        out[HALVES[1], :] = dot(thin[HALVES[1], :], own[...])
    else:
        out[HALVES[0], :] = dot(thin[HALVES[0], :], own[...])
        out[HALVES[1], HALVES[1]] = dot(thin[HALVES[1], HALVES[1]], own[HALVES[1], HALVES[1]])


def full_by_side(side, half_col, full, thin):
    rows = RANGE[side][half_col]
    return dot(full[rows, rows], thin[rows, HALVES[half_col]])


def add_turned(side, left, right, out):
    if side == 0:
        out[HALVES[0], HALVES[0]] += dot_tn(left[:, HALVES[0]], right[:, HALVES[0]])
        out[HALVES[0], HALVES[1]] += dot_tn(left[HALVES[1], HALVES[0]], right[HALVES[1], HALVES[1]])
        out[HALVES[1], :] += dot_tn(left[HALVES[1], HALVES[1]], right[HALVES[1], :])
    else:
        out[HALVES[0], :] += dot_tn(left[HALVES[0], HALVES[0]], right[HALVES[0], :])
        out[HALVES[1], HALVES[0]] += dot_tn(left[HALVES[0], HALVES[1]], right[HALVES[0], HALVES[0]])
        out[HALVES[1], HALVES[1]] += dot_tn(left[:, HALVES[1]], right[:, HALVES[1]])


def own_square(
    density, pattern_far, orbitals_far, packed_own, wide, square, packed, packed_both, kept, local, cube, pattern, orbitals, squared, sems
):
    copies = load([(orbitals_far, orbitals), (pattern_far, pattern)], sems)
    packed_both[:PACKED, :] = packed_own[...]
    for copy in copies:
        copy.wait()
    for c in range(COLS):
        for slot in range(BAND):
            kept[c * BAND + slot : c * BAND + slot + 1, :] = jnp.full((1, T), pattern[c, slot], jnp.int32)
    count = orbitals.shape[0]
    first = lax.axis_index(AXES) * COLS
    used = [orbitals[lax.rem(first + r - REACH + count, count)] for r in range(COLS + 2 * REACH)]
    row, col = rows_cols()
    zero = jnp.zeros((T, T), BF16)
    for c in range(COLS):
        for r in range(COLS + 2 * REACH):
            if c <= r < c + BAND:
                visible = (row < used[r] * pattern[c, r - c]) & (col < used[c + REACH])
                wide[at(r), at(c)] = jnp.where(visible, density[c, r - c].astype(F32), 0.0).astype(BF16)
            else:
                wide[at(r), at(c)] = zero
    own = wide.at[SIDE : 2 * SIDE]
    square[...] = dot(own[...], own[...])
    for side in range(2):
        add_turned(side, side_of(wide, side), side_of(wide, side), square)
    for b in range(COLS):
        for a in range(COLS):
            squared[at(a), at(b)] = jnp.where(pattern[b, a - b + REACH] == 1, square[at(a), at(b)], 0.0).astype(BF16)
    pack(packed, lambda a, b: squared[at(a), at(b)])
    packed_both[PACKED:, :] = packed[...]
    cube[...] = dot(squared[...], own[...])
    for side in range(2):
        side_by_own(side, side_of(wide, side), own, local.at[side])


def by_side(turn, one):
    odd = lax.rem(lax.axis_index(AXES), 2)

    @pl.when(odd == turn)
    def _():
        one(1)

    @pl.when(odd != turn)
    def _():
        one(0)


def second_reader(swapped, to_first, to_last, offset):
    me = lax.axis_index(AXES)
    last = lax.axis_size(AXES) - 1

    def read(rows):
        late = to_last[rows.start + offset : rows.stop + offset, :]
        return jnp.where(me == 0, to_first[rows, :], jnp.where(me == last, late, swapped[rows, :]))

    return read


def cross_step(side, full, wide, kept, local, crossed, acc, cube):
    thin, own = side_of(wide, side), wide.at[SIDE : 2 * SIDE]
    for j in range(2):
        local[side, RANGE[side][j], HALVES[j]] += full_by_side(side, j, full, thin)
    crossed[...] = jnp.zeros((SIDE, SIDE), BF16)
    for a, c, slot, place in side_blocks(side):
        crossed[at(a), at(c)] = jnp.where(keep(kept, c, slot), local[side, at(a), at(c)], 0.0).astype(BF16)
    side_by_own(side, crossed, own, acc)
    for a, c, slot, place in side_blocks(side):
        acc[at(a), at(c)] = 3.0 * local[side, at(a), at(c)] - 2.0 * acc[at(a), at(c)]
    add_turned(side, crossed, thin, cube)


def cross_first(packed, wide, kept, local_far, cube_far, acc, cube, full, local, crossed):
    unpack(lambda rows: packed[rows, :], full)
    cube[...] = cube_far[...]

    def one(side):
        local[side] = local_far[side]
        cross_step(side, full, wide, kept, local, crossed, acc, cube)

    by_side(0, one)


def cross_second(
    packed, to_first, to_last, wide, kept, local_far, cube_far, square, acc, out, cube, full, local, crossed, held, sems
):
    unpack(second_reader(packed, to_first, to_last, 0), full)
    cube[...] = cube_far[...]

    def one(side):
        local[side] = local_far[side]
        cross_step(side, full, wide, kept, local, crossed, acc, cube)

    by_side(1, one)
    copies = []
    for c in range(COLS):
        for a in range(COLS):
            mixed = 3.0 * square[at(a), at(c)] - 2.0 * cube[at(a), at(c)]
            held[c, a] = jnp.where(keep(kept, c, a - c + REACH), mixed, 0.0).astype(BF16)
        copies.append(pltpu.make_async_copy(held.at[c], out.at[c, pl.ds(REACH - c, COLS)], sems.at[c]))
        copies[-1].start()
    for copy in copies:
        copy.wait()


def finish(
    packed_first, packed_second, to_first, to_last, wide, kept, acc_first, acc_second, begun, out, full, held, sems
):
    del begun
    unpack(lambda rows: packed_first[rows, :], full.at[0])
    unpack(second_reader(packed_second, to_first, to_last, PACKED), full.at[1])

    def one(turn, acc, side):
        thin = side_of(wide, side)
        cross = [full_by_side(side, j, full.at[turn], thin) for j in range(2)]
        copies = []
        start = 0
        blocks = list(side_blocks(side))
        for c in range(COLS):
            here = [block for block in blocks if block[1] == c]
            for a, _, slot, place in here:
                top = a * T - RANGE[side][c // 2].start
                mixed = acc[at(a), at(c)] - 2.0 * cross[c // 2][top : top + T, at(c % 2)]
                held[turn, place] = jnp.where(keep(kept, c, slot), mixed, 0.0).astype(BF16)
            copies.append(
                pltpu.make_async_copy(
                    held.at[turn, pl.ds(here[0][3], len(here))],
                    out.at[c, pl.ds(here[0][2], len(here))],
                    sems.at[turn, c],
                )
            )
            copies[-1].start()
        return copies

    def both(side):
        for copy in one(0, acc_first, side) + one(1, acc_second, 1 - side):
            copy.wait()

    by_side(0, both)


def call(kernel, outs, ins, out_specs, scratch, flops, moved, **more):
    return pl.pallas_call(
        kernel,
        out_shape=outs,
        in_specs=ins,
        out_specs=out_specs,
        scratch_shapes=scratch,
        compiler_params=pltpu.CompilerParams(vmem_limit_bytes=LIMIT),
        cost_estimate=pl.CostEstimate(flops=flops, bytes_accessed=moved, transcendentals=0),
        **more,
    )


def shape(*dims, dtype=BF16):
    return jax.ShapeDtypeStruct(dims, dtype)


def per_device(density, pattern, orbitals):
    count = lax.axis_size(AXES)
    pairs = [(i, i ^ 1) for i in range(count)]
    others = [(i, i + 1 if i % 2 else i - 1) for i in range(1, count - 1)]
    last = count - 1

    def send(array, to):
        return lax.ppermute(array, AXES, to)

    far = [pltpu.with_memory_space_constraint(array, pltpu.HBM) for array in (density, pattern, orbitals)]
    small = [pltpu.SMEM(pattern.shape, jnp.int32), pltpu.SMEM(orbitals.shape, jnp.int32)]
    whole = pltpu.VMEM((SIDE, SIDE), BF16)
    wide_f32 = shape(SIDE, SIDE, dtype=F32)
    packed = call(
        pack_own,
        shape(PACKED, T),
        [ANY] * 3,
        VMEM,
        [pltpu.VMEM((COLS, COLS, T, T), BF16), *small, pltpu.SemaphoreType.DMA((COLS + 2,))],
        0,
        2**20,
    )(*far)
    own_first = send(packed, pairs)
    own_to_first = send(packed, [(last, 0)])
    own_second = send(packed, others)
    wide, square, packed_square, packed_both, kept, local, cube = call(
        own_square,
        (
            shape(3 * SIDE, SIDE),
            wide_f32,
            shape(PACKED, T),
            shape(2 * PACKED, T),
            shape(40, T, dtype=jnp.int32),
            shape(2, SIDE, SIDE, dtype=F32),
            wide_f32,
        ),
        [VMEM, ANY, ANY, VMEM],
        (VMEM,) * 7,
        [*small, whole, pltpu.SemaphoreType.DMA((2,))],
        2**30,
        2**22,
    )(density, *far[1:], packed)
    square_first = send(packed_square, pairs)
    square_to_first = send(packed_square, [(last, 0)])
    square_second = send(packed_square, others)
    to_last = send(packed_both, [(0, last)])
    crossing = [whole, pltpu.VMEM((2, SIDE, SIDE), F32), whole]
    acc_first, cube = call(
        cross_first,
        (wide_f32, wide_f32),
        [VMEM] * 5,
        (VMEM, VMEM),
        crossing,
        2**30,
        2**21,
    )(own_first, wide, kept, local, cube)
    acc_second, begun = call(
        cross_second,
        (wide_f32, shape(*density.shape)),
        [VMEM] * 8,
        (VMEM, ANY),
        [
            pltpu.VMEM((SIDE, SIDE), F32),
            *crossing,
            pltpu.VMEM((COLS, COLS, T, T), BF16),
            pltpu.SemaphoreType.DMA((COLS,)),
        ],
        2**30,
        2**21,
    )(own_second, own_to_first, to_last, wide, kept, local, cube, square)
    return call(
        finish,
        shape(*density.shape),
        [VMEM] * 8 + [ANY],
        ANY,
        [
            pltpu.VMEM((2, SIDE, SIDE), BF16),
            pltpu.VMEM((2, 10, T, T), BF16),
            pltpu.SemaphoreType.DMA((2, COLS)),
        ],
        2**28,
        2**21,
        input_output_aliases={8: 0},
    )(square_first, square_second, square_to_first, to_last, wide, kept, acc_first, acc_second, begun)


def solution(mesh):
    placed = (P(AXES, None, None, None), P(AXES, None), P())
    return jax.shard_map(
        per_device, mesh=mesh, in_specs=placed, out_specs=P(AXES, None, None, None), check_vma=False
    )
```

time: 24.8 us -> 36.3 us (1.46)
  starting transfers between devices: 9.83 us -> 16.9 us
  waiting for transfers between devices: 5.93 us -> 10.5 us
  Pallas kernels: 8.84 us -> 8.43 us
    ppermute x4 -> x7, starting transfers between devices: 9.83 us -> 16.9 us  [send(): return lax.ppermute(array, AXES, to)]
    ppermute x4 -> x7, waiting for transfers between devices: 5.93 us -> 10.5 us  [send(): return lax.ppermute(array, AXES, to)]
    pallas_call x4, Pallas kernels: 7.6 us -> 7.18 us  [the longest x1 2.53 us: per_device(): call(own_square, (shape(3 * SIDE, SIDE), wide_f32, shape(PACKED, T), shap...]
  transfers between devices with their start and end apart: 4 -> 7, of which waited for: 3 -> 3; matrix products, arithmetic and copies ran while one was open for 0% -> 0% of each run, Pallas kernels for 26% -> 9%
where the time goes in v3:
time: 36.3 us; the launch traced here: 36 us
  starting transfers between devices  16.9 us (47%)
  waiting for transfers between devices  10.5 us (29%)
  Pallas kernels  8.43 us (23%)
    ppermute x7, starting transfers between devices, send(): return lax.ppermute(array, AXES, to)  16.9 us
    ppermute x7, waiting for transfers between devices, send(): return lax.ppermute(array, AXES, to)  10.5 us
    pallas_call x1, Pallas kernels, per_device(): call(own_square, (shape(3 * SIDE, SIDE), wide_f32, shape(PACKED, T), shap...  2.53 us
    pallas_call x1, Pallas kernels, per_device(): call(cross_second, (wide_f32, shape(*density.shape)), [VMEM] * 8, (VMEM,...  2.04 us
    pallas_call x1, Pallas kernels, per_device(): call(finish, shape(*density.shape), [VMEM] * 8 + [ANY], ANY, [pltpu.VMEM(...  1.59 us
    pallas_call x1, Pallas kernels, per_device(): call(pack_own, shape(PACKED, T), [ANY] * 3, VMEM, [pltpu.VMEM((COLS, COLS...  1.24 us
    pallas_call x1, Pallas kernels, per_device(): call(cross_first, (wide_f32, wide_f32), [VMEM] * 5, (VMEM, VMEM), crossin...  1.03 us
  transfers between devices with their start and end apart: 7, of which 3 were waited for; matrix products, arithmetic and copies ran while one was open for 0% of the time, Pallas kernels for 9%

profile of v3, /device:TPU:0, one launch (start us, length us, event | category | flops | bytes accessed | tf_op | source)
XLA Modules:
  0.0 36.0 jit_solution(15660142095734672939)
XLA Ops:
  0.0 0.0 copy-start
  0.0 1.2 %shard_map.37.packed_own = bf16[1040,128]{1,0:T(8,128)(2,1)S(1)} custom-call(bf16[4,9,128,128]{3,2,1,0:T(8,128)(2,1)} %density.3, s32[4,9]{1,0:T(4,128)} %pattern_far.1, s32[512]{0:T(512)} %orbitals_far.1), custom_call_target="tpu_custom_call" | custom-call | bytes 1048576 | tf_op jit(solution)/shard_map/pallas_call | solution.py:319
  1.3 0.2 copy-done
  1.4 2.5 %shard_map.38 = (bf16[1536,512]{1,0:T(8,128)(2,1)S(1)}, f32[512,512]{1,0:T(8,128)S(1)}, bf16[1040,128]{1,0:T(8,128)(2,1)S(1)}, bf16[2080,128]{1,0:T(8,128)(2,1)S...) custom-call(bf16[4,9,128,128]{3,2,1,0:T(8,128)(2,1)S(1)} %copy-done, ...), custom_call_target="tpu_custom_call" | custom-call | flops 1073741824 | bytes 4194304 | tf_op jit(solution)/shard_map/pallas_call | solution.py:331
  4.0 10.1 %collective-permute-start.3 = (bf16[2080,128]{1,0:T(8,128)(2,1)S(1)}, bf16[2080,128]{1,0:T(8,128)(2,1)S(1)}, u32[]{:S(2)}, u32[]{:S(2)}) collective-permute-start(bf16[2080,128]{1,0:T(8,128)(2,1)S(1)} %get-tuple-element.17), channel_id=1, source_target_pairs={{0,127}} | collective-permute-start | bytes 1597448 | tf_op jit(solution)/shard_map/ppermute | solution.py:313
  14.1 0.1 collective-permute-start.4
  14.2 0.7 %collective-permute-start.5 = (bf16[1040,128]{1,0:T(8,128)(2,1)S(1)}, bf16[1040,128]{1,0:T(8,128)(2,1)S(1)}, u32[]{:S(2)}, u32[]{:S(2)}) collective-permute-start(bf16[1040,128]{1,0:T(8,128)(2,1)S(1)} %shard_map.37.packed_own), channel_id=1, source_target_pairs={{1,2},{2,1},{3,4},{4,3},{5,6},{6,5},{7,8},{8,7},{9,10},{10,9},{11,... | collective-permute-start | bytes 798728 | tf_op jit(solution)/shard_map/ppermute | solution.py:313
  14.9 1.3 %collective-permute-start.6 = (bf16[1040,128]{1,0:T(8,128)(2,1)S(1)}, bf16[1040,128]{1,0:T(8,128)(2,1)S(1)}, u32[]{:S(2)}, u32[]{:S(2)}) collective-permute-start(bf16[1040,128]{1,0:T(8,128)(2,1)S(1)} %shard_map.37.packed_own), channel_id=1, source_target_pairs={{127,0}} | collective-permute-start | bytes 798728 | tf_op jit(solution)/shard_map/ppermute | solution.py:313
  16.2 2.7 %collective-permute-start = (bf16[1040,128]{1,0:T(8,128)(2,1)S(1)}, bf16[1040,128]{1,0:T(8,128)(2,1)S(1)}, u32[]{:S(2)}, u32[]{:S(2)}) collective-permute-start(bf16[1040,128]{1,0:T(8,128)(2,1)S(1)} %get-tuple-element.16), channel_id=1, source_target_pairs={{0,1},{1,0},{2,3},{3,2},{4,5},{5,4},{6,7},{7,6},{8,9},{9,8},{10,11... | collective-permute-start | bytes 798728 | tf_op jit(solution)/shard_map/ppermute | solution.py:313
  18.9 1.7 %collective-permute-done.4.packed = bf16[1040,128]{1,0:T(8,128)(2,1)S(1)} collective-permute-done((bf16[1040,128]{1,0:T(8,128)(2,1)S(1)}, bf16[1040,128]{1,0:T(8,128)(2,1)S(1)}, u32[]{:S(2)}, u32[]{:S(2)}) %collective-permute-start.4) | collective-permute-done | bytes 266272 | tf_op jit(solution)/shard_map/ppermute | solution.py:313
  20.6 0.7 %collective-permute-start.1 = (bf16[1040,128]{1,0:T(8,128)(2,1)S(1)}, bf16[1040,128]{1,0:T(8,128)(2,1)S(1)}, u32[]{:S(2)}, u32[]{:S(2)}) collective-permute-start(bf16[1040,128]{1,0:T(8,128)(2,1)S(1)} %get-tuple-element.16), channel_id=1, source_target_pairs={{1,2},{2,1},{3,4},{4,3},{5,6},{6,5},{7,8},{8,7},{9,10},{10,9},{11,... | collective-permute-start | bytes 798728 | tf_op jit(solution)/shard_map/ppermute | solution.py:313
  21.3 0.0 collective-permute-done.5.packed
  21.3 1.3 %collective-permute-start.2 = (bf16[1040,128]{1,0:T(8,128)(2,1)S(1)}, bf16[1040,128]{1,0:T(8,128)(2,1)S(1)}, u32[]{:S(2)}, u32[]{:S(2)}) collective-permute-start(bf16[1040,128]{1,0:T(8,128)(2,1)S(1)} %get-tuple-element.16), channel_id=1, source_target_pairs={{127,0}} | collective-permute-start | bytes 798728 | tf_op jit(solution)/shard_map/ppermute | solution.py:313
  22.6 1.0 %shard_map.39 = (f32[512,512]{1,0:T(8,128)S(1)}, f32[512,512]{1,0:T(8,128)S(1)}) custom-call(bf16[1040,128]{1,0:T(8,128)(2,1)S(1)} %collective-permute-done.4.packed, bf16[1536,512]{1,0:T(8,128)(2,1)S(1)} %get-tuple-element.18.wide, s32[40,128]{1,0:T(8,128)S(1)} %get-tuple-element.19.kept, f32[2,512,512]{2,1,0:T(8,128)S(1)} %get-tuple-element.20.local_far, ...), custom_call_target="tpu_custom_call" | custom-call | flops 1073741824 | bytes 2097152 | tf_op jit(solution)/shard_map/pallas_call | solution.py:353
  23.6 4.5 %collective-permute-done.6.to_first = bf16[1040,128]{1,0:T(8,128)(2,1)S(1)} collective-permute-done((bf16[1040,128]{1,0:T(8,128)(2,1)S(1)}, bf16[1040,128]{1,0:T(8,128)(2,1)S(1)}, u32[]{:S(2)}, u32[]{:S(2)}) %collective-permute-start.6) | collective-permute-done | bytes 266272 | tf_op jit(solution)/shard_map/ppermute | solution.py:313
  28.2 0.0 collective-permute-done.3.to_last
  28.2 2.0 %shard_map.40 = (f32[512,512]{1,0:T(8,128)S(1)}, bf16[4,9,128,128]{3,2,1,0:T(8,128)(2,1)}) custom-call(bf16[1040,128]{1,0:T(8,128)(2,1)S(1)} %collective-permute-done.5.packed, bf16[1040,128]{1,0:T(8,128)(2,1)S(1)} %collective-permute-done.6.to_first, bf16[2080,128]{1,0:T(8,128)(2,1)S(1)} %collective-permute-done.3.to_last, ...), custom_call_target="tpu_custom_call" | custom-call | flops 1073741824 | bytes 2097152 | tf_op jit(solution)/shard_map/pallas_call | solution.py:362
  30.2 0.0 collective-permute-done.packed_first
  30.2 0.0 collective-permute-done.1.packed_second
  30.2 4.2 %collective-permute-done.2.to_first = bf16[1040,128]{1,0:T(8,128)(2,1)S(1)} collective-permute-done((bf16[1040,128]{1,0:T(8,128)(2,1)S(1)}, bf16[1040,128]{1,0:T(8,128)(2,1)S(1)}, u32[]{:S(2)}, u32[]{:S(2)}) %collective-permute-start.2) | collective-permute-done | bytes 266272 | tf_op jit(solution)/shard_map/ppermute | solution.py:313
  34.5 1.6 %shard_map.41 = bf16[4,9,128,128]{3,2,1,0:T(8,128)(2,1)} custom-call(bf16[1040,128]{1,0:T(8,128)(2,1)S(1)} %collective-permute-done.packed_first, bf16[1040,128]{1,0:T(8,128)(2,1)S(1)} %collective-permute-done.1.packed_second, bf16[1040,128]{1,0:T(8,128)(2,1)S(1)} %collective-permute-done.2.to_first, ...), custom_call_target="tpu_custom_call", output_to_operand_aliasing={{}: (8, {})} | custom-call | flops 268435456 | bytes 2097152 | tf_op jit(solution)/shard_map/pallas_call | solution.py:376
Async XLA Ops:
  0.0 1.4 %copy-start = (bf16[4,9,128,128]{3,2,1,0:T(8,128)(2,1)S(1)}, bf16[4,9,128,128]{3,2,1,0:T(8,128)(2,1)}, u32[]{:S(2)}) copy-start(bf16[4,9,128,128]{3,2,1,0:T(8,128)(2,1)} %density.3) | copy-start | bytes 3538948
  4.0 24.2 %collective-permute-start.3 = (bf16[2080,128]{1,0:T(8,128)(2,1)S(1)}, bf16[2080,128]{1,0:T(8,128)(2,1)S(1)}, u32[]{:S(2)}, u32[]{:S(2)}) collective-permute-start(bf16[2080,128]{1,0:T(8,128)(2,1)S(1)} %get-tuple-element.17), channel_id=1, source_target_pairs={{0,127}} | collective-permute-start | bytes 1597448 | tf_op jit(solution)/shard_map/ppermute | solution.py:313
  14.1 6.5 %collective-permute-start.4 = (bf16[1040,128]{1,0:T(8,128)(2,1)S(1)}, bf16[1040,128]{1,0:T(8,128)(2,1)S(1)}, u32[]{:S(2)}, u32[]{:S(2)}) collective-permute-start(bf16[1040,128]{1,0:T(8,128)(2,1)S(1)} %shard_map.37.packed_own), channel_id=1, source_target_pairs={{0,1},{1,0},{2,3},{3,2},{4,5},{5,4},{6,7},{7,6},{8,9},{9,8},{10,11... | collective-permute-start | bytes 798728 | tf_op jit(solution)/shard_map/ppermute | solution.py:313
  14.2 7.1 %collective-permute-start.5 = (bf16[1040,128]{1,0:T(8,128)(2,1)S(1)}, bf16[1040,128]{1,0:T(8,128)(2,1)S(1)}, u32[]{:S(2)}, u32[]{:S(2)}) collective-permute-start(bf16[1040,128]{1,0:T(8,128)(2,1)S(1)} %shard_map.37.packed_own), channel_id=1, source_target_pairs={{1,2},{2,1},{3,4},{4,3},{5,6},{6,5},{7,8},{8,7},{9,10},{10,9},{11,... | collective-permute-start | bytes 798728 | tf_op jit(solution)/shard_map/ppermute | solution.py:313
  14.9 13.3 %collective-permute-start.6 = (bf16[1040,128]{1,0:T(8,128)(2,1)S(1)}, bf16[1040,128]{1,0:T(8,128)(2,1)S(1)}, u32[]{:S(2)}, u32[]{:S(2)}) collective-permute-start(bf16[1040,128]{1,0:T(8,128)(2,1)S(1)} %shard_map.37.packed_own), channel_id=1, source_target_pairs={{127,0}} | collective-permute-start | bytes 798728 | tf_op jit(solution)/shard_map/ppermute | solution.py:313
  16.2 14.0 %collective-permute-start = (bf16[1040,128]{1,0:T(8,128)(2,1)S(1)}, bf16[1040,128]{1,0:T(8,128)(2,1)S(1)}, u32[]{:S(2)}, u32[]{:S(2)}) collective-permute-start(bf16[1040,128]{1,0:T(8,128)(2,1)S(1)} %get-tuple-element.16), channel_id=1, source_target_pairs={{0,1},{1,0},{2,3},{3,2},{4,5},{5,4},{6,7},{7,6},{8,9},{9,8},{10,11... | collective-permute-start | bytes 798728 | tf_op jit(solution)/shard_map/ppermute | solution.py:313
  20.6 9.6 %collective-permute-start.1 = (bf16[1040,128]{1,0:T(8,128)(2,1)S(1)}, bf16[1040,128]{1,0:T(8,128)(2,1)S(1)}, u32[]{:S(2)}, u32[]{:S(2)}) collective-permute-start(bf16[1040,128]{1,0:T(8,128)(2,1)S(1)} %get-tuple-element.16), channel_id=1, source_target_pairs={{1,2},{2,1},{3,4},{4,3},{5,6},{6,5},{7,8},{8,7},{9,10},{10,9},{11,... | collective-permute-start | bytes 798728 | tf_op jit(solution)/shard_map/ppermute | solution.py:313
  21.3 13.2 %collective-permute-start.2 = (bf16[1040,128]{1,0:T(8,128)(2,1)S(1)}, bf16[1040,128]{1,0:T(8,128)(2,1)S(1)}, u32[]{:S(2)}, u32[]{:S(2)}) collective-permute-start(bf16[1040,128]{1,0:T(8,128)(2,1)S(1)} %get-tuple-element.16), channel_id=1, source_target_pairs={{127,0}} | collective-permute-start | bytes 798728 | tf_op jit(solution)/shard_map/ppermute | solution.py:313

commit v4 on v3

v4 whole, which is shorter than its diff:
```python
import jax
import jax.numpy as jnp
from jax import lax
from jax.experimental import pallas as pl
from jax.experimental.pallas import tpu as pltpu
from jax.sharding import PartitionSpec as P

AXES = ("blk", "rep")
T = 128
COLS = 4
REACH = 4
BAND = 9
SIDE = COLS * T
BELOW = [(a, b) for b in range(COLS) for a in range(b + 1, COLS)]
PACKED = (len(BELOW) + COLS // 2) * T + 16
F32 = jnp.float32
BF16 = jnp.bfloat16
LIMIT = 40 * 1024 * 1024

VMEM = pl.BlockSpec(memory_space=pltpu.VMEM)
SMEM = pl.BlockSpec(memory_space=pltpu.SMEM)
ANY = pl.BlockSpec(memory_space=pl.ANY)


def rows_cols():
    return (
        lax.broadcasted_iota(jnp.int32, (T, T), 0),
        lax.broadcasted_iota(jnp.int32, (T, T), 1),
    )


def at(index):
    return slice(index * T, (index + 1) * T)


def dot(a, b):
    return lax.dot_general(a, b, (((1,), (0,)), ((), ())), preferred_element_type=F32)


def dot_tn(a, b):
    return lax.dot_general(a, b, (((0,), (0,)), ((), ())), preferred_element_type=F32)


def pack(out_ref, block):
    row, col = rows_cols()
    for index, (a, b) in enumerate(BELOW):
        out_ref[at(index), :] = block(a, b).astype(BF16)
    strip_row = lax.broadcasted_iota(jnp.int32, (16, T), 0)
    strip = jnp.zeros((16, T), F32)
    for pair in range(COLS // 2):
        first = block(2 * pair, 2 * pair).astype(F32)
        second = block(2 * pair + 1, 2 * pair + 1).astype(F32)
        out_ref[at(len(BELOW) + pair), :] = jnp.where(row >= col, first, second).astype(BF16)
        diagonal = jnp.sum(jnp.where(row == col, second, 0.0), axis=0, keepdims=True)
        strip = jnp.where(strip_row == pair, diagonal, strip)
    out_ref[PACKED - 16 : PACKED, :] = strip.astype(BF16)


def unpack(read, full_ref):
    row, col = rows_cols()
    for index, (a, b) in enumerate(BELOW):
        block = read(at(index))
        full_ref[at(a), at(b)] = block
        full_ref[at(b), at(a)] = block.T
    strip = read(slice(PACKED - 16, PACKED)).astype(F32)
    for pair in range(COLS // 2):
        both = read(at(len(BELOW) + pair)).astype(F32)
        turned = both.T
        first = jnp.where(row >= col, both, turned)
        second = jnp.where(row < col, both, turned)
        second = jnp.where(row == col, strip[pair : pair + 1, :], second)
        full_ref[at(2 * pair), at(2 * pair)] = first.astype(BF16)
        full_ref[at(2 * pair + 1), at(2 * pair + 1)] = second.astype(BF16)


def load(pairs, sems):
    copies = [pltpu.make_async_copy(source, target, sems.at[i]) for i, (source, target) in enumerate(pairs)]
    for copy in copies:
        copy.start()
    return copies


def pack_own(density, pattern, orbitals, out, counts, held, pattern_now, orbitals_now, sems):
    first = lax.axis_index(AXES) * COLS
    pairs = [(density.at[b, pl.ds(REACH, COLS - b)], held.at[b, pl.ds(0, COLS - b)]) for b in range(COLS)]
    copies = load([(orbitals, orbitals_now), (pattern, pattern_now)] + pairs, sems)
    row, col = rows_cols()
    for copy in copies[:2]:
        copy.wait()
    total = orbitals.shape[0]
    used = [orbitals_now[lax.rem(first + r - REACH + total, total)] for r in range(COLS + 2 * REACH)]
    seen = {}
    for c in range(COLS):
        for slot in range(BAND):
            seen[c, slot] = used[c + slot] * pattern_now[c, slot]
    for copy in copies[2:]:
        copy.wait()

    def block(a, b):
        visible = (row < seen[b, a - b + REACH]) & (col < used[b + REACH])
        return jnp.where(visible, held[b, a - b].astype(F32), 0.0)

    pack(out, block)
    for c in range(COLS):
        for slot in range(BAND):
            counts[count_row(c, slot), :] = jnp.full((1, T), seen[c, slot], jnp.int32)
        counts[COLS * BAND + c : COLS * BAND + c + 1, :] = jnp.full((1, T), used[c + REACH], jnp.int32)


def count_row(c, slot):
    return slice(c * BAND + slot, c * BAND + slot + 1)


def span(first, last):
    return slice(2 * first * T, 2 * (last + 1) * T)


RANGE = ((span(0, 1), span(1, 1)), (span(0, 0), span(0, 1)))
HALVES = (span(0, 0), span(1, 1))


def side_blocks(side):
    place = 0
    for c in range(COLS):
        for a in range(c, COLS) if side == 0 else range(c + 1):
            yield a, c, a - c + 2 * REACH * side, place
            place += 1


def keep(counts, c, slot):
    return counts[count_row(c, slot), :] > 0


def side_of(wide, side):
    return wide.at[side * 2 * SIDE : (side * 2 + 1) * SIDE]


def side_by_own(side, thin, own, out):
    if side == 0:
        out[HALVES[0], HALVES[0]] = dot(thin[HALVES[0], HALVES[0]], own[HALVES[0], HALVES[0]])
        out[HALVES[1], :] = dot(thin[HALVES[1], :], own[...])
    else:
        out[HALVES[0], :] = dot(thin[HALVES[0], :], own[...])
        out[HALVES[1], HALVES[1]] = dot(thin[HALVES[1], HALVES[1]], own[HALVES[1], HALVES[1]])


def full_by_side(side, half_col, full, thin):
    rows = RANGE[side][half_col]
    return dot(full[rows, rows], thin[rows, HALVES[half_col]])


def add_turned(side, left, right, before, out, lower=False):
    low, high = HALVES
    if side == 0:
        out[low, low] = before[low, low] + dot_tn(left[:, low], right[:, low])
        if not lower:
            out[low, high] = before[low, high] + dot_tn(left[high, low], right[high, high])
        out[high, :] = before[high, :] + dot_tn(left[high, high], right[high, :])
    else:
        inner = low if lower else slice(0, SIDE)
        out[low, inner] = before[low, inner] + dot_tn(left[low, low], right[low, inner])
        out[high, low] = before[high, low] + dot_tn(left[low, high], right[low, low])
        out[high, high] = before[high, high] + dot_tn(left[:, high], right[:, high])


def own_square(density, counts, packed_own, wide, square, squared, packed, both):
    row, col = rows_cols()
    zero = jnp.zeros((T, T), BF16)
    both[:PACKED, :] = packed_own[...]
    for c in range(COLS):
        in_cols = col < counts[COLS * BAND + c : COLS * BAND + c + 1, :]
        for r in range(COLS + 2 * REACH):
            if c <= r < c + BAND:
                visible = (row < counts[count_row(c, r - c), :]) & in_cols
                wide[at(r), at(c)] = jnp.where(visible, density[c, r - c].astype(F32), 0.0).astype(BF16)
            else:
                wide[at(r), at(c)] = zero
    own = wide.at[SIDE : 2 * SIDE]
    low, high = HALVES
    square[low, low] = dot(own[low, :], own[:, low])
    square[high, :] = dot(own[high, :], own[...])
    for side in range(2):
        add_turned(side, side_of(wide, side), side_of(wide, side), square, square, lower=True)
    for b in range(COLS):
        for a in range(b, COLS):
            block = jnp.where(keep(counts, b, a - b + REACH), square[at(a), at(b)], 0.0).astype(BF16)
            squared[at(a), at(b)] = block
    pack(packed, lambda a, b: squared[at(a), at(b)])
    both[PACKED:, :] = packed[...]


def own_products(wide, squared, local, cube, full):
    own = wide.at[SIDE : 2 * SIDE]
    full[...] = squared[...]
    for b in range(COLS):
        for a in range(b):
            full[at(a), at(b)] = squared[at(b), at(a)].T
    cube[...] = dot(full[...], own[...])
    for side in range(2):
        side_by_own(side, side_of(wide, side), own, local.at[side])


def by_side(turn, one):
    odd = lax.rem(lax.axis_index(AXES), 2)

    @pl.when(odd == turn)
    def _():
        one(1)

    @pl.when(odd != turn)
    def _():
        one(0)


def second_reader(swapped, to_last, offset):
    is_last = lax.axis_index(AXES) == lax.axis_size(AXES) - 1

    def read(rows):
        return jnp.where(is_last, to_last[rows.start + offset : rows.stop + offset, :], swapped[rows, :])

    return read


def cross_step(side, full, wide, counts, local, crossed, acc, before, cube):
    thin, own = side_of(wide, side), wide.at[SIDE : 2 * SIDE]
    for j in range(2):
        rows = RANGE[side][j]
        acc[rows, HALVES[j]] = local[side, rows, HALVES[j]] + full_by_side(side, j, full, thin)
    for a in range(COLS):
        for c in range(COLS):
            if (a >= c) if side == 0 else (a <= c):
                block = jnp.where(keep(counts, c, a - c + 2 * REACH * side), acc[at(a), at(c)], 0.0).astype(BF16)
            else:
                block = jnp.zeros((T, T), BF16)
            crossed[at(a), at(c)] = block
    low, high = HALVES
    for rows, inner, cols in (
        ((low, low, low), (high, slice(0, SIDE), slice(0, SIDE)))
        if side == 0
        else ((low, slice(0, SIDE), slice(0, SIDE)), (high, high, high))
    ):
        acc[rows, cols] = 3.0 * acc[rows, cols] - 2.0 * dot(crossed[rows, inner], own[inner, cols])
    add_turned(side, crossed, thin, before, cube)


def cross_first(packed, wide, counts, local, before, acc, cube, full, crossed):
    unpack(lambda rows: packed[rows, :], full)
    by_side(0, lambda side: cross_step(side, full, wide, counts, local, crossed, acc, before, cube))


def cross_second(packed, to_last, wide, counts, local, before, square, acc, out, cube, full, crossed, held, sems):
    unpack(second_reader(packed, to_last, 0), full)
    by_side(1, lambda side: cross_step(side, full, wide, counts, local, crossed, acc, before, cube))
    copies = []
    for c in range(COLS):
        for a in range(COLS):
            own = square[at(a), at(c)] if a // 2 >= c // 2 else square[at(c), at(a)].T
            mixed = 3.0 * own - 2.0 * cube[at(a), at(c)]
            held[c, a] = jnp.where(keep(counts, c, a - c + REACH), mixed, 0.0).astype(BF16)
        copies.append(pltpu.make_async_copy(held.at[c], out.at[c, pl.ds(REACH - c, COLS)], sems.at[c]))
        copies[-1].start()
    for copy in copies:
        copy.wait()


def finish(
    packed_first, packed_second, to_last, wide, counts, acc_first, acc_second, begun, out, full, held, sems
):
    del begun
    unpack(lambda rows: packed_first[rows, :], full.at[0])
    unpack(second_reader(packed_second, to_last, PACKED), full.at[1])

    def one(turn, acc, side):
        thin = side_of(wide, side)
        cross = [full_by_side(side, j, full.at[turn], thin) for j in range(2)]
        copies = []
        start = 0
        blocks = list(side_blocks(side))
        for c in range(COLS):
            here = [block for block in blocks if block[1] == c]
            for a, _, slot, place in here:
                top = a * T - RANGE[side][c // 2].start
                mixed = acc[at(a), at(c)] - 2.0 * cross[c // 2][top : top + T, at(c % 2)]
                held[turn, place] = jnp.where(keep(counts, c, slot), mixed, 0.0).astype(BF16)
            copies.append(
                pltpu.make_async_copy(
                    held.at[turn, pl.ds(here[0][3], len(here))],
                    out.at[c, pl.ds(here[0][2], len(here))],
                    sems.at[turn, c],
                )
            )
            copies[-1].start()
        return copies

    def both(side):
        for copy in one(0, acc_first, side) + one(1, acc_second, 1 - side):
            copy.wait()

    by_side(0, both)


def call(kernel, outs, ins, out_specs, scratch, flops, moved, **more):
    return pl.pallas_call(
        kernel,
        out_shape=outs,
        in_specs=ins,
        out_specs=out_specs,
        scratch_shapes=scratch,
        compiler_params=pltpu.CompilerParams(vmem_limit_bytes=LIMIT),
        cost_estimate=pl.CostEstimate(flops=flops, bytes_accessed=moved, transcendentals=0),
        **more,
    )


def shape(*dims, dtype=BF16):
    return jax.ShapeDtypeStruct(dims, dtype)


def per_device(density, pattern, orbitals):
    count = lax.axis_size(AXES)
    last = count - 1
    pairs = [(i, i ^ 1) for i in range(count)]
    others = [(i, (i + 1) % count if i % 2 else i - 1) for i in range(1, count)]

    def send(array, to):
        return lax.ppermute(array, AXES, to)

    far = [pltpu.with_memory_space_constraint(array, pltpu.HBM) for array in (density, pattern, orbitals)]
    whole = pltpu.VMEM((SIDE, SIDE), BF16)
    whole_f32 = shape(SIDE, SIDE, dtype=F32)
    packed, counts = call(
        pack_own,
        (shape(PACKED, T), shape(COLS * BAND + COLS, T, dtype=jnp.int32)),
        [ANY] * 3,
        (VMEM,) * 2,
        [
            pltpu.VMEM((COLS, COLS, T, T), BF16),
            pltpu.SMEM(pattern.shape, jnp.int32),
            pltpu.SMEM(orbitals.shape, jnp.int32),
            pltpu.SemaphoreType.DMA((COLS + 2,)),
        ],
        0,
        2**20,
    )(*far)
    own_first = send(packed, pairs)
    own_second = send(packed, others)
    wide, square, squared, packed_square, both = call(
        own_square,
        (shape(3 * SIDE, SIDE), whole_f32, shape(SIDE, SIDE), shape(PACKED, T), shape(2 * PACKED, T)),
        [VMEM] * 3,
        (VMEM,) * 5,
        [],
        2**30,
        2**22,
    )(density, counts, packed)
    square_first = send(packed_square, pairs)
    square_second = send(packed_square, others)
    to_last = send(both, [(0, last)])
    local, cube = call(
        own_products,
        (shape(2, SIDE, SIDE, dtype=F32), whole_f32),
        [VMEM] * 2,
        (VMEM,) * 2,
        [whole],
        17179869184,
        2**20,
    )(wide, squared)
    acc_first, cube = call(
        cross_first,
        (whole_f32, whole_f32),
        [VMEM] * 5,
        (VMEM, VMEM),
        [whole, whole],
        17179869184,
        2**20,
    )(own_first, wide, counts, local, cube)
    acc_second, begun = call(
        cross_second,
        (whole_f32, shape(*density.shape)),
        [VMEM] * 7,
        (VMEM, ANY),
        [
            pltpu.VMEM((SIDE, SIDE), F32),
            whole,
            whole,
            pltpu.VMEM((COLS, COLS, T, T), BF16),
            pltpu.SemaphoreType.DMA((COLS,)),
        ],
        2**30,
        2**21,
    )(own_second, to_last, wide, counts, local, cube, square)
    return call(
        finish,
        shape(*density.shape),
        [VMEM] * 7 + [ANY],
        ANY,
        [
            pltpu.VMEM((2, SIDE, SIDE), BF16),
            pltpu.VMEM((2, 10, T, T), BF16),
            pltpu.SemaphoreType.DMA((2, COLS)),
        ],
        2**28,
        2**21,
        input_output_aliases={7: 0},
    )(square_first, square_second, to_last, wide, counts, acc_first, acc_second, begun)


def solution(mesh):
    placed = (P(AXES, None, None, None), P(AXES, None), P())
    return jax.shard_map(
        per_device, mesh=mesh, in_specs=placed, out_specs=P(AXES, None, None, None), check_vma=False
    )
```

time: 36.3 us -> 30.4 us (0.84)
  waiting for transfers between devices: 10.5 us -> 4.9 us
  Pallas kernels: 8.43 us -> 7.6 us
  starting transfers between devices: 16.9 us -> 17.6 us
    ppermute x7 -> x5, waiting for transfers between devices: 10.5 us -> 4.9 us  [send(): return lax.ppermute(array, AXES, to)]
    pallas_call x5 -> x6, Pallas kernels: 8.43 us -> 7.6 us  [the longest x1 1.96 us: per_device(): call(cross_second, (whole_f32, shape(*density.shape)), [VMEM] * 7, (VMEM,...]
    ppermute x7 -> x5, starting transfers between devices: 16.9 us -> 17.6 us  [send(): return lax.ppermute(array, AXES, to)]
  transfers between devices with their start and end apart: 7 -> 5, of which waited for: 3 -> 1; matrix products, arithmetic and copies ran while one was open for 0% -> 0% of each run, Pallas kernels for 9% -> 16%
where the time goes in v4:
time: 30.4 us; the launch traced here: 30.2 us
  starting transfers between devices  17.6 us (58%)
  Pallas kernels  7.6 us (25%)
  waiting for transfers between devices  4.9 us (16%)
    ppermute x5, starting transfers between devices, send(): return lax.ppermute(array, AXES, to)  17.6 us
    ppermute x5, waiting for transfers between devices, send(): return lax.ppermute(array, AXES, to)  4.9 us
    pallas_call x1, Pallas kernels, per_device(): call(cross_second, (whole_f32, shape(*density.shape)), [VMEM] * 7, (VMEM,...  1.96 us
    pallas_call x1, Pallas kernels, per_device(): call(finish, shape(*density.shape), [VMEM] * 7 + [ANY], ANY, [pltpu.VMEM(...  1.58 us
    pallas_call x1, Pallas kernels, per_device(): call(pack_own, (shape(PACKED, T), shape(COLS * BAND + COLS, T, dtype=jnp....  1.24 us
    pallas_call x1, Pallas kernels, per_device(): call(cross_first, (whole_f32, whole_f32), [VMEM] * 5, (VMEM, VMEM), [whol...  1 us
    pallas_call x1, Pallas kernels, per_device(): call(own_square, (shape(3 * SIDE, SIDE), whole_f32, shape(SIDE, SIDE), sh...  1 us
    pallas_call x1, Pallas kernels, per_device(): call(own_products, (shape(2, SIDE, SIDE, dtype=F32), whole_f32), [VMEM] *...  0.81 us
  transfers between devices with their start and end apart: 5, of which 1 were waited for; matrix products, arithmetic and copies ran while one was open for 0% of the time, Pallas kernels for 16%

profile of v4, /device:TPU:0, one launch (start us, length us, event | category | flops | bytes accessed | tf_op | source)
XLA Modules:
  0.0 30.2 jit_solution(4993039428726497066)
XLA Ops:
  0.0 0.0 copy-start
  0.0 1.2 %shard_map.37 = (bf16[1040,128]{1,0:T(8,128)(2,1)S(1)}, s32[40,128]{1,0:T(8,128)S(1)}) custom-call(bf16[4,9,128,128]{3,2,1,0:T(8,128)(2,1)} %density.3, s32[4,9]{1,0:T(4,128)} %pattern.1, s32[512]{0:T(512)} %orbitals.1), custom_call_target="tpu_custom_call" | custom-call | bytes 1048576 | tf_op jit(solution)/shard_map/pallas_call | solution.py:331
  1.3 1.7 %collective-permute-start.3 = (bf16[1040,128]{1,0:T(8,128)(2,1)S(1)}, bf16[1040,128]{1,0:T(8,128)(2,1)S(1)}, u32[]{:S(2)}, u32[]{:S(2)}) collective-permute-start(bf16[1040,128]{1,0:T(8,128)(2,1)S(1)} %get-tuple-element.19.packed_own), channel_id=1, source_target_pairs={{0,1},{1,0},{2,3},{3,2},{4,5},{5,4},{6,7},{7,6},{8,9},{9,8},{10,11... | collective-permute-start | bytes 798728 | tf_op jit(solution)/shard_map/ppermute | solution.py:326
  3.0 1.3 %collective-permute-start.4 = (bf16[1040,128]{1,0:T(8,128)(2,1)S(1)}, bf16[1040,128]{1,0:T(8,128)(2,1)S(1)}, u32[]{:S(2)}, u32[]{:S(2)}) collective-permute-start(bf16[1040,128]{1,0:T(8,128)(2,1)S(1)} %get-tuple-element.19.packed_own), channel_id=1, source_target_pairs={{1,2},{2,1},{3,4},{4,3},{5,6},{6,5},{7,8},{8,7},{9,10},{10,9},{11,... | collective-permute-start | bytes 798728 | tf_op jit(solution)/shard_map/ppermute | solution.py:326
  4.3 0.0 copy-done
  4.3 1.0 %shard_map.38 = (bf16[1536,512]{1,0:T(8,128)(2,1)S(1)}, f32[512,512]{1,0:T(8,128)S(1)}, bf16[512,512]{1,0:T(8,128)(2,1)S(1)}, bf16[1040,128]{1,0:T(8,128)(2,1)S(1)}, bf16[2080,128]{1,0:T(8,128)(2,1)S(1)}) custom-call(bf16[4,9,128,128]{3,2,1,0:T(8,128)(2,1)S(1)} %copy-done, s32[40,128]{1,0:T(8,128)S(1)} %get-tuple-element.18.counts, ...), custom_call_target="tpu_custom_call" | custom-call | flops 1073741824 | bytes 4194304 | tf_op jit(solution)/shard_map/pallas_call | solution.py:347
  5.3 3.6 %collective-permute-start = (bf16[1040,128]{1,0:T(8,128)(2,1)S(1)}, bf16[1040,128]{1,0:T(8,128)(2,1)S(1)}, u32[]{:S(2)}, u32[]{:S(2)}) collective-permute-start(bf16[1040,128]{1,0:T(8,128)(2,1)S(1)} %get-tuple-element.20), channel_id=1, source_target_pairs={{0,1},{1,0},{2,3},{3,2},{4,5},{5,4},{6,7},{7,6},{8,9},{9,8},{10,11... | collective-permute-start | bytes 798728 | tf_op jit(solution)/shard_map/ppermute | solution.py:326
  8.8 1.3 %collective-permute-start.1 = (bf16[1040,128]{1,0:T(8,128)(2,1)S(1)}, bf16[1040,128]{1,0:T(8,128)(2,1)S(1)}, u32[]{:S(2)}, u32[]{:S(2)}) collective-permute-start(bf16[1040,128]{1,0:T(8,128)(2,1)S(1)} %get-tuple-element.20), channel_id=1, source_target_pairs={{1,2},{2,1},{3,4},{4,3},{5,6},{6,5},{7,8},{8,7},{9,10},{10,9},{11,... | collective-permute-start | bytes 798728 | tf_op jit(solution)/shard_map/ppermute | solution.py:326
  10.1 9.7 %collective-permute-start.2 = (bf16[2080,128]{1,0:T(8,128)(2,1)S(1)}, bf16[2080,128]{1,0:T(8,128)(2,1)S(1)}, u32[]{:S(2)}, u32[]{:S(2)}) collective-permute-start(bf16[2080,128]{1,0:T(8,128)(2,1)S(1)} %get-tuple-element.21), channel_id=1, source_target_pairs={{0,127}} | collective-permute-start | bytes 1597448 | tf_op jit(solution)/shard_map/ppermute | solution.py:326
  19.9 0.8 %shard_map.39 = (f32[2,512,512]{2,1,0:T(8,128)S(1)}, f32[512,512]{1,0:T(8,128)S(1)}) custom-call(bf16[1536,512]{1,0:T(8,128)(2,1)S(1)} %get-tuple-element.22.wide, bf16[512,512]{1,0:T(8,128)(2,1)S(1)} %get-tuple-element.23.squared), custom_call_target="tpu_custom_call" | custom-call | flops 17179869184 | bytes 1048576 | tf_op jit(solution)/shard_map/pallas_call | solution.py:359
  20.7 0.0 collective-permute-done.3.packed
  20.7 1.0 %shard_map.40 = (f32[512,512]{1,0:T(8,128)S(1)}, f32[512,512]{1,0:T(8,128)S(1)}) custom-call(bf16[1040,128]{1,0:T(8,128)(2,1)S(1)} %collective-permute-done.3.packed, bf16[1536,512]{1,0:T(8,128)(2,1)S(1)} %get-tuple-element.22.wide, s32[40,128]{1,0:T(8,128)S(1)} %get-tuple-element.18.counts, f32[2,512,512]{2,1,0:T(8,128)S(1)} %get-tuple-element.24.local, ...), custom_call_target="tpu_custom_call" | custom-call | flops 17179869184 | bytes 1048576 | tf_op jit(solution)/shard_map/pallas_call | solution.py:368
  21.7 0.0 collective-permute-done.4.packed
  21.7 4.9 %collective-permute-done.2.to_last = bf16[2080,128]{1,0:T(8,128)(2,1)S(1)} collective-permute-done((bf16[2080,128]{1,0:T(8,128)(2,1)S(1)}, bf16[2080,128]{1,0:T(8,128)(2,1)S(1)}, u32[]{:S(2)}, u32[]{:S(2)}) %collective-permute-start.2) | collective-permute-done | bytes 532512 | tf_op jit(solution)/shard_map/ppermute | solution.py:326
  26.6 2.0 %shard_map.41 = (f32[512,512]{1,0:T(8,128)S(1)}, bf16[4,9,128,128]{3,2,1,0:T(8,128)(2,1)}) custom-call(bf16[1040,128]{1,0:T(8,128)(2,1)S(1)} %collective-permute-done.4.packed, bf16[2080,128]{1,0:T(8,128)(2,1)S(1)} %collective-permute-done.2.to_last, bf16[1536,512]{1,0:T(8,128)(2,1)S(1)} %get-tuple-element.22.wide, s32[40,128]{1,0:T(8,128)S(1)} %get-tuple-element.18.counts, ...), custom_call_target="tpu_custom_call" | custom-call | flops 1073741824 | bytes 2097152 | tf_op jit(solution)/shard_map/pallas_call | solution.py:377
  28.6 0.0 collective-permute-done.packed_first
  28.6 0.0 collective-permute-done.1.packed_second
  28.6 1.6 %shard_map.42 = bf16[4,9,128,128]{3,2,1,0:T(8,128)(2,1)} custom-call(bf16[1040,128]{1,0:T(8,128)(2,1)S(1)} %collective-permute-done.packed_first, bf16[1040,128]{1,0:T(8,128)(2,1)S(1)} %collective-permute-done.1.packed_second, bf16[2080,128]{1,0:T(8,128)(2,1)S(1)} %collective-permute-done.2.to_last, ...), custom_call_target="tpu_custom_call", output_to_operand_aliasing={{}: (7, {})} | custom-call | flops 268435456 | bytes 2097152 | tf_op jit(solution)/shard_map/pallas_call | solution.py:392
Async XLA Ops:
  0.0 4.3 %copy-start = (bf16[4,9,128,128]{3,2,1,0:T(8,128)(2,1)S(1)}, bf16[4,9,128,128]{3,2,1,0:T(8,128)(2,1)}, u32[]{:S(2)}) copy-start(bf16[4,9,128,128]{3,2,1,0:T(8,128)(2,1)} %density.3) | copy-start | bytes 3538948
  1.3 19.4 %collective-permute-start.3 = (bf16[1040,128]{1,0:T(8,128)(2,1)S(1)}, bf16[1040,128]{1,0:T(8,128)(2,1)S(1)}, u32[]{:S(2)}, u32[]{:S(2)}) collective-permute-start(bf16[1040,128]{1,0:T(8,128)(2,1)S(1)} %get-tuple-element.19.packed_own), channel_id=1, source_target_pairs={{0,1},{1,0},{2,3},{3,2},{4,5},{5,4},{6,7},{7,6},{8,9},{9,8},{10,11... | collective-permute-start | bytes 798728 | tf_op jit(solution)/shard_map/ppermute | solution.py:326
  3.0 18.7 %collective-permute-start.4 = (bf16[1040,128]{1,0:T(8,128)(2,1)S(1)}, bf16[1040,128]{1,0:T(8,128)(2,1)S(1)}, u32[]{:S(2)}, u32[]{:S(2)}) collective-permute-start(bf16[1040,128]{1,0:T(8,128)(2,1)S(1)} %get-tuple-element.19.packed_own), channel_id=1, source_target_pairs={{1,2},{2,1},{3,4},{4,3},{5,6},{6,5},{7,8},{8,7},{9,10},{10,9},{11,... | collective-permute-start | bytes 798728 | tf_op jit(solution)/shard_map/ppermute | solution.py:326
  5.3 23.3 %collective-permute-start = (bf16[1040,128]{1,0:T(8,128)(2,1)S(1)}, bf16[1040,128]{1,0:T(8,128)(2,1)S(1)}, u32[]{:S(2)}, u32[]{:S(2)}) collective-permute-start(bf16[1040,128]{1,0:T(8,128)(2,1)S(1)} %get-tuple-element.20), channel_id=1, source_target_pairs={{0,1},{1,0},{2,3},{3,2},{4,5},{5,4},{6,7},{7,6},{8,9},{9,8},{10,11... | collective-permute-start | bytes 798728 | tf_op jit(solution)/shard_map/ppermute | solution.py:326
  8.8 19.8 %collective-permute-start.1 = (bf16[1040,128]{1,0:T(8,128)(2,1)S(1)}, bf16[1040,128]{1,0:T(8,128)(2,1)S(1)}, u32[]{:S(2)}, u32[]{:S(2)}) collective-permute-start(bf16[1040,128]{1,0:T(8,128)(2,1)S(1)} %get-tuple-element.20), channel_id=1, source_target_pairs={{1,2},{2,1},{3,4},{4,3},{5,6},{6,5},{7,8},{8,7},{9,10},{10,9},{11,... | collective-permute-start | bytes 798728 | tf_op jit(solution)/shard_map/ppermute | solution.py:326
  10.1 16.5 %collective-permute-start.2 = (bf16[2080,128]{1,0:T(8,128)(2,1)S(1)}, bf16[2080,128]{1,0:T(8,128)(2,1)S(1)}, u32[]{:S(2)}, u32[]{:S(2)}) collective-permute-start(bf16[2080,128]{1,0:T(8,128)(2,1)S(1)} %get-tuple-element.21), channel_id=1, source_target_pairs={{0,127}} | collective-permute-start | bytes 1597448 | tf_op jit(solution)/shard_map/ppermute | solution.py:326

commit v5 on v4

v5 whole, which is shorter than its diff:
```python
import jax
import jax.numpy as jnp
from jax import lax
from jax.experimental import pallas as pl
from jax.experimental.pallas import tpu as pltpu
from jax.sharding import PartitionSpec as P

AXES = ("blk", "rep")
T = 128
COLS = 4
REACH = 4
BAND = 9
SIDE = COLS * T
BELOW = [(a, b) for b in range(COLS) for a in range(b + 1, COLS)]
PACKED = (len(BELOW) + COLS // 2) * T + 16
F32 = jnp.float32
BF16 = jnp.bfloat16
LIMIT = 40 * 1024 * 1024

VMEM = pl.BlockSpec(memory_space=pltpu.VMEM)
SMEM = pl.BlockSpec(memory_space=pltpu.SMEM)
ANY = pl.BlockSpec(memory_space=pl.ANY)


def rows_cols():
    return (
        lax.broadcasted_iota(jnp.int32, (T, T), 0),
        lax.broadcasted_iota(jnp.int32, (T, T), 1),
    )


def at(index):
    return slice(index * T, (index + 1) * T)


def dot(a, b):
    return lax.dot_general(a, b, (((1,), (0,)), ((), ())), preferred_element_type=F32)


def dot_tn(a, b):
    return lax.dot_general(a, b, (((0,), (0,)), ((), ())), preferred_element_type=F32)


def pack(out_ref, block):
    row, col = rows_cols()
    for index, (a, b) in enumerate(BELOW):
        out_ref[at(index), :] = block(a, b).astype(BF16)
    strip_row = lax.broadcasted_iota(jnp.int32, (16, T), 0)
    strip = jnp.zeros((16, T), F32)
    for pair in range(COLS // 2):
        first = block(2 * pair, 2 * pair).astype(F32)
        second = block(2 * pair + 1, 2 * pair + 1).astype(F32)
        out_ref[at(len(BELOW) + pair), :] = jnp.where(row >= col, first, second).astype(BF16)
        diagonal = jnp.sum(jnp.where(row == col, second, 0.0), axis=0, keepdims=True)
        strip = jnp.where(strip_row == pair, diagonal, strip)
    out_ref[PACKED - 16 : PACKED, :] = strip.astype(BF16)


def unpack(read, full_ref):
    row, col = rows_cols()
    for index, (a, b) in enumerate(BELOW):
        block = read(at(index))
        full_ref[at(a), at(b)] = block
        full_ref[at(b), at(a)] = block.T
    strip = read(slice(PACKED - 16, PACKED)).astype(F32)
    for pair in range(COLS // 2):
        both = read(at(len(BELOW) + pair)).astype(F32)
        turned = both.T
        first = jnp.where(row >= col, both, turned)
        second = jnp.where(row < col, both, turned)
        second = jnp.where(row == col, strip[pair : pair + 1, :], second)
        full_ref[at(2 * pair), at(2 * pair)] = first.astype(BF16)
        full_ref[at(2 * pair + 1), at(2 * pair + 1)] = second.astype(BF16)


def load(pairs, sems):
    copies = [pltpu.make_async_copy(source, target, sems.at[i]) for i, (source, target) in enumerate(pairs)]
    for copy in copies:
        copy.start()
    return copies


def count_row(c, slot):
    return slice(c * BAND + slot, c * BAND + slot + 1)


def span(first, last):
    return slice(2 * first * T, 2 * (last + 1) * T)


RANGE = ((span(0, 1), span(1, 1)), (span(0, 0), span(0, 1)))
HALVES = (span(0, 0), span(1, 1))


def side_blocks(side):
    place = 0
    for c in range(COLS):
        for a in range(c, COLS) if side == 0 else range(c + 1):
            yield a, c, a - c + 2 * REACH * side, place
            place += 1


def keep(counts, c, slot):
    return counts[count_row(c, slot), :] > 0


def side_of(wide, side):
    return wide.at[side * 2 * SIDE : (side * 2 + 1) * SIDE]


def side_by_own(side, thin, own, out):
    if side == 0:
        out[HALVES[0], HALVES[0]] = dot(thin[HALVES[0], HALVES[0]], own[HALVES[0], HALVES[0]])
        out[HALVES[1], :] = dot(thin[HALVES[1], :], own[...])
    else:
        out[HALVES[0], :] = dot(thin[HALVES[0], :], own[...])
        out[HALVES[1], HALVES[1]] = dot(thin[HALVES[1], HALVES[1]], own[HALVES[1], HALVES[1]])


def full_by_side(side, half_col, full, thin):
    rows = RANGE[side][half_col]
    return dot(full[rows, rows], thin[rows, HALVES[half_col]])


def add_turned(side, left, right, before, out, lower=False):
    low, high = HALVES
    if side == 0:
        out[low, low] = before[low, low] + dot_tn(left[:, low], right[:, low])
        if not lower:
            out[low, high] = before[low, high] + dot_tn(left[high, low], right[high, high])
        out[high, :] = before[high, :] + dot_tn(left[high, high], right[high, :])
    else:
        inner = low if lower else slice(0, SIDE)
        out[low, inner] = before[low, inner] + dot_tn(left[low, low], right[low, inner])
        out[high, low] = before[high, low] + dot_tn(left[low, high], right[low, low])
        out[high, high] = before[high, high] + dot_tn(left[:, high], right[:, high])


def own_square(
    density, pattern, orbitals, wide, counts, square, squared, both, held, pattern_now, orbitals_now, sems
):
    pairs = [(density.at[c], held.at[c]) for c in range(COLS)]
    copies = load([(orbitals, orbitals_now), (pattern, pattern_now)] + pairs, sems)
    row, col = rows_cols()
    zero = jnp.zeros((T, T), BF16)
    for c in range(COLS):
        for r in range(COLS + 2 * REACH):
            if not c <= r < c + BAND:
                wide[at(r), at(c)] = zero
    for copy in copies[:2]:
        copy.wait()
    first = lax.axis_index(AXES) * COLS
    total = orbitals.shape[0]
    used = [orbitals_now[lax.rem(first + r - REACH + total, total)] for r in range(COLS + 2 * REACH)]
    for c in range(COLS):
        seen = [used[c + slot] * pattern_now[c, slot] for slot in range(BAND)]
        copies[2 + c].wait()
        for slot in range(BAND):
            visible = (row < seen[slot]) & (col < used[c + REACH])
            wide[at(c + slot), at(c)] = jnp.where(visible, held[c, slot].astype(F32), 0.0).astype(BF16)
            counts[count_row(c, slot), :] = jnp.full((1, T), seen[slot], jnp.int32)
    own = wide.at[SIDE : 2 * SIDE]
    low, high = HALVES
    square[low, low] = dot(own[low, :], own[:, low])
    square[high, :] = dot(own[high, :], own[...])
    for side in range(2):
        add_turned(side, side_of(wide, side), side_of(wide, side), square, square, lower=True)
    pack(both.at[:PACKED], lambda a, b: own[at(a), at(b)])
    for b in range(COLS):
        for a in range(b, COLS):
            block = jnp.where(keep(counts, b, a - b + REACH), square[at(a), at(b)], 0.0).astype(BF16)
            squared[at(a), at(b)] = block
    pack(both.at[PACKED:], lambda a, b: squared[at(a), at(b)])


def own_products(wide, squared, local, cube, full):
    own = wide.at[SIDE : 2 * SIDE]
    full[...] = squared[...]
    for b in range(COLS):
        for a in range(b):
            full[at(a), at(b)] = squared[at(b), at(a)].T
    cube[...] = dot(full[...], own[...])
    for side in range(2):
        side_by_own(side, side_of(wide, side), own, local.at[side])


def by_side(turn, one):
    odd = lax.rem(lax.axis_index(AXES), 2)

    @pl.when(odd == turn)
    def _():
        one(1)

    @pl.when(odd != turn)
    def _():
        one(0)


def cross_step(side, full, wide, counts, local, crossed, acc, before, cube):
    thin = side_of(wide, side)
    for j in range(2):
        rows = RANGE[side][j]
        acc[rows, HALVES[j]] = local[side, rows, HALVES[j]] + full_by_side(side, j, full, thin)
    for a in range(COLS):
        for c in range(COLS):
            if (a >= c) if side == 0 else (a <= c):
                block = jnp.where(keep(counts, c, a - c + 2 * REACH * side), acc[at(a), at(c)], 0.0).astype(BF16)
            else:
                block = jnp.zeros((T, T), BF16)
            crossed[at(a), at(c)] = block
    add_turned(side, crossed, thin, before, cube)


def send_side(side, counts, held, out, sems, mixed):
    copies = []
    blocks = list(side_blocks(side))
    for c in range(COLS):
        here = [block for block in blocks if block[1] == c]
        for a, _, slot, place in here:
            held[place] = jnp.where(keep(counts, c, slot), mixed(a, c), 0.0).astype(BF16)
        copies.append(
            pltpu.make_async_copy(
                held.at[pl.ds(here[0][3], len(here))], out.at[c, pl.ds(here[0][2], len(here))], sems.at[c]
            )
        )
        copies[-1].start()
    return copies


def finish_side(turn, both, wide, counts, local, before, crossed, full, full_square, acc, cube, term, held, out, sems, copies_own):
    own = wide.at[SIDE : 2 * SIDE]
    unpack(lambda rows: both[rows, :], full)
    unpack(lambda rows: both[rows.start + PACKED : rows.stop + PACKED, :], full_square)

    def one(side):
        thin = side_of(wide, side)
        cross_step(side, full, wide, counts, local, crossed, acc, before, cube)
        copies = copies_own()
        side_by_own(side, crossed, own, term)
        for j in range(2):
            term[RANGE[side][j], HALVES[j]] += full_by_side(side, j, full_square, thin)
        copies += send_side(
            side, counts, held, out, sems, lambda a, c: 3.0 * acc[at(a), at(c)] - 2.0 * term[at(a), at(c)]
        )
        for copy in copies:
            copy.wait()

    by_side(turn, one)


def finish_first(both, wide, counts, local, before, out, cube, full, full_square, crossed, acc, term, held, sems):
    finish_side(0, both, wide, counts, local, before, crossed, full, full_square, acc, cube, term, held, out, sems, list)


def finish_second(
    both, wide, counts, local, before, square, begun, out, full, full_square, crossed, acc, term, held, sems, cube, held_own, sems_own
):
    del begun

    def copies_own():
        copies = []
        for c in range(COLS):
            for a in range(COLS):
                there = square[at(a), at(c)] if a // 2 >= c // 2 else square[at(c), at(a)].T
                mixed = 3.0 * there - 2.0 * cube[at(a), at(c)]
                held_own[c, a] = jnp.where(keep(counts, c, a - c + REACH), mixed, 0.0).astype(BF16)
            copies.append(pltpu.make_async_copy(held_own.at[c], out.at[c, pl.ds(REACH - c, COLS)], sems_own.at[c]))
            copies[-1].start()
        return copies

    finish_side(1, both, wide, counts, local, before, crossed, full, full_square, acc, cube, term, held, out, sems, copies_own)


def call(kernel, outs, ins, out_specs, scratch, flops, moved, **more):
    return pl.pallas_call(
        kernel,
        out_shape=outs,
        in_specs=ins,
        out_specs=out_specs,
        scratch_shapes=scratch,
        compiler_params=pltpu.CompilerParams(vmem_limit_bytes=LIMIT),
        cost_estimate=pl.CostEstimate(flops=flops, bytes_accessed=moved, transcendentals=0),
        **more,
    )


def shape(*dims, dtype=BF16):
    return jax.ShapeDtypeStruct(dims, dtype)


def per_device(density, pattern, orbitals):
    count = lax.axis_size(AXES)
    pairs = [(i, i ^ 1) for i in range(count)]
    others = [(i, (i + 1 if i % 2 else i - 1) % count) for i in range(count)]

    def send(array, to):
        return lax.ppermute(array, AXES, to)

    far = [pltpu.with_memory_space_constraint(array, pltpu.HBM) for array in (density, pattern, orbitals)]
    whole = pltpu.VMEM((SIDE, SIDE), BF16)
    whole_f32 = shape(SIDE, SIDE, dtype=F32)
    wide, counts, square, squared, both = call(
        own_square,
        (
            shape(3 * SIDE, SIDE),
            shape(COLS * BAND, T, dtype=jnp.int32),
            whole_f32,
            shape(SIDE, SIDE),
            shape(2 * PACKED, T),
        ),
        [ANY] * 3,
        (VMEM,) * 5,
        [
            pltpu.VMEM(density.shape, BF16),
            pltpu.SMEM(pattern.shape, jnp.int32),
            pltpu.SMEM(orbitals.shape, jnp.int32),
            pltpu.SemaphoreType.DMA((COLS + 2,)),
        ],
        2**30,
        2**22,
    )(*far)
    both_first = send(both, pairs)
    both_second = send(both, others)
    local, cube = call(
        own_products,
        (shape(2, SIDE, SIDE, dtype=F32), whole_f32),
        [VMEM] * 2,
        (VMEM,) * 2,
        [whole],
        2**29,
        2**20,
    )(wide, squared)
    total = pltpu.VMEM((SIDE, SIDE), F32)
    sems = pltpu.SemaphoreType.DMA((COLS,))
    room = [whole, whole, whole, total, total, pltpu.VMEM((10, T, T), BF16), sems]
    begun, cube = call(
        finish_first,
        (shape(*density.shape), whole_f32),
        [VMEM] * 5,
        (ANY, VMEM),
        room,
        2**31,
        2**21,
    )(both_first, wide, counts, local, cube)
    return call(
        finish_second,
        shape(*density.shape),
        [VMEM] * 6 + [ANY],
        ANY,
        [*room, total, pltpu.VMEM((COLS, COLS, T, T), BF16), sems],
        2**30,
        2**21,
        input_output_aliases={6: 0},
    )(both_second, wide, counts, local, cube, square, begun)


def solution(mesh):
    placed = (P(AXES, None, None, None), P(AXES, None), P())
    return jax.shard_map(
        per_device, mesh=mesh, in_specs=placed, out_specs=P(AXES, None, None, None), check_vma=False
    )
```

time: 30.4 us -> 22.5 us (0.74)
  the two profiles are of different devices: /device:TPU:0 before, /device:TPU:1 now
where the time goes in v5:
time: 22.5 us; the launch traced here: 22.4 us
  waiting for transfers between devices  10.1 us (45%)
  Pallas kernels  7.34 us (33%)
  starting transfers between devices  4.95 us (22%)
    ppermute x2, waiting for transfers between devices, send(): return lax.ppermute(array, AXES, to)  10.1 us
    ppermute x2, starting transfers between devices, send(): return lax.ppermute(array, AXES, to)  4.95 us
    pallas_call x1, Pallas kernels, per_device(): call(finish_second, shape(*density.shape), [VMEM] * 6 + [ANY], ANY, [*roo...  2.45 us
    pallas_call x1, Pallas kernels, per_device(): call(own_square, (shape(3 * SIDE, SIDE), shape(COLS * BAND, T, dtype=jnp....  2.11 us
    pallas_call x1, Pallas kernels, per_device(): call(finish_first, (shape(*density.shape), whole_f32), [VMEM] * 5, (ANY,...  1.96 us
    pallas_call x1, Pallas kernels, per_device(): call(own_products, (shape(2, SIDE, SIDE, dtype=F32), whole_f32), [VMEM] *...  0.83 us
  transfers between devices with their start and end apart: 2, of which 2 were waited for; matrix products, arithmetic and copies ran while one was open for 0% of the time, Pallas kernels for 12%

profile of v5, /device:TPU:1, one launch (start us, length us, event | category | flops | bytes accessed | tf_op | source)
XLA Modules:
  0.0 22.4 jit_solution(964190268151939619)
XLA Ops:
  0.0 2.1 %shard_map.37 = (bf16[1536,512]{1,0:T(8,128)(2,1)S(1)}, s32[36,128]{1,0:T(8,128)S(1)}, f32[512,512]{1,0:T(8,128)S(1)}, bf16[512,512]{1,0:T(8,128)(2,1)S(1)}, bf16[2080,128]{1,0:T(8,128)(2,1)S(1)}) custom-call(bf16[4,9,128,128]{3,2,1,0:T(8,128)(2,1)} %density.1, s32[4,9]{1,0:T(4,128)} %pattern.1, s32[512]{0:T(512)} %orbitals.1), custom_call_target="tpu_custom_call" | custom-call | flops 1073741824 | bytes 4194304 | tf_op jit(solution)/shard_map/pallas_call | solution.py:302
  2.1 2.2 %collective-permute-start.1 = (bf16[2080,128]{1,0:T(8,128)(2,1)S(1)}, bf16[2080,128]{1,0:T(8,128)(2,1)S(1)}, u32[]{:S(2)}, u32[]{:S(2)}) collective-permute-start(bf16[2080,128]{1,0:T(8,128)(2,1)S(1)} %get-tuple-element.14), channel_id=1, source_target_pairs={{0,1},{1,0},{2,3},{3,2},{4,5},{5,4},{6,7},{7,6},{8,9},{9,8},{10,11... | collective-permute-start | bytes 1597448 | tf_op jit(solution)/shard_map/ppermute | solution.py:297
  4.3 2.7 %collective-permute-start = (bf16[2080,128]{1,0:T(8,128)(2,1)S(1)}, bf16[2080,128]{1,0:T(8,128)(2,1)S(1)}, u32[]{:S(2)}, u32[]{:S(2)}) collective-permute-start(bf16[2080,128]{1,0:T(8,128)(2,1)S(1)} %get-tuple-element.14), channel_id=1, source_target_pairs={{0,127},{1,2},{2,1},{3,4},{4,3},{5,6},{6,5},{7,8},{8,7},{9,10},{10... | collective-permute-start | bytes 1597448 | tf_op jit(solution)/shard_map/ppermute | solution.py:297
  7.1 0.8 %shard_map.38 = (f32[2,512,512]{2,1,0:T(8,128)S(1)}, f32[512,512]{1,0:T(8,128)S(1)}) custom-call(bf16[1536,512]{1,0:T(8,128)(2,1)S(1)} %get-tuple-element.15.wide, bf16[512,512]{1,0:T(8,128)(2,1)S(1)} %get-tuple-element.17.squared), custom_call_target="tpu_custom_call" | custom-call | flops 536870912 | bytes 1048576 | tf_op jit(solution)/shard_map/pallas_call | solution.py:324
  7.9 7.8 %collective-permute-done.1.both = bf16[2080,128]{1,0:T(8,128)(2,1)S(1)} collective-permute-done((bf16[2080,128]{1,0:T(8,128)(2,1)S(1)}, bf16[2080,128]{1,0:T(8,128)(2,1)S(1)}, u32[]{:S(2)}, u32[]{:S(2)}) %collective-permute-start.1) | collective-permute-done | bytes 532512 | tf_op jit(solution)/shard_map/ppermute | solution.py:297
  15.7 2.0 %shard_map.39 = (bf16[4,9,128,128]{3,2,1,0:T(8,128)(2,1)}, f32[512,512]{1,0:T(8,128)S(1)}) custom-call(bf16[2080,128]{1,0:T(8,128)(2,1)S(1)} %collective-permute-done.1.both, bf16[1536,512]{1,0:T(8,128)(2,1)S(1)} %get-tuple-element.15.wide, s32[36,128]{1,0:T(8,128)S(1)} %get-tuple-element.16.counts, f32[2,512,512]{2,1,0:T(8,128)S(1)} %get-tuple-element.18.local, ...), custom_call_target="tpu_custom_call" | custom-call | flops 2147483648 | bytes 2097152 | tf_op jit(solution)/shard_map/pallas_call | solution.py:336
  17.7 2.2 %collective-permute-done.both = bf16[2080,128]{1,0:T(8,128)(2,1)S(1)} collective-permute-done((bf16[2080,128]{1,0:T(8,128)(2,1)S(1)}, bf16[2080,128]{1,0:T(8,128)(2,1)S(1)}, u32[]{:S(2)}, u32[]{:S(2)}) %collective-permute-start) | collective-permute-done | bytes 532512 | tf_op jit(solution)/shard_map/ppermute | solution.py:297
  19.9 2.4 %shard_map.40 = bf16[4,9,128,128]{3,2,1,0:T(8,128)(2,1)} custom-call(bf16[2080,128]{1,0:T(8,128)(2,1)S(1)} %collective-permute-done.both, bf16[1536,512]{1,0:T(8,128)(2,1)S(1)} %get-tuple-element.15.wide, s32[36,128]{1,0:T(8,128)S(1)} %get-tuple-element.16.counts, f32[2,512,512]{2,1,0:T(8,128)S(1)} %get-tuple-element.18.local, ...), custom_call_target="tpu_custom_call", output_to_operand_aliasing={{}: (6, {})} | custom-call | flops 1073741824 | bytes 2097152 | tf_op jit(solution)/shard_map/pallas_call | solution.py:345
Async XLA Ops:
  2.1 13.6 %collective-permute-start.1 = (bf16[2080,128]{1,0:T(8,128)(2,1)S(1)}, bf16[2080,128]{1,0:T(8,128)(2,1)S(1)}, u32[]{:S(2)}, u32[]{:S(2)}) collective-permute-start(bf16[2080,128]{1,0:T(8,128)(2,1)S(1)} %get-tuple-element.14), channel_id=1, source_target_pairs={{0,1},{1,0},{2,3},{3,2},{4,5},{5,4},{6,7},{7,6},{8,9},{9,8},{10,11... | collective-permute-start | bytes 1597448 | tf_op jit(solution)/shard_map/ppermute | solution.py:297
  4.3 15.6 %collective-permute-start = (bf16[2080,128]{1,0:T(8,128)(2,1)S(1)}, bf16[2080,128]{1,0:T(8,128)(2,1)S(1)}, u32[]{:S(2)}, u32[]{:S(2)}) collective-permute-start(bf16[2080,128]{1,0:T(8,128)(2,1)S(1)} %get-tuple-element.14), channel_id=1, source_target_pairs={{0,127},{1,2},{2,1},{3,4},{4,3},{5,6},{6,5},{7,8},{8,7},{9,10},{10... | collective-permute-start | bytes 1597448 | tf_op jit(solution)/shard_map/ppermute | solution.py:297

commit v6 on v5

--- a/solution.py
+++ b/solution.py
@@ -137,7 +137,7 @@
 
 
 def own_square(
-    density, pattern, orbitals, wide, counts, square, squared, both, held, pattern_now, orbitals_now, sems
+    density, pattern, orbitals, wide, counts, square, squared, both, longer, held, pattern_now, orbitals_now, sems
 ):
     pairs = [(density.at[c], held.at[c]) for c in range(COLS)]
     copies = load([(orbitals, orbitals_now), (pattern, pattern_now)] + pairs, sems)
@@ -171,6 +171,8 @@
             block = jnp.where(keep(counts, b, a - b + REACH), square[at(a), at(b)], 0.0).astype(BF16)
             squared[at(a), at(b)] = block
     pack(both.at[PACKED:], lambda a, b: squared[at(a), at(b)])
+    longer[: 2 * PACKED, :] = both[...]
+    longer[2 * PACKED :, :] = jnp.zeros((16, T), BF16)
 
 
 def own_products(wide, squared, local, cube, full):
@@ -185,15 +187,7 @@
 
 
 def by_side(turn, one):
-    odd = lax.rem(lax.axis_index(AXES), 2)
-
-    @pl.when(odd == turn)
-    def _():
-        one(1)
-
-    @pl.when(odd != turn)
-    def _():
-        one(0)
+    one(1 - turn)
 
 
 def cross_step(side, full, wide, counts, local, crossed, acc, before, cube):
@@ -211,51 +205,54 @@
     add_turned(side, crossed, thin, before, cube)
 
 
-def send_side(side, counts, held, out, sems, mixed):
+def write_side(side, held, out, sems, start=True, columns=range(COLS)):
     copies = []
     blocks = list(side_blocks(side))
-    for c in range(COLS):
+    for c in columns:
         here = [block for block in blocks if block[1] == c]
-        for a, _, slot, place in here:
-            held[place] = jnp.where(keep(counts, c, slot), mixed(a, c), 0.0).astype(BF16)
         copies.append(
             pltpu.make_async_copy(
                 held.at[pl.ds(here[0][3], len(here))], out.at[c, pl.ds(here[0][2], len(here))], sems.at[c]
             )
         )
-        copies[-1].start()
+        if start:
+            copies[-1].start()
     return copies
 
 
-def finish_side(turn, both, wide, counts, local, before, crossed, full, full_square, acc, cube, term, held, out, sems, copies_own):
-    own = wide.at[SIDE : 2 * SIDE]
+def finish_side(turn, both, wide, counts, local, before, full, terms, acc, cube, term, held, out, sems, copies_own, write):
     unpack(lambda rows: both[rows, :], full)
-    unpack(lambda rows: both[rows.start + PACKED : rows.stop + PACKED, :], full_square)
 
     def one(side):
-        thin = side_of(wide, side)
+        terms_square = terms.at[:, side * SIDE : (side + 1) * SIDE]
+        crossed = terms.at[:, (1 - side) * SIDE : (2 - side) * SIDE]
+        unpack(lambda rows: both[rows.start + PACKED : rows.stop + PACKED, :], terms_square)
         cross_step(side, full, wide, counts, local, crossed, acc, before, cube)
         copies = copies_own()
-        side_by_own(side, crossed, own, term)
         for j in range(2):
-            term[RANGE[side][j], HALVES[j]] += full_by_side(side, j, full_square, thin)
-        copies += send_side(
-            side, counts, held, out, sems, lambda a, c: 3.0 * acc[at(a), at(c)] - 2.0 * term[at(a), at(c)]
-        )
+            rows = RANGE[side][j]
+            inner = slice(rows.start, 2 * SIDE) if side == 0 else slice(0, SIDE + rows.stop)
+            below = slice(inner.start + side * SIDE, inner.stop + side * SIDE)
+            term[rows, HALVES[j]] = dot(terms[rows, inner], wide[below, HALVES[j]])
+            for a, c, slot, place in side_blocks(side):
+                if c // 2 == j:
+                    mixed = 3.0 * acc[at(a), at(c)] - 2.0 * term[at(a), at(c)]
+                    held[place] = jnp.where(keep(counts, c, slot), mixed, 0.0).astype(BF16)
+            copies += write_side(side, held, out, sems, columns=(2 * j, 2 * j + 1)) if write else []
         for copy in copies:
             copy.wait()
 
     by_side(turn, one)
 
 
-def finish_first(both, wide, counts, local, before, out, cube, full, full_square, crossed, acc, term, held, sems):
-    finish_side(0, both, wide, counts, local, before, crossed, full, full_square, acc, cube, term, held, out, sems, list)
+def finish_first(both, wide, counts, local, before, held, cube, full, terms, acc, term):
+    finish_side(0, both, wide, counts, local, before, full, terms, acc, cube, term, held, None, None, list, False)
 
 
 def finish_second(
-    both, wide, counts, local, before, square, begun, out, full, full_square, crossed, acc, term, held, sems, cube, held_own, sems_own
+    both, wide, counts, local, before, square, first, out, full, terms, acc, term, held, sems, cube, held_own, sems_own, sems_first
 ):
-    del begun
+    by_side(0, lambda side: write_side(side, first, out, sems_first) and None)
 
     def copies_own():
         copies = []
@@ -268,7 +265,13 @@
             copies[-1].start()
         return copies
 
-    finish_side(1, both, wide, counts, local, before, crossed, full, full_square, acc, cube, term, held, out, sems, copies_own)
+    finish_side(1, both, wide, counts, local, before, full, terms, acc, cube, term, held, out, sems, copies_own, True)
+
+    def first_done(side):
+        for copy in write_side(side, first, out, sems_first, start=False):
+            copy.wait()
+
+    by_side(0, first_done)
 
 
 def call(kernel, outs, ins, out_specs, scratch, flops, moved, **more):
@@ -290,8 +293,8 @@
 
 def per_device(density, pattern, orbitals):
     count = lax.axis_size(AXES)
-    pairs = [(i, i ^ 1) for i in range(count)]
-    others = [(i, (i + 1 if i % 2 else i - 1) % count) for i in range(count)]
+    rightward = [(i, (i + 1) % count) for i in range(count)]
+    leftward = [(i, (i - 1) % count) for i in range(count)]
 
     def send(array, to):
         return lax.ppermute(array, AXES, to)
@@ -299,7 +302,7 @@
     far = [pltpu.with_memory_space_constraint(array, pltpu.HBM) for array in (density, pattern, orbitals)]
     whole = pltpu.VMEM((SIDE, SIDE), BF16)
     whole_f32 = shape(SIDE, SIDE, dtype=F32)
-    wide, counts, square, squared, both = call(
+    wide, counts, square, squared, both, longer = call(
         own_square,
         (
             shape(3 * SIDE, SIDE),
@@ -307,9 +310,10 @@
             whole_f32,
             shape(SIDE, SIDE),
             shape(2 * PACKED, T),
+            shape(2 * PACKED + 16, T),
         ),
         [ANY] * 3,
-        (VMEM,) * 5,
+        (VMEM,) * 6,
         [
             pltpu.VMEM(density.shape, BF16),
             pltpu.SMEM(pattern.shape, jnp.int32),
@@ -319,8 +323,8 @@
         2**30,
         2**22,
     )(*far)
-    both_first = send(both, pairs)
-    both_second = send(both, others)
+    both_left = send(longer, rightward)
+    both_right = send(both, leftward)
     local, cube = call(
         own_products,
         (shape(2, SIDE, SIDE, dtype=F32), whole_f32),
@@ -332,26 +336,33 @@
     )(wide, squared)
     total = pltpu.VMEM((SIDE, SIDE), F32)
     sems = pltpu.SemaphoreType.DMA((COLS,))
-    room = [whole, whole, whole, total, total, pltpu.VMEM((10, T, T), BF16), sems]
-    begun, cube = call(
+    room = [whole, pltpu.VMEM((SIDE, 2 * SIDE), BF16), total, total]
+    first, cube = call(
         finish_first,
-        (shape(*density.shape), whole_f32),
+        (shape(10, T, T), whole_f32),
         [VMEM] * 5,
-        (ANY, VMEM),
+        (VMEM, VMEM),
         room,
-        2**31,
-        2**21,
-    )(both_first, wide, counts, local, cube)
+        33554432,
+        1024,
+    )(both_right, wide, counts, local, cube)
     return call(
         finish_second,
         shape(*density.shape),
-        [VMEM] * 6 + [ANY],
+        [VMEM] * 7,
         ANY,
-        [*room, total, pltpu.VMEM((COLS, COLS, T, T), BF16), sems],
+        [
+            *room,
+            pltpu.VMEM((10, T, T), BF16),
+            sems,
+            total,
+            pltpu.VMEM((COLS, COLS, T, T), BF16),
+            sems,
+            sems,
+        ],
         2**30,
         2**21,
-        input_output_aliases={6: 0},
-    )(both_second, wide, counts, local, cube, square, begun)
+    )(both_left, wide, counts, local, cube, square, first)
 
 
 def solution(mesh):

time: 22.5 us -> 21.9 us (0.973)
  waiting for transfers between devices: 10.1 us -> 11.1 us
  Pallas kernels: 7.34 us -> 6.36 us
  starting transfers between devices: 4.95 us -> 4.28 us
    ppermute x2, waiting for transfers between devices: 10.1 us -> 11.1 us  [send(): return lax.ppermute(array, AXES, to)]
    pallas_call x2, Pallas kernels: 4.4 us -> 3.41 us  [the longest x1 2.19 us: per_device(): call(finish_second, shape(*density.shape), [VMEM] * 7, ANY, [*room, pltpu...]
    ppermute x2, starting transfers between devices: 4.95 us -> 4.28 us  [send(): return lax.ppermute(array, AXES, to)]
  transfers between devices with their start and end apart: 2 -> 2, of which waited for: 2 -> 1; matrix products, arithmetic and copies ran while one was open for 0% -> 0% of each run, Pallas kernels for 12% -> 9%
where the time goes in v6:
time: 21.9 us; the launch traced here: 21.8 us
  waiting for transfers between devices  11.1 us (51%)
  Pallas kernels  6.36 us (29%)
  starting transfers between devices  4.28 us (20%)
    ppermute x2, waiting for transfers between devices, send(): return lax.ppermute(array, AXES, to)  11.1 us
    ppermute x2, starting transfers between devices, send(): return lax.ppermute(array, AXES, to)  4.28 us
    pallas_call x1, Pallas kernels, per_device(): call(finish_second, shape(*density.shape), [VMEM] * 7, ANY, [*room, pltpu...  2.19 us
    pallas_call x1, Pallas kernels, per_device(): call(own_square, (shape(3 * SIDE, SIDE), shape(COLS * BAND, T, dtype=jnp....  2.14 us
    pallas_call x1, Pallas kernels, per_device(): call(finish_first, (shape(10, T, T), whole_f32), [VMEM] * 5, (VMEM, VMEM)...  1.22 us
    pallas_call x1, Pallas kernels, per_device(): call(own_products, (shape(2, SIDE, SIDE, dtype=F32), whole_f32), [VMEM] *...  0.81 us
  transfers between devices with their start and end apart: 2, of which 1 were waited for; matrix products, arithmetic and copies ran while one was open for 0% of the time, Pallas kernels for 9%

profile of v6, /device:TPU:1, one launch (start us, length us, event | category | flops | bytes accessed | tf_op | source)
XLA Modules:
  0.0 21.8 jit_solution(5212718691100513540)
XLA Ops:
  0.0 2.1 %shard_map.37 = (bf16[1536,512]{1,0:T(8,128)(2,1)S(1)}, s32[36,128]{1,0:T(8,128)S(1)}, f32[512,512]{1,0:T(8,128)S(1)}, bf16[512,512]{1,0:T(8,128)(2,1)S(1)}, bf1...) custom-call(bf16[4,9,128,128]{3,2,1,0:T(8,128)(2,1)} %density.1, s32[4,9]{1,0:T(4,128)} %pattern.1, s32[512]{0:T(512)} %orbitals.1), custom_call_target="tpu_custom_call" | custom-call | flops 1073741824 | bytes 4194304 | tf_op jit(solution)/shard_map/pallas_call | solution.py:305
  2.1 2.2 %collective-permute-start = (bf16[2096,128]{1,0:T(8,128)(2,1)S(1)}, bf16[2096,128]{1,0:T(8,128)(2,1)S(1)}, u32[]{:S(2)}, u32[]{:S(2)}) collective-permute-start(bf16[2096,128]{1,0:T(8,128)(2,1)S(1)} %get-tuple-element.15), channel_id=1, source_target_pairs={{0,1},{1,2},{2,3},{3,4},{4,5},{5,6},{6,7},{7,8},{8,9},{9,10},{10,1... | collective-permute-start | bytes 1609736 | tf_op jit(solution)/shard_map/ppermute | solution.py:300
  4.3 2.1 %collective-permute-start.1 = (bf16[2080,128]{1,0:T(8,128)(2,1)S(1)}, bf16[2080,128]{1,0:T(8,128)(2,1)S(1)}, u32[]{:S(2)}, u32[]{:S(2)}) collective-permute-start(bf16[2080,128]{1,0:T(8,128)(2,1)S(1)} %get-tuple-element.20), channel_id=1, source_target_pairs={{0,127},{1,0},{2,1},{3,2},{4,3},{5,4},{6,5},{7,6},{8,7},{9,8},{10,... | collective-permute-start | bytes 1597448 | tf_op jit(solution)/shard_map/ppermute | solution.py:300
  6.4 0.8 %shard_map.38 = (f32[2,512,512]{2,1,0:T(8,128)S(1)}, f32[512,512]{1,0:T(8,128)S(1)}) custom-call(bf16[1536,512]{1,0:T(8,128)(2,1)S(1)} %get-tuple-element.16.wide, bf16[512,512]{1,0:T(8,128)(2,1)S(1)} %get-tuple-element.18.squared), custom_call_target="tpu_custom_call" | custom-call | flops 536870912 | bytes 1048576 | tf_op jit(solution)/shard_map/pallas_call | solution.py:328
  7.2 11.1 %collective-permute-done.1.both = bf16[2080,128]{1,0:T(8,128)(2,1)S(1)} collective-permute-done((bf16[2080,128]{1,0:T(8,128)(2,1)S(1)}, bf16[2080,128]{1,0:T(8,128)(2,1)S(1)}, u32[]{:S(2)}, u32[]{:S(2)}) %collective-permute-start.1) | collective-permute-done | bytes 532512 | tf_op jit(solution)/shard_map/ppermute | solution.py:300
  18.4 1.2 %shard_map.39 = (bf16[10,128,128]{2,1,0:T(8,128)(2,1)S(1)}, f32[512,512]{1,0:T(8,128)S(1)}) custom-call(bf16[2080,128]{1,0:T(8,128)(2,1)S(1)} %collective-permute-done.1.both, bf16[1536,512]{1,0:T(8,128)(2,1)S(1)} %get-tuple-element.16.wide, s32[36,128]{1,0:T(8,128)S(1)} %get-tuple-element.17.counts, f32[2,512,512]{2,1,0:T(8,128)S(1)} %get-tuple-element.19.local, ...), custom_call_target="tpu_custom_call" | custom-call | flops 33554432 | bytes 1024 | tf_op jit(solution)/shard_map/pallas_call | solution.py:340
  19.6 0.0 collective-permute-done.both
  19.6 2.2 %shard_map.40 = bf16[4,9,128,128]{3,2,1,0:T(8,128)(2,1)} custom-call(bf16[2096,128]{1,0:T(8,128)(2,1)S(1)} %collective-permute-done.both, bf16[1536,512]{1,0:T(8,128)(2,1)S(1)} %get-tuple-element.16.wide, s32[36,128]{1,0:T(8,128)S(1)} %get-tuple-element.17.counts, f32[2,512,512]{2,1,0:T(8,128)S(1)} %get-tuple-element.19.local, ...), custom_call_target="tpu_custom_call" | custom-call | flops 1073741824 | bytes 2097152 | tf_op jit(solution)/shard_map/pallas_call | solution.py:349
Async XLA Ops:
  2.1 17.4 %collective-permute-start = (bf16[2096,128]{1,0:T(8,128)(2,1)S(1)}, bf16[2096,128]{1,0:T(8,128)(2,1)S(1)}, u32[]{:S(2)}, u32[]{:S(2)}) collective-permute-start(bf16[2096,128]{1,0:T(8,128)(2,1)S(1)} %get-tuple-element.15), channel_id=1, source_target_pairs={{0,1},{1,2},{2,3},{3,4},{4,5},{5,6},{6,7},{7,8},{8,9},{9,10},{10,1... | collective-permute-start | bytes 1609736 | tf_op jit(solution)/shard_map/ppermute | solution.py:300
  4.3 14.0 %collective-permute-start.1 = (bf16[2080,128]{1,0:T(8,128)(2,1)S(1)}, bf16[2080,128]{1,0:T(8,128)(2,1)S(1)}, u32[]{:S(2)}, u32[]{:S(2)}) collective-permute-start(bf16[2080,128]{1,0:T(8,128)(2,1)S(1)} %get-tuple-element.20), channel_id=1, source_target_pairs={{0,127},{1,0},{2,1},{3,2},{4,3},{5,4},{6,5},{7,6},{8,7},{9,8},{10,... | collective-permute-start | bytes 1597448 | tf_op jit(solution)/shard_map/ppermute | solution.py:300

commit v7 on v6

--- a/solution.py
+++ b/solution.py
@@ -152,6 +152,8 @@
     first = lax.axis_index(AXES) * COLS
     total = orbitals.shape[0]
     used = [orbitals_now[lax.rem(first + r - REACH + total, total)] for r in range(COLS + 2 * REACH)]
+    left, own, right = (wide.at[k * SIDE : (k + 1) * SIDE] for k in range(3))
+    low, high = HALVES
     for c in range(COLS):
         seen = [used[c + slot] * pattern_now[c, slot] for slot in range(BAND)]
         copies[2 + c].wait()
@@ -159,12 +161,21 @@
             visible = (row < seen[slot]) & (col < used[c + REACH])
             wide[at(c + slot), at(c)] = jnp.where(visible, held[c, slot].astype(F32), 0.0).astype(BF16)
             counts[count_row(c, slot), :] = jnp.full((1, T), seen[slot], jnp.int32)
-    own = wide.at[SIDE : 2 * SIDE]
-    low, high = HALVES
-    square[low, low] = dot(own[low, :], own[:, low])
-    square[high, :] = dot(own[high, :], own[...])
-    for side in range(2):
-        add_turned(side, side_of(wide, side), side_of(wide, side), square, square, lower=True)
+    square[low, low] = (
+        dot(own[low, :], own[:, low])
+        + dot_tn(left[:, low], left[:, low])
+        + dot_tn(right[low, low], right[low, low])
+    )
+    square[high, low] = (
+        dot(own[high, :], own[:, low])
+        + dot_tn(left[high, high], left[high, low])
+        + dot_tn(right[low, high], right[low, low])
+    )
+    square[high, high] = (
+        dot(own[high, :], own[:, high])
+        + dot_tn(left[high, high], left[high, high])
+        + dot_tn(right[:, high], right[:, high])
+    )
     pack(both.at[:PACKED], lambda a, b: own[at(a), at(b)])
     for b in range(COLS):
         for a in range(b, COLS):
@@ -175,26 +186,56 @@
     longer[2 * PACKED :, :] = jnp.zeros((16, T), BF16)
 
 
-def own_products(wide, squared, local, cube, full):
+def own_products(wide, square, squared, local, base, full):
     own = wide.at[SIDE : 2 * SIDE]
     full[...] = squared[...]
     for b in range(COLS):
         for a in range(b):
             full[at(a), at(b)] = squared[at(b), at(a)].T
-    cube[...] = dot(full[...], own[...])
+    base[...] = -2.0 * dot(full[...], own[...])
+    for b in range(COLS):
+        for a in range(COLS):
+            there = square[at(a), at(b)] if a >= b else square[at(b), at(a)].T
+            base[at(a), at(b)] += 3.0 * there
     for side in range(2):
         side_by_own(side, side_of(wide, side), own, local.at[side])
 
 
-def by_side(turn, one):
-    one(1 - turn)
-
-
-def cross_step(side, full, wide, counts, local, crossed, acc, before, cube):
-    thin = side_of(wide, side)
+def turned_terms(side, left, right):
+    low, high = HALVES
+    if side == 0:
+        yield 0, 0, dot_tn(left[:, low], right[:, low])
+        yield 0, 2, dot_tn(left[high, low], right[high, high])
+        yield 2, 0, dot_tn(left[high, high], right[high, :])
+    else:
+        yield 0, 0, dot_tn(left[low, low], right[low, :])
+        yield 2, 0, dot_tn(left[low, high], right[low, low])
+        yield 2, 2, dot_tn(left[:, high], right[:, high])
+
+
+def write_side(side, held, out, sems):
+    copies = []
+    blocks = list(side_blocks(side))
+    for c in range(COLS):
+        here = [block for block in blocks if block[1] == c]
+        copies.append(
+            pltpu.make_async_copy(
+                held.at[pl.ds(here[0][3], len(here))], out.at[c, pl.ds(here[0][2], len(here))], sems.at[c]
+            )
+        )
+        copies[-1].start()
+    return copies
+
+
+def side_terms(side, both, wide, counts, local, full, square, crossed, acc, term, held):
+    thin, own = side_of(wide, side), wide.at[SIDE : 2 * SIDE]
+    unpack(lambda rows: both[rows, :], full)
     for j in range(2):
         rows = RANGE[side][j]
         acc[rows, HALVES[j]] = local[side, rows, HALVES[j]] + full_by_side(side, j, full, thin)
+    unpack(lambda rows: both[rows.start + PACKED : rows.stop + PACKED, :], square)
+    for j in range(2):
+        term[RANGE[side][j], HALVES[j]] = full_by_side(side, j, square, thin)
     for a in range(COLS):
         for c in range(COLS):
             if (a >= c) if side == 0 else (a <= c):
@@ -202,76 +243,42 @@
             else:
                 block = jnp.zeros((T, T), BF16)
             crossed[at(a), at(c)] = block
-    add_turned(side, crossed, thin, before, cube)
-
-
-def write_side(side, held, out, sems, start=True, columns=range(COLS)):
-    copies = []
-    blocks = list(side_blocks(side))
-    for c in columns:
-        here = [block for block in blocks if block[1] == c]
-        copies.append(
-            pltpu.make_async_copy(
-                held.at[pl.ds(here[0][3], len(here))], out.at[c, pl.ds(here[0][2], len(here))], sems.at[c]
-            )
-        )
-        if start:
-            copies[-1].start()
-    return copies
-
-
-def finish_side(turn, both, wide, counts, local, before, full, terms, acc, cube, term, held, out, sems, copies_own, write):
-    unpack(lambda rows: both[rows, :], full)
-
-    def one(side):
-        terms_square = terms.at[:, side * SIDE : (side + 1) * SIDE]
-        crossed = terms.at[:, (1 - side) * SIDE : (2 - side) * SIDE]
-        unpack(lambda rows: both[rows.start + PACKED : rows.stop + PACKED, :], terms_square)
-        cross_step(side, full, wide, counts, local, crossed, acc, before, cube)
-        copies = copies_own()
-        for j in range(2):
-            rows = RANGE[side][j]
-            inner = slice(rows.start, 2 * SIDE) if side == 0 else slice(0, SIDE + rows.stop)
-            below = slice(inner.start + side * SIDE, inner.stop + side * SIDE)
-            term[rows, HALVES[j]] = dot(terms[rows, inner], wide[below, HALVES[j]])
-            for a, c, slot, place in side_blocks(side):
-                if c // 2 == j:
-                    mixed = 3.0 * acc[at(a), at(c)] - 2.0 * term[at(a), at(c)]
-                    held[place] = jnp.where(keep(counts, c, slot), mixed, 0.0).astype(BF16)
-            copies += write_side(side, held, out, sems, columns=(2 * j, 2 * j + 1)) if write else []
-        for copy in copies:
-            copy.wait()
-
-    by_side(turn, one)
-
-
-def finish_first(both, wide, counts, local, before, held, cube, full, terms, acc, term):
-    finish_side(0, both, wide, counts, local, before, full, terms, acc, cube, term, held, None, None, list, False)
-
-
-def finish_second(
-    both, wide, counts, local, before, square, first, out, full, terms, acc, term, held, sems, cube, held_own, sems_own, sems_first
-):
-    by_side(0, lambda side: write_side(side, first, out, sems_first) and None)
-
-    def copies_own():
-        copies = []
-        for c in range(COLS):
-            for a in range(COLS):
-                there = square[at(a), at(c)] if a // 2 >= c // 2 else square[at(c), at(a)].T
-                mixed = 3.0 * there - 2.0 * cube[at(a), at(c)]
+    low, high = HALVES
+    every = slice(0, SIDE)
+    for rows, inner, cols in (
+        ((low, low, low), (high, every, every)) if side == 0 else ((low, every, every), (high, high, high))
+    ):
+        piece = dot(crossed[rows, inner], own[inner, cols])
+        for a, c, slot, place in side_blocks(side):
+            if rows.start <= a * T < rows.stop:
+                here = piece[a * T - rows.start : (a + 1) * T - rows.start, c * T - cols.start : (c + 1) * T - cols.start]
+                mixed = 3.0 * acc[at(a), at(c)] - 2.0 * (term[at(a), at(c)] + here)
+                held[place] = jnp.where(keep(counts, c, slot), mixed, 0.0).astype(BF16)
+
+
+def finish_first(both, wide, counts, local, before, held, base, full, square, crossed, acc, term):
+    side_terms(1, both, wide, counts, local, full, square, crossed, acc, term, held)
+    for first_row, first_col, piece in turned_terms(1, crossed, side_of(wide, 1)):
+        rows = slice(first_row * T, first_row * T + piece.shape[0])
+        cols = slice(first_col * T, first_col * T + piece.shape[1])
+        base[rows, cols] = before[rows, cols] - 2.0 * piece
+
+
+def finish_second(both, wide, counts, local, base, first, out, full, square, crossed, acc, term, held, sems, held_own, sems_own, sems_first):
+    copies = write_side(1, first, out, sems_first)
+    side_terms(0, both, wide, counts, local, full, square, crossed, acc, term, held)
+    copies += write_side(0, held, out, sems)
+    for first_row, first_col, piece in turned_terms(0, crossed, side_of(wide, 0)):
+        for i in range(piece.shape[0] // T):
+            for j in range(piece.shape[1] // T):
+                a, c = first_row + i, first_col + j
+                mixed = base[at(a), at(c)] - 2.0 * piece[at(i), at(j)]
                 held_own[c, a] = jnp.where(keep(counts, c, a - c + REACH), mixed, 0.0).astype(BF16)
-            copies.append(pltpu.make_async_copy(held_own.at[c], out.at[c, pl.ds(REACH - c, COLS)], sems_own.at[c]))
-            copies[-1].start()
-        return copies
-
-    finish_side(1, both, wide, counts, local, before, full, terms, acc, cube, term, held, out, sems, copies_own, True)
-
-    def first_done(side):
-        for copy in write_side(side, first, out, sems_first, start=False):
-            copy.wait()
-
-    by_side(0, first_done)
+    for c in range(COLS):
+        copies.append(pltpu.make_async_copy(held_own.at[c], out.at[c, pl.ds(REACH - c, COLS)], sems_own.at[c]))
+        copies[-1].start()
+    for copy in copies:
+        copy.wait()
 
 
 def call(kernel, outs, ins, out_specs, scratch, flops, moved, **more):
@@ -325,44 +332,37 @@
     )(*far)
     both_left = send(longer, rightward)
     both_right = send(both, leftward)
-    local, cube = call(
+    local, base = call(
         own_products,
         (shape(2, SIDE, SIDE, dtype=F32), whole_f32),
-        [VMEM] * 2,
+        [VMEM] * 3,
         (VMEM,) * 2,
         [whole],
         2**29,
         2**20,
-    )(wide, squared)
+    )(wide, square, squared)
+    sems = pltpu.SemaphoreType.DMA((COLS,))
     total = pltpu.VMEM((SIDE, SIDE), F32)
-    sems = pltpu.SemaphoreType.DMA((COLS,))
-    room = [whole, pltpu.VMEM((SIDE, 2 * SIDE), BF16), total, total]
-    first, cube = call(
+    room = [whole, whole, whole, total, total]
+    ten = pltpu.VMEM((10, T, T), BF16)
+    first, base = call(
         finish_first,
         (shape(10, T, T), whole_f32),
         [VMEM] * 5,
         (VMEM, VMEM),
         room,
-        33554432,
-        1024,
-    )(both_right, wide, counts, local, cube)
+        2**25,
+        2**10,
+    )(both_right, wide, counts, local, base)
     return call(
         finish_second,
         shape(*density.shape),
-        [VMEM] * 7,
+        [VMEM] * 6,
         ANY,
-        [
-            *room,
-            pltpu.VMEM((10, T, T), BF16),
-            sems,
-            total,
-            pltpu.VMEM((COLS, COLS, T, T), BF16),
-            sems,
-            sems,
-        ],
+        [*room, ten, sems, pltpu.VMEM((COLS, COLS, T, T), BF16), sems, sems],
         2**30,
         2**21,
-    )(both_left, wide, counts, local, cube, square, first)
+    )(both_left, wide, counts, local, base, first)
 
 
 def solution(mesh):

time: 21.9 us -> 21.4 us (0.977)
  Pallas kernels: 6.36 us -> 5.89 us
    pallas_call x1, Pallas kernels: 2.19 us -> 1.9 us  [per_device(): call(finish_second, shape(*density.shape), [VMEM] * 6, ANY, [*room, ten,...]
where the time goes in v7:
time: 21.4 us; the launch traced here: 21.3 us
  waiting for transfers between devices  11.1 us (52%)
  Pallas kernels  5.89 us (28%)
  starting transfers between devices  4.28 us (20%)
    ppermute x2, waiting for transfers between devices, send(): return lax.ppermute(array, AXES, to)  11.1 us
    ppermute x2, starting transfers between devices, send(): return lax.ppermute(array, AXES, to)  4.28 us
    pallas_call x1, Pallas kernels, per_device(): call(own_square, (shape(3 * SIDE, SIDE), shape(COLS * BAND, T, dtype=jnp....  2.13 us
    pallas_call x1, Pallas kernels, per_device(): call(finish_second, shape(*density.shape), [VMEM] * 6, ANY, [*room, ten,...  1.9 us
    pallas_call x1, Pallas kernels, per_device(): call(finish_first, (shape(10, T, T), whole_f32), [VMEM] * 5, (VMEM, VMEM)...  1 us
    pallas_call x1, Pallas kernels, per_device(): call(own_products, (shape(2, SIDE, SIDE, dtype=F32), whole_f32), [VMEM] *...  0.86 us
  transfers between devices with their start and end apart: 2, of which 1 were waited for; matrix products, arithmetic and copies ran while one was open for 0% of the time, Pallas kernels for 9%

profile of v7, /device:TPU:1, one launch (start us, length us, event | category | flops | bytes accessed | tf_op | source)
XLA Modules:
  0.0 21.3 jit_solution(7382374570146625979)
XLA Ops:
  0.0 2.1 %shard_map.37 = (bf16[1536,512]{1,0:T(8,128)(2,1)S(1)}, s32[36,128]{1,0:T(8,128)S(1)}, f32[512,512]{1,0:T(8,128)S(1)}, bf16[512,512]{1,0:T(8,128)(2,1)S(1)}, bf1...) custom-call(bf16[4,9,128,128]{3,2,1,0:T(8,128)(2,1)} %density.1, s32[4,9]{1,0:T(4,128)} %pattern.1, s32[512]{0:T(512)} %orbitals.1), custom_call_target="tpu_custom_call" | custom-call | flops 1073741824 | bytes 4194304 | tf_op jit(solution)/shard_map/pallas_call | solution.py:312
  2.1 2.2 %collective-permute-start = (bf16[2096,128]{1,0:T(8,128)(2,1)S(1)}, bf16[2096,128]{1,0:T(8,128)(2,1)S(1)}, u32[]{:S(2)}, u32[]{:S(2)}) collective-permute-start(bf16[2096,128]{1,0:T(8,128)(2,1)S(1)} %get-tuple-element.15), channel_id=1, source_target_pairs={{0,1},{1,2},{2,3},{3,4},{4,5},{5,6},{6,7},{7,8},{8,9},{9,10},{10,1... | collective-permute-start | bytes 1609736 | tf_op jit(solution)/shard_map/ppermute | solution.py:307
  4.3 2.1 %collective-permute-start.1 = (bf16[2080,128]{1,0:T(8,128)(2,1)S(1)}, bf16[2080,128]{1,0:T(8,128)(2,1)S(1)}, u32[]{:S(2)}, u32[]{:S(2)}) collective-permute-start(bf16[2080,128]{1,0:T(8,128)(2,1)S(1)} %get-tuple-element.21), channel_id=1, source_target_pairs={{0,127},{1,0},{2,1},{3,2},{4,3},{5,4},{6,5},{7,6},{8,7},{9,8},{10,... | collective-permute-start | bytes 1597448 | tf_op jit(solution)/shard_map/ppermute | solution.py:307
  6.4 0.9 %shard_map.38 = (f32[2,512,512]{2,1,0:T(8,128)S(1)}, f32[512,512]{1,0:T(8,128)S(1)}) custom-call(bf16[1536,512]{1,0:T(8,128)(2,1)S(1)} %get-tuple-element.16.wide, f32[512,512]{1,0:T(8,128)S(1)} %get-tuple-element.18.square, bf16[512,512]{1,0:T(8,128)(2,1)S(1)} %get-tuple-element.19.squared), custom_call_target="tpu_custom_call" | custom-call | flops 536870912 | bytes 1048576 | tf_op jit(solution)/shard_map/pallas_call | solution.py:335
  7.3 11.0 %collective-permute-done.1.both = bf16[2080,128]{1,0:T(8,128)(2,1)S(1)} collective-permute-done((bf16[2080,128]{1,0:T(8,128)(2,1)S(1)}, bf16[2080,128]{1,0:T(8,128)(2,1)S(1)}, u32[]{:S(2)}, u32[]{:S(2)}) %collective-permute-start.1) | collective-permute-done | bytes 532512 | tf_op jit(solution)/shard_map/ppermute | solution.py:307
  18.3 1.0 %shard_map.39 = (bf16[10,128,128]{2,1,0:T(8,128)(2,1)S(1)}, f32[512,512]{1,0:T(8,128)S(1)}) custom-call(bf16[2080,128]{1,0:T(8,128)(2,1)S(1)} %collective-permute-done.1.both, bf16[1536,512]{1,0:T(8,128)(2,1)S(1)} %get-tuple-element.16.wide, s32[36,128]{1,0:T(8,128)S(1)} %get-tuple-element.17.counts, f32[2,512,512]{2,1,0:T(8,128)S(1)} %get-tuple-element.20.local, ...), custom_call_target="tpu_custom_call" | custom-call | flops 33554432 | bytes 1024 | tf_op jit(solution)/shard_map/pallas_call | solution.py:348
  19.3 0.0 collective-permute-done.both
  19.4 1.9 %shard_map.40 = bf16[4,9,128,128]{3,2,1,0:T(8,128)(2,1)} custom-call(bf16[2096,128]{1,0:T(8,128)(2,1)S(1)} %collective-permute-done.both, bf16[1536,512]{1,0:T(8,128)(2,1)S(1)} %get-tuple-element.16.wide, s32[36,128]{1,0:T(8,128)S(1)} %get-tuple-element.17.counts, f32[2,512,512]{2,1,0:T(8,128)S(1)} %get-tuple-element.20.local, ...), custom_call_target="tpu_custom_call" | custom-call | flops 1073741824 | bytes 2097152 | tf_op jit(solution)/shard_map/pallas_call | solution.py:357
Async XLA Ops:
  2.1 17.2 %collective-permute-start = (bf16[2096,128]{1,0:T(8,128)(2,1)S(1)}, bf16[2096,128]{1,0:T(8,128)(2,1)S(1)}, u32[]{:S(2)}, u32[]{:S(2)}) collective-permute-start(bf16[2096,128]{1,0:T(8,128)(2,1)S(1)} %get-tuple-element.15), channel_id=1, source_target_pairs={{0,1},{1,2},{2,3},{3,4},{4,5},{5,6},{6,7},{7,8},{8,9},{9,10},{10,1... | collective-permute-start | bytes 1609736 | tf_op jit(solution)/shard_map/ppermute | solution.py:307
  4.3 14.0 %collective-permute-start.1 = (bf16[2080,128]{1,0:T(8,128)(2,1)S(1)}, bf16[2080,128]{1,0:T(8,128)(2,1)S(1)}, u32[]{:S(2)}, u32[]{:S(2)}) collective-permute-start(bf16[2080,128]{1,0:T(8,128)(2,1)S(1)} %get-tuple-element.21), channel_id=1, source_target_pairs={{0,127},{1,0},{2,1},{3,2},{4,3},{5,4},{6,5},{7,6},{8,7},{9,8},{10,... | collective-permute-start | bytes 1597448 | tf_op jit(solution)/shard_map/ppermute | solution.py:307

commit v8 on v7

--- a/solution.py
+++ b/solution.py
@@ -12,7 +12,8 @@
 BAND = 9
 SIDE = COLS * T
 BELOW = [(a, b) for b in range(COLS) for a in range(b + 1, COLS)]
-PACKED = (len(BELOW) + COLS // 2) * T + 16
+PACKED = (len(BELOW) + COLS // 2) * T
+SENT = 2 * PACKED + 16
 F32 = jnp.float32
 BF16 = jnp.bfloat16
 LIMIT = 40 * 1024 * 1024
@@ -41,34 +42,40 @@
     return lax.dot_general(a, b, (((0,), (0,)), ((), ())), preferred_element_type=F32)
 
 
-def pack(out_ref, block):
+def pack(outs, offset, block):
     row, col = rows_cols()
+
+    def put(first_row, value):
+        for out in outs:
+            out[offset + first_row : offset + first_row + value.shape[0], :] = value.astype(BF16)
+
     for index, (a, b) in enumerate(BELOW):
-        out_ref[at(index), :] = block(a, b).astype(BF16)
-    strip_row = lax.broadcasted_iota(jnp.int32, (16, T), 0)
-    strip = jnp.zeros((16, T), F32)
+        put(index * T, block(a, b))
+    diagonals = []
     for pair in range(COLS // 2):
         first = block(2 * pair, 2 * pair).astype(F32)
         second = block(2 * pair + 1, 2 * pair + 1).astype(F32)
-        out_ref[at(len(BELOW) + pair), :] = jnp.where(row >= col, first, second).astype(BF16)
-        diagonal = jnp.sum(jnp.where(row == col, second, 0.0), axis=0, keepdims=True)
-        strip = jnp.where(strip_row == pair, diagonal, strip)
-    out_ref[PACKED - 16 : PACKED, :] = strip.astype(BF16)
-
-
-def unpack(read, full_ref):
+        put((len(BELOW) + pair) * T, jnp.where(row >= col, first, second))
+        diagonals.append(jnp.sum(jnp.where(row == col, second, 0.0), axis=0, keepdims=True))
+    return diagonals
+
+
+def unpack(both, which, full_ref):
+    def read(rows):
+        return both[rows.start + which * PACKED : rows.stop + which * PACKED, :]
+
     row, col = rows_cols()
     for index, (a, b) in enumerate(BELOW):
         block = read(at(index))
         full_ref[at(a), at(b)] = block
         full_ref[at(b), at(a)] = block.T
-    strip = read(slice(PACKED - 16, PACKED)).astype(F32)
+    strip = both[2 * PACKED : SENT, :].astype(F32)
     for pair in range(COLS // 2):
-        both = read(at(len(BELOW) + pair)).astype(F32)
-        turned = both.T
-        first = jnp.where(row >= col, both, turned)
-        second = jnp.where(row < col, both, turned)
-        second = jnp.where(row == col, strip[pair : pair + 1, :], second)
+        two = read(at(len(BELOW) + pair)).astype(F32)
+        turned = two.T
+        first = jnp.where(row >= col, two, turned)
+        second = jnp.where(row < col, two, turned)
+        second = jnp.where(row == col, strip[2 * which + pair : 2 * which + pair + 1, :], second)
         full_ref[at(2 * pair), at(2 * pair)] = first.astype(BF16)
         full_ref[at(2 * pair + 1), at(2 * pair + 1)] = second.astype(BF16)
 
@@ -161,6 +168,7 @@
             visible = (row < seen[slot]) & (col < used[c + REACH])
             wide[at(c + slot), at(c)] = jnp.where(visible, held[c, slot].astype(F32), 0.0).astype(BF16)
             counts[count_row(c, slot), :] = jnp.full((1, T), seen[slot], jnp.int32)
+    diagonals = pack((both, longer), 0, lambda a, b: own[at(a), at(b)])
     square[low, low] = (
         dot(own[low, :], own[:, low])
         + dot_tn(left[:, low], left[:, low])
@@ -176,14 +184,18 @@
         + dot_tn(left[high, high], left[high, high])
         + dot_tn(right[:, high], right[:, high])
     )
-    pack(both.at[:PACKED], lambda a, b: own[at(a), at(b)])
     for b in range(COLS):
         for a in range(b, COLS):
             block = jnp.where(keep(counts, b, a - b + REACH), square[at(a), at(b)], 0.0).astype(BF16)
             squared[at(a), at(b)] = block
-    pack(both.at[PACKED:], lambda a, b: squared[at(a), at(b)])
-    longer[: 2 * PACKED, :] = both[...]
-    longer[2 * PACKED :, :] = jnp.zeros((16, T), BF16)
+    diagonals += pack((both, longer), PACKED, lambda a, b: squared[at(a), at(b)])
+    strip_row = lax.broadcasted_iota(jnp.int32, (16, T), 0)
+    strip = jnp.zeros((16, T), F32)
+    for index, diagonal in enumerate(diagonals):
+        strip = jnp.where(strip_row == index, diagonal, strip)
+    both[2 * PACKED : SENT, :] = strip.astype(BF16)
+    longer[2 * PACKED : SENT, :] = strip.astype(BF16)
+    longer[SENT:, :] = jnp.zeros((16, T), BF16)
 
 
 def own_products(wide, square, squared, local, base, full):
@@ -229,11 +241,11 @@
 
 def side_terms(side, both, wide, counts, local, full, square, crossed, acc, term, held):
     thin, own = side_of(wide, side), wide.at[SIDE : 2 * SIDE]
-    unpack(lambda rows: both[rows, :], full)
+    unpack(both, 0, full)
     for j in range(2):
         rows = RANGE[side][j]
         acc[rows, HALVES[j]] = local[side, rows, HALVES[j]] + full_by_side(side, j, full, thin)
-    unpack(lambda rows: both[rows.start + PACKED : rows.stop + PACKED, :], square)
+    unpack(both, 1, square)
     for j in range(2):
         term[RANGE[side][j], HALVES[j]] = full_by_side(side, j, square, thin)
     for a in range(COLS):
@@ -316,8 +328,8 @@
             shape(COLS * BAND, T, dtype=jnp.int32),
             whole_f32,
             shape(SIDE, SIDE),
-            shape(2 * PACKED, T),
-            shape(2 * PACKED + 16, T),
+            shape(SENT, T),
+            shape(SENT + 16, T),
         ),
         [ANY] * 3,
         (VMEM,) * 6,

time: 21.4 us -> 21.2 us (level)
  transfers between devices with their start and end apart: 2 -> 2, of which waited for: 1 -> 1; matrix products, arithmetic and copies ran while one was open for 0% -> 0% of each run, Pallas kernels for 9% -> 8%
where the time goes in v8:
time: 21.2 us; the launch traced here: 21.1 us
  waiting for transfers between devices  11 us (52%)
  Pallas kernels  5.72 us (27%)
  starting transfers between devices  4.28 us (20%)
    ppermute x2, waiting for transfers between devices, send(): return lax.ppermute(array, AXES, to)  11 us
    ppermute x2, starting transfers between devices, send(): return lax.ppermute(array, AXES, to)  4.28 us
    pallas_call x1, Pallas kernels, per_device(): call(own_square, (shape(3 * SIDE, SIDE), shape(COLS * BAND, T, dtype=jnp....  2.1 us
    pallas_call x1, Pallas kernels, per_device(): call(finish_second, shape(*density.shape), [VMEM] * 6, ANY, [*room, ten,...  1.86 us
    pallas_call x1, Pallas kernels, per_device(): call(finish_first, (shape(10, T, T), whole_f32), [VMEM] * 5, (VMEM, VMEM)...  0.94 us
    pallas_call x1, Pallas kernels, per_device(): call(own_products, (shape(2, SIDE, SIDE, dtype=F32), whole_f32), [VMEM] *...  0.81 us
  transfers between devices with their start and end apart: 2, of which 1 were waited for; matrix products, arithmetic and copies ran while one was open for 0% of the time, Pallas kernels for 8%

profile of v8, /device:TPU:1, one launch (start us, length us, event | category | flops | bytes accessed | tf_op | source)
XLA Modules:
  0.0 21.1 jit_solution(6564482744153249674)
XLA Ops:
  0.0 2.1 %shard_map.37 = (bf16[1536,512]{1,0:T(8,128)(2,1)S(1)}, s32[36,128]{1,0:T(8,128)S(1)}, f32[512,512]{1,0:T(8,128)S(1)}, bf16[512,512]{1,0:T(8,128)(2,1)S(1)}, bf1...) custom-call(bf16[4,9,128,128]{3,2,1,0:T(8,128)(2,1)} %density.1, s32[4,9]{1,0:T(4,128)} %pattern.1, s32[512]{0:T(512)} %orbitals.1), custom_call_target="tpu_custom_call" | custom-call | flops 1073741824 | bytes 4194304 | tf_op jit(solution)/shard_map/pallas_call | solution.py:324
  2.1 2.2 %collective-permute-start = (bf16[2080,128]{1,0:T(8,128)(2,1)S(1)}, bf16[2080,128]{1,0:T(8,128)(2,1)S(1)}, u32[]{:S(2)}, u32[]{:S(2)}) collective-permute-start(bf16[2080,128]{1,0:T(8,128)(2,1)S(1)} %get-tuple-element.15), channel_id=1, source_target_pairs={{0,1},{1,2},{2,3},{3,4},{4,5},{5,6},{6,7},{7,8},{8,9},{9,10},{10,1... | collective-permute-start | bytes 1597448 | tf_op jit(solution)/shard_map/ppermute | solution.py:319
  4.3 2.1 %collective-permute-start.1 = (bf16[2064,128]{1,0:T(8,128)(2,1)S(1)}, bf16[2064,128]{1,0:T(8,128)(2,1)S(1)}, u32[]{:S(2)}, u32[]{:S(2)}) collective-permute-start(bf16[2064,128]{1,0:T(8,128)(2,1)S(1)} %get-tuple-element.21), channel_id=1, source_target_pairs={{0,127},{1,0},{2,1},{3,2},{4,3},{5,4},{6,5},{7,6},{8,7},{9,8},{10,... | collective-permute-start | bytes 1585160 | tf_op jit(solution)/shard_map/ppermute | solution.py:319
  6.4 0.8 %shard_map.38 = (f32[2,512,512]{2,1,0:T(8,128)S(1)}, f32[512,512]{1,0:T(8,128)S(1)}) custom-call(bf16[1536,512]{1,0:T(8,128)(2,1)S(1)} %get-tuple-element.16.wide, f32[512,512]{1,0:T(8,128)S(1)} %get-tuple-element.18.square, bf16[512,512]{1,0:T(8,128)(2,1)S(1)} %get-tuple-element.19.squared), custom_call_target="tpu_custom_call" | custom-call | flops 536870912 | bytes 1048576 | tf_op jit(solution)/shard_map/pallas_call | solution.py:347
  7.2 11.0 %collective-permute-done.1.both = bf16[2064,128]{1,0:T(8,128)(2,1)S(1)} collective-permute-done((bf16[2064,128]{1,0:T(8,128)(2,1)S(1)}, bf16[2064,128]{1,0:T(8,128)(2,1)S(1)}, u32[]{:S(2)}, u32[]{:S(2)}) %collective-permute-start.1) | collective-permute-done | bytes 528416 | tf_op jit(solution)/shard_map/ppermute | solution.py:319
  18.2 0.9 %shard_map.39 = (bf16[10,128,128]{2,1,0:T(8,128)(2,1)S(1)}, f32[512,512]{1,0:T(8,128)S(1)}) custom-call(bf16[2064,128]{1,0:T(8,128)(2,1)S(1)} %collective-permute-done.1.both, bf16[1536,512]{1,0:T(8,128)(2,1)S(1)} %get-tuple-element.16.wide, s32[36,128]{1,0:T(8,128)S(1)} %get-tuple-element.17.counts, f32[2,512,512]{2,1,0:T(8,128)S(1)} %get-tuple-element.20.local, ...), custom_call_target="tpu_custom_call" | custom-call | flops 33554432 | bytes 1024 | tf_op jit(solution)/shard_map/pallas_call | solution.py:360
  19.2 0.0 collective-permute-done.both
  19.2 1.9 %shard_map.40 = bf16[4,9,128,128]{3,2,1,0:T(8,128)(2,1)} custom-call(bf16[2080,128]{1,0:T(8,128)(2,1)S(1)} %collective-permute-done.both, bf16[1536,512]{1,0:T(8,128)(2,1)S(1)} %get-tuple-element.16.wide, s32[36,128]{1,0:T(8,128)S(1)} %get-tuple-element.17.counts, f32[2,512,512]{2,1,0:T(8,128)S(1)} %get-tuple-element.20.local, ...), custom_call_target="tpu_custom_call" | custom-call | flops 1073741824 | bytes 2097152 | tf_op jit(solution)/shard_map/pallas_call | solution.py:369
Async XLA Ops:
  2.1 17.1 %collective-permute-start = (bf16[2080,128]{1,0:T(8,128)(2,1)S(1)}, bf16[2080,128]{1,0:T(8,128)(2,1)S(1)}, u32[]{:S(2)}, u32[]{:S(2)}) collective-permute-start(bf16[2080,128]{1,0:T(8,128)(2,1)S(1)} %get-tuple-element.15), channel_id=1, source_target_pairs={{0,1},{1,2},{2,3},{3,4},{4,5},{5,6},{6,7},{7,8},{8,9},{9,10},{10,1... | collective-permute-start | bytes 1597448 | tf_op jit(solution)/shard_map/ppermute | solution.py:319
  4.3 13.9 %collective-permute-start.1 = (bf16[2064,128]{1,0:T(8,128)(2,1)S(1)}, bf16[2064,128]{1,0:T(8,128)(2,1)S(1)}, u32[]{:S(2)}, u32[]{:S(2)}) collective-permute-start(bf16[2064,128]{1,0:T(8,128)(2,1)S(1)} %get-tuple-element.21), channel_id=1, source_target_pairs={{0,127},{1,0},{2,1},{3,2},{4,3},{5,4},{6,5},{7,6},{8,7},{9,8},{10,... | collective-permute-start | bytes 1585160 | tf_op jit(solution)/shard_map/ppermute | solution.py:319

commit v9 on v8

--- a/solution.py
+++ b/solution.py
@@ -242,19 +242,19 @@
 def side_terms(side, both, wide, counts, local, full, square, crossed, acc, term, held):
     thin, own = side_of(wide, side), wide.at[SIDE : 2 * SIDE]
     unpack(both, 0, full)
+    unpack(both, 1, square)
     for j in range(2):
         rows = RANGE[side][j]
         acc[rows, HALVES[j]] = local[side, rows, HALVES[j]] + full_by_side(side, j, full, thin)
-    unpack(both, 1, square)
     for j in range(2):
         term[RANGE[side][j], HALVES[j]] = full_by_side(side, j, square, thin)
-    for a in range(COLS):
-        for c in range(COLS):
+    for c in range(COLS):
+        for a in range(COLS):
             if (a >= c) if side == 0 else (a <= c):
                 block = jnp.where(keep(counts, c, a - c + 2 * REACH * side), acc[at(a), at(c)], 0.0).astype(BF16)
-            else:
-                block = jnp.zeros((T, T), BF16)
-            crossed[at(a), at(c)] = block
+                crossed[at(a), at(c)] = block
+            elif a // 2 == c // 2:
+                crossed[at(a), at(c)] = jnp.zeros((T, T), BF16)
     low, high = HALVES
     every = slice(0, SIDE)
     for rows, inner, cols in (

time: 21.2 us -> 21.2 us (level)
  no operation moved by 1% of the time
where the time goes in v9:
time: 21.2 us; the launch traced here: 21.1 us
  waiting for transfers between devices  11 us (52%)
  Pallas kernels  5.72 us (27%)
  starting transfers between devices  4.28 us (20%)
    ppermute x2, waiting for transfers between devices, send(): return lax.ppermute(array, AXES, to)  11 us
    ppermute x2, starting transfers between devices, send(): return lax.ppermute(array, AXES, to)  4.28 us
    pallas_call x1, Pallas kernels, per_device(): call(own_square, (shape(3 * SIDE, SIDE), shape(COLS * BAND, T, dtype=jnp....  2.1 us
    pallas_call x1, Pallas kernels, per_device(): call(finish_second, shape(*density.shape), [VMEM] * 6, ANY, [*room, ten,...  1.86 us
    pallas_call x1, Pallas kernels, per_device(): call(finish_first, (shape(10, T, T), whole_f32), [VMEM] * 5, (VMEM, VMEM)...  0.94 us
    pallas_call x1, Pallas kernels, per_device(): call(own_products, (shape(2, SIDE, SIDE, dtype=F32), whole_f32), [VMEM] *...  0.81 us
  transfers between devices with their start and end apart: 2, of which 1 were waited for; matrix products, arithmetic and copies ran while one was open for 0% of the time, Pallas kernels for 8%

profile of v9, /device:TPU:1, one launch (start us, length us, event | category | flops | bytes accessed | tf_op | source)
XLA Modules:
  0.0 21.1 jit_solution(6564482744153249674)
XLA Ops:
  0.0 2.1 %shard_map.37 = (bf16[1536,512]{1,0:T(8,128)(2,1)S(1)}, s32[36,128]{1,0:T(8,128)S(1)}, f32[512,512]{1,0:T(8,128)S(1)}, bf16[512,512]{1,0:T(8,128)(2,1)S(1)}, bf1...) custom-call(bf16[4,9,128,128]{3,2,1,0:T(8,128)(2,1)} %density.1, s32[4,9]{1,0:T(4,128)} %pattern.1, s32[512]{0:T(512)} %orbitals.1), custom_call_target="tpu_custom_call" | custom-call | flops 1073741824 | bytes 4194304 | tf_op jit(solution)/shard_map/pallas_call | solution.py:324
  2.1 2.2 %collective-permute-start = (bf16[2080,128]{1,0:T(8,128)(2,1)S(1)}, bf16[2080,128]{1,0:T(8,128)(2,1)S(1)}, u32[]{:S(2)}, u32[]{:S(2)}) collective-permute-start(bf16[2080,128]{1,0:T(8,128)(2,1)S(1)} %get-tuple-element.15), channel_id=1, source_target_pairs={{0,1},{1,2},{2,3},{3,4},{4,5},{5,6},{6,7},{7,8},{8,9},{9,10},{10,1... | collective-permute-start | bytes 1597448 | tf_op jit(solution)/shard_map/ppermute | solution.py:319
  4.3 2.1 %collective-permute-start.1 = (bf16[2064,128]{1,0:T(8,128)(2,1)S(1)}, bf16[2064,128]{1,0:T(8,128)(2,1)S(1)}, u32[]{:S(2)}, u32[]{:S(2)}) collective-permute-start(bf16[2064,128]{1,0:T(8,128)(2,1)S(1)} %get-tuple-element.21), channel_id=1, source_target_pairs={{0,127},{1,0},{2,1},{3,2},{4,3},{5,4},{6,5},{7,6},{8,7},{9,8},{10,... | collective-permute-start | bytes 1585160 | tf_op jit(solution)/shard_map/ppermute | solution.py:319
  6.4 0.8 %shard_map.38 = (f32[2,512,512]{2,1,0:T(8,128)S(1)}, f32[512,512]{1,0:T(8,128)S(1)}) custom-call(bf16[1536,512]{1,0:T(8,128)(2,1)S(1)} %get-tuple-element.16.wide, f32[512,512]{1,0:T(8,128)S(1)} %get-tuple-element.18.square, bf16[512,512]{1,0:T(8,128)(2,1)S(1)} %get-tuple-element.19.squared), custom_call_target="tpu_custom_call" | custom-call | flops 536870912 | bytes 1048576 | tf_op jit(solution)/shard_map/pallas_call | solution.py:347
  7.2 11.0 %collective-permute-done.1.both = bf16[2064,128]{1,0:T(8,128)(2,1)S(1)} collective-permute-done((bf16[2064,128]{1,0:T(8,128)(2,1)S(1)}, bf16[2064,128]{1,0:T(8,128)(2,1)S(1)}, u32[]{:S(2)}, u32[]{:S(2)}) %collective-permute-start.1) | collective-permute-done | bytes 528416 | tf_op jit(solution)/shard_map/ppermute | solution.py:319
  18.2 0.9 %shard_map.39 = (bf16[10,128,128]{2,1,0:T(8,128)(2,1)S(1)}, f32[512,512]{1,0:T(8,128)S(1)}) custom-call(bf16[2064,128]{1,0:T(8,128)(2,1)S(1)} %collective-permute-done.1.both, bf16[1536,512]{1,0:T(8,128)(2,1)S(1)} %get-tuple-element.16.wide, s32[36,128]{1,0:T(8,128)S(1)} %get-tuple-element.17.counts, f32[2,512,512]{2,1,0:T(8,128)S(1)} %get-tuple-element.20.local, ...), custom_call_target="tpu_custom_call" | custom-call | flops 33554432 | bytes 1024 | tf_op jit(solution)/shard_map/pallas_call | solution.py:360
  19.2 0.0 collective-permute-done.both
  19.2 1.9 %shard_map.40 = bf16[4,9,128,128]{3,2,1,0:T(8,128)(2,1)} custom-call(bf16[2080,128]{1,0:T(8,128)(2,1)S(1)} %collective-permute-done.both, bf16[1536,512]{1,0:T(8,128)(2,1)S(1)} %get-tuple-element.16.wide, s32[36,128]{1,0:T(8,128)S(1)} %get-tuple-element.17.counts, f32[2,512,512]{2,1,0:T(8,128)S(1)} %get-tuple-element.20.local, ...), custom_call_target="tpu_custom_call" | custom-call | flops 1073741824 | bytes 2097152 | tf_op jit(solution)/shard_map/pallas_call | solution.py:369
Async XLA Ops:
  2.1 17.1 %collective-permute-start = (bf16[2080,128]{1,0:T(8,128)(2,1)S(1)}, bf16[2080,128]{1,0:T(8,128)(2,1)S(1)}, u32[]{:S(2)}, u32[]{:S(2)}) collective-permute-start(bf16[2080,128]{1,0:T(8,128)(2,1)S(1)} %get-tuple-element.15), channel_id=1, source_target_pairs={{0,1},{1,2},{2,3},{3,4},{4,5},{5,6},{6,7},{7,8},{8,9},{9,10},{10,1... | collective-permute-start | bytes 1597448 | tf_op jit(solution)/shard_map/ppermute | solution.py:319
  4.3 13.9 %collective-permute-start.1 = (bf16[2064,128]{1,0:T(8,128)(2,1)S(1)}, bf16[2064,128]{1,0:T(8,128)(2,1)S(1)}, u32[]{:S(2)}, u32[]{:S(2)}) collective-permute-start(bf16[2064,128]{1,0:T(8,128)(2,1)S(1)} %get-tuple-element.21), channel_id=1, source_target_pairs={{0,127},{1,0},{2,1},{3,2},{4,3},{5,4},{6,5},{7,6},{8,7},{9,8},{10,... | collective-permute-start | bytes 1585160 | tf_op jit(solution)/shard_map/ppermute | solution.py:319

commit v10 on v9

--- a/solution.py
+++ b/solution.py
@@ -68,7 +68,7 @@
     for index, (a, b) in enumerate(BELOW):
         block = read(at(index))
         full_ref[at(a), at(b)] = block
-        full_ref[at(b), at(a)] = block.T
+        full_ref[at(b), at(a)] = block.astype(F32).T.astype(BF16)
     strip = both[2 * PACKED : SENT, :].astype(F32)
     for pair in range(COLS // 2):
         two = read(at(len(BELOW) + pair)).astype(F32)

time: 21.2 us -> 21.2 us (level)
  no operation moved by 1% of the time
where the time goes in v10:
time: 21.2 us; the launch traced here: 21.1 us
  waiting for transfers between devices  11 us (52%)
  Pallas kernels  5.75 us (27%)
  starting transfers between devices  4.28 us (20%)
    ppermute x2, waiting for transfers between devices, send(): return lax.ppermute(array, AXES, to)  11 us
    ppermute x2, starting transfers between devices, send(): return lax.ppermute(array, AXES, to)  4.28 us
    pallas_call x1, Pallas kernels, per_device(): call(own_square, (shape(3 * SIDE, SIDE), shape(COLS * BAND, T, dtype=jnp....  2.1 us
    pallas_call x1, Pallas kernels, per_device(): call(finish_second, shape(*density.shape), [VMEM] * 6, ANY, [*room, ten,...  1.86 us
    pallas_call x1, Pallas kernels, per_device(): call(finish_first, (shape(10, T, T), whole_f32), [VMEM] * 5, (VMEM, VMEM)...  0.97 us
    pallas_call x1, Pallas kernels, per_device(): call(own_products, (shape(2, SIDE, SIDE, dtype=F32), whole_f32), [VMEM] *...  0.81 us
  transfers between devices with their start and end apart: 2, of which 1 were waited for; matrix products, arithmetic and copies ran while one was open for 0% of the time, Pallas kernels for 8%

profile of v10, /device:TPU:1, one launch (start us, length us, event | category | flops | bytes accessed | tf_op | source)
XLA Modules:
  0.0 21.1 jit_solution(9963487203146472100)
XLA Ops:
  0.0 2.1 %shard_map.37 = (bf16[1536,512]{1,0:T(8,128)(2,1)S(1)}, s32[36,128]{1,0:T(8,128)S(1)}, f32[512,512]{1,0:T(8,128)S(1)}, bf16[512,512]{1,0:T(8,128)(2,1)S(1)}, bf1...) custom-call(bf16[4,9,128,128]{3,2,1,0:T(8,128)(2,1)} %density.1, s32[4,9]{1,0:T(4,128)} %pattern.1, s32[512]{0:T(512)} %orbitals.1), custom_call_target="tpu_custom_call" | custom-call | flops 1073741824 | bytes 4194304 | tf_op jit(solution)/shard_map/pallas_call | solution.py:324
  2.1 2.2 %collective-permute-start = (bf16[2080,128]{1,0:T(8,128)(2,1)S(1)}, bf16[2080,128]{1,0:T(8,128)(2,1)S(1)}, u32[]{:S(2)}, u32[]{:S(2)}) collective-permute-start(bf16[2080,128]{1,0:T(8,128)(2,1)S(1)} %get-tuple-element.15), channel_id=1, source_target_pairs={{0,1},{1,2},{2,3},{3,4},{4,5},{5,6},{6,7},{7,8},{8,9},{9,10},{10,1... | collective-permute-start | bytes 1597448 | tf_op jit(solution)/shard_map/ppermute | solution.py:319
  4.3 2.1 %collective-permute-start.1 = (bf16[2064,128]{1,0:T(8,128)(2,1)S(1)}, bf16[2064,128]{1,0:T(8,128)(2,1)S(1)}, u32[]{:S(2)}, u32[]{:S(2)}) collective-permute-start(bf16[2064,128]{1,0:T(8,128)(2,1)S(1)} %get-tuple-element.21), channel_id=1, source_target_pairs={{0,127},{1,0},{2,1},{3,2},{4,3},{5,4},{6,5},{7,6},{8,7},{9,8},{10,... | collective-permute-start | bytes 1585160 | tf_op jit(solution)/shard_map/ppermute | solution.py:319
  6.4 0.8 %shard_map.38 = (f32[2,512,512]{2,1,0:T(8,128)S(1)}, f32[512,512]{1,0:T(8,128)S(1)}) custom-call(bf16[1536,512]{1,0:T(8,128)(2,1)S(1)} %get-tuple-element.16.wide, f32[512,512]{1,0:T(8,128)S(1)} %get-tuple-element.18.square, bf16[512,512]{1,0:T(8,128)(2,1)S(1)} %get-tuple-element.19.squared), custom_call_target="tpu_custom_call" | custom-call | flops 536870912 | bytes 1048576 | tf_op jit(solution)/shard_map/pallas_call | solution.py:347
  7.2 11.0 %collective-permute-done.1.both = bf16[2064,128]{1,0:T(8,128)(2,1)S(1)} collective-permute-done((bf16[2064,128]{1,0:T(8,128)(2,1)S(1)}, bf16[2064,128]{1,0:T(8,128)(2,1)S(1)}, u32[]{:S(2)}, u32[]{:S(2)}) %collective-permute-start.1) | collective-permute-done | bytes 528416 | tf_op jit(solution)/shard_map/ppermute | solution.py:319
  18.2 1.0 %shard_map.39 = (bf16[10,128,128]{2,1,0:T(8,128)(2,1)S(1)}, f32[512,512]{1,0:T(8,128)S(1)}) custom-call(bf16[2064,128]{1,0:T(8,128)(2,1)S(1)} %collective-permute-done.1.both, bf16[1536,512]{1,0:T(8,128)(2,1)S(1)} %get-tuple-element.16.wide, s32[36,128]{1,0:T(8,128)S(1)} %get-tuple-element.17.counts, f32[2,512,512]{2,1,0:T(8,128)S(1)} %get-tuple-element.20.local, ...), custom_call_target="tpu_custom_call" | custom-call | flops 33554432 | bytes 1024 | tf_op jit(solution)/shard_map/pallas_call | solution.py:360
  19.2 0.0 collective-permute-done.both
  19.2 1.9 %shard_map.40 = bf16[4,9,128,128]{3,2,1,0:T(8,128)(2,1)} custom-call(bf16[2080,128]{1,0:T(8,128)(2,1)S(1)} %collective-permute-done.both, bf16[1536,512]{1,0:T(8,128)(2,1)S(1)} %get-tuple-element.16.wide, s32[36,128]{1,0:T(8,128)S(1)} %get-tuple-element.17.counts, f32[2,512,512]{2,1,0:T(8,128)S(1)} %get-tuple-element.20.local, ...), custom_call_target="tpu_custom_call" | custom-call | flops 1073741824 | bytes 2097152 | tf_op jit(solution)/shard_map/pallas_call | solution.py:369
Async XLA Ops:
  2.1 17.1 %collective-permute-start = (bf16[2080,128]{1,0:T(8,128)(2,1)S(1)}, bf16[2080,128]{1,0:T(8,128)(2,1)S(1)}, u32[]{:S(2)}, u32[]{:S(2)}) collective-permute-start(bf16[2080,128]{1,0:T(8,128)(2,1)S(1)} %get-tuple-element.15), channel_id=1, source_target_pairs={{0,1},{1,2},{2,3},{3,4},{4,5},{5,6},{6,7},{7,8},{8,9},{9,10},{10,1... | collective-permute-start | bytes 1597448 | tf_op jit(solution)/shard_map/ppermute | solution.py:319
  4.3 13.9 %collective-permute-start.1 = (bf16[2064,128]{1,0:T(8,128)(2,1)S(1)}, bf16[2064,128]{1,0:T(8,128)(2,1)S(1)}, u32[]{:S(2)}, u32[]{:S(2)}) collective-permute-start(bf16[2064,128]{1,0:T(8,128)(2,1)S(1)} %get-tuple-element.21), channel_id=1, source_target_pairs={{0,127},{1,0},{2,1},{3,2},{4,3},{5,4},{6,5},{7,6},{8,7},{9,8},{10,... | collective-permute-start | bytes 1585160 | tf_op jit(solution)/shard_map/ppermute | solution.py:319
